TPU v7x, 256 devices: a whole 4x4x8 slice. The times are simulated.
256 devices in a mesh: dp: 32 (over z, y_hi, core), fsdp: 8 (over y_lo, x).
Axes of the slice: x: 4, y: 4 (y_hi: 2, y_lo: 2; y = y_hi * 2 + y_lo), z: 8, core: 2. Of those that a mesh axis runs over, the one named last changes fastest.
Arguments:
- query_embedding_rows: bfloat16 [2048, 2048], P('dp', 'fsdp'), may hold values from -6 to 6
- passage_embedding_rows: bfloat16 [2048, 2048], P('dp', 'fsdp'), may hold values from -6 to 6
- positive: int32 [2048], P('dp'), may hold values from 0 to 2047
- layer_input_rows: bfloat16 [512, 128, 4096], P(('dp', 'fsdp')), may hold values from -6 to 6
- input_norm_gain: float32 [4096], replicated, may hold values from 0.25 to 2.75
- frozen_projection_weight: bfloat16 [4096, 3072], P('fsdp'), may hold values from -0.09375 to 0.09375
- adapter_down_maps: bfloat16 [4096, 48], P('fsdp'), may hold values from -0.09375 to 0.09375
- adapter_up_maps: bfloat16 [3072, 16], P('fsdp'), may hold values from -1.5 to 1.5
Outputs:
- query_grad: float32 [2048, 2048], P('dp', 'fsdp')
- passage_gradient: float32 [2048, 2048], P('dp', 'fsdp')
- grad_down: float32 [4096, 48], P('fsdp')
- grad_up: float32 [3072, 16], P('fsdp')
All inputs are finite; a program needn't handle non-finite values.
Results may differ from a plain program's by a relative error of at most 0.007.
The roundings to bfloat16 on the way count: a program that leaves them out, or rounds other values in their place, can miss the bound.
Values may be sent and summed in bfloat16 or wider, within the bound.
No kernel may reach another device: no remote copies, remote signals or barrier semaphores. Data moves between devices by JAX's collectives and lax.ppermute only.
A program may use at most 128 MiB of HBM per device.

v0:
```python
import math

import jax
import jax.numpy as jnp
from jax import lax
from jax.sharding import PartitionSpec as P

MODEL_WIDTH = 4096
HD = 128
HQ = 16
HK = 4
ADAPTER_RANK = 16
L = 128


EPS_NORM = 1e-06
SOFTMAX_TEMPER = 0.02
ADAPTER_SCALE = 2.0
RMS_EPS = 1e-05
ROPE_BASE = 10000.0
MAX_NORM = 1.0
PRECISE = lax.Precision.HIGHEST


def rounded(value):
    return lax.optimization_barrier(value.astype(jnp.bfloat16)).astype(jnp.float32)


def through(value):
    return value + lax.stop_gradient(rounded(value) - value)


def normalize_rows(token_rows, gain):
    values = token_rows.astype(jnp.float32)
    scale = lax.rsqrt(jnp.mean(values * values, axis=-1, keepdims=True) + RMS_EPS)
    return (values * scale * gain[None, :]).astype(jnp.bfloat16)


def rotate_pairs(values):
    half_size = HD // 2
    freqs = ROPE_BASE ** (-(jnp.arange(half_size, dtype=jnp.float32) * 2.0) / HD)
    angles = jnp.arange(L, dtype=jnp.float32)[:, None] * freqs[None, :]
    cosine = jnp.cos(angles)[None, :, None, :]
    sine = jnp.sin(angles)[None, :, None, :]
    first = values[..., :half_size]
    second = values[..., half_size:]
    return jnp.concatenate(
        [first * cosine - second * sine, second * cosine + first * sine], axis=-1
    )


def attend(queries, keys, values):
    seq_count = queries.shape[0]
    grouped = queries.reshape(seq_count, L, HK, HQ // HK, HD)
    similarity_scores = jnp.einsum(
        "slkgd,smkd->skglm", grouped, keys, precision=PRECISE
    ) / math.sqrt(HD)
    causal = jnp.arange(L)[:, None] >= jnp.arange(L)[None, :]
    similarity_scores = jnp.where(causal, similarity_scores, -1e30)
    row_max = lax.stop_gradient(jnp.max(similarity_scores, axis=-1, keepdims=True))
    weights = jnp.exp(similarity_scores - row_max)
    weights = through(weights / jnp.sum(weights, axis=-1, keepdims=True))
    outputs = jnp.einsum("skglm,smkd->slkgd", weights, values, precision=PRECISE)
    return jnp.mean(outputs.reshape(seq_count, L, HQ * HD), axis=1)


def surrogate(low_rank_activation, up_map_transposed, frozen_projection, embedding_gradient_pair):
    seq_count = embedding_gradient_pair.shape[0]
    low_rank = through(low_rank_activation)
    slice_list = []
    offset = 0
    for block, span_width in enumerate((HQ * HD, HK * HD, HK * HD)):
        slice_list.append(
            jnp.dot(
                low_rank[:, ADAPTER_RANK * block : ADAPTER_RANK * (block + 1)],
                up_map_transposed[offset : offset + span_width].T,
                precision=PRECISE,
            )
        )
        offset = offset + span_width
    projection_output = frozen_projection + ADAPTER_SCALE * jnp.concatenate(slice_list, axis=1)
    queries = projection_output[:, : HQ * HD].reshape(seq_count, L, HQ, HD)
    keys = projection_output[:, HQ * HD : (HQ + HK) * HD].reshape(seq_count, L, HK, HD)
    values = projection_output[:, (HQ + HK) * HD :].reshape(seq_count, L, HK, HD)
    queries = through(rotate_pairs(queries))
    keys = through(rotate_pairs(keys))
    values = through(values)
    embedded = attend(queries, keys, values)
    return jnp.sum(embedded * embedding_gradient_pair)


def shards(
    query_embedding_rows,
    passage_embedding_rows,
    positive,
    layer_input_rows,
    input_norm_gain,
    frozen_projection_weight,
    adapter_down_maps,
    adapter_up_maps,
):
    query_f32 = query_embedding_rows.astype(jnp.float32)
    passage_single_float = passage_embedding_rows.astype(jnp.float32)
    q_square, p_square = lax.psum(
        (
            jnp.sum(query_f32 * query_f32, axis=1),
            jnp.sum(passage_single_float * passage_single_float, axis=1),
        ),
        "fsdp",
    )
    query_norm_value = jnp.sqrt(q_square + EPS_NORM)
    passage_norm_value = jnp.sqrt(p_square + EPS_NORM)
    passage_all = lax.all_gather(passage_embedding_rows, "dp", axis=0, tiled=True)
    passage_norm_every = lax.all_gather(passage_norm_value, "dp", axis=0, tiled=True)
    unscaled_scores = jnp.dot(
        query_embedding_rows, passage_all.T, preferred_element_type=jnp.float32
    )
    similarity_scores = lax.psum(
        unscaled_scores
        / (query_norm_value[:, None] * passage_norm_every[None, :] * SOFTMAX_TEMPER),
        "fsdp",
    )
    row_max = jnp.max(similarity_scores, axis=1, keepdims=True)
    expd = jnp.exp(similarity_scores - row_max)
    softmax = expd / jnp.sum(expd, axis=1, keepdims=True)
    onehot = (
        jnp.arange(similarity_scores.shape[1], dtype=jnp.int32)[None, :] == positive[:, None]
    ).astype(jnp.float32)
    score_gradient = softmax - onehot
    score_terms = score_gradient * similarity_scores
    cross_term = jnp.sum(score_terms, axis=1)
    passage_all32 = passage_all.astype(jnp.float32)
    weighted_passages = score_gradient / (passage_norm_every[None, :] * SOFTMAX_TEMPER)
    query_grad = (
        jnp.dot(weighted_passages, passage_all32, precision=PRECISE) / query_norm_value[:, None]
        - (cross_term / (query_norm_value * query_norm_value))[:, None] * query_f32
    )
    column_loss_term = jnp.sum(score_terms, axis=0)
    query_unit = query_f32 / query_norm_value[:, None]
    pulled_gradient = jnp.dot(score_gradient.T, query_unit, precision=PRECISE)
    passage_gradient = lax.psum_scatter(
        pulled_gradient / (passage_norm_every * SOFTMAX_TEMPER)[:, None]
        - (column_loss_term / (passage_norm_every * passage_norm_every))[:, None] * passage_all32,
        "dp",
        scatter_dimension=0,
        tiled=True,
    )
    seq_count = layer_input_rows.shape[0]
    rerun_count = lax.axis_size("fsdp") * seq_count
    embedding_gradient_pair = lax.all_to_all(
        query_grad[:rerun_count], "fsdp", split_axis=0, concat_axis=1, tiled=True
    )
    normalized_input = normalize_rows(
        layer_input_rows.reshape(seq_count * L, MODEL_WIDTH), input_norm_gain
    )
    weight_piece = lax.all_gather(frozen_projection_weight, "fsdp", axis=0, tiled=True)
    down_map_slice = lax.all_gather(adapter_down_maps, "fsdp", axis=0, tiled=True)
    frozen_projection = jnp.dot(normalized_input, weight_piece, preferred_element_type=jnp.float32)
    low_rank_activation = jnp.dot(
        normalized_input, down_map_slice, preferred_element_type=jnp.float32
    )
    up_map_complete = lax.all_gather(adapter_up_maps, "fsdp", axis=0, tiled=True).astype(
        jnp.float32
    )
    _, pullback = jax.vjp(
        lambda low_in, up_in: surrogate(low_in, up_in, frozen_projection, embedding_gradient_pair),
        low_rank_activation,
        up_map_complete,
    )
    dlow, up_map_gradient = pullback(jnp.ones((), jnp.float32))
    down_map_gradient = jnp.dot(normalized_input.astype(jnp.float32).T, dlow, precision=PRECISE)
    down_shard, up_shard = (
        lax.psum_scatter(down_map_gradient, "fsdp", scatter_dimension=0, tiled=True),
        lax.psum_scatter(up_map_gradient, "fsdp", scatter_dimension=0, tiled=True),
    )
    down_shard, up_shard = lax.psum((down_shard, up_shard), "dp")
    square_sum = lax.psum(jnp.sum(down_shard * down_shard) + jnp.sum(up_shard * up_shard), "fsdp")
    grad_norm = jnp.sqrt(square_sum)
    clip_factor = jnp.minimum(1.0, MAX_NORM / (grad_norm + 1e-06))
    unit_scale = math.sqrt(3 * MODEL_WIDTH * ADAPTER_RANK + (HQ + 2 * HK) * HD * ADAPTER_RANK)
    return (
        query_grad,
        passage_gradient,
        down_shard * (clip_factor * unit_scale),
        up_shard * (clip_factor * unit_scale),
    )


def solution(mesh):
    in_specs = (
        P("dp", "fsdp"),
        P("dp", "fsdp"),
        P("dp"),
        P(("dp", "fsdp"), None, None),
        P(),
        P("fsdp", None),
        P("fsdp", None),
        P("fsdp", None),
    )
    out_specs = (P("dp", "fsdp"), P("dp", "fsdp"), P("fsdp", None), P("fsdp", None))
    return jax.shard_map(shards, mesh=mesh, in_specs=in_specs, out_specs=out_specs, check_vma=False)
```

profile of v0, /device:TPU:1, one launch (start us, length us, event | category | flops | bytes accessed | tf_op | source)
XLA Modules:
  0.0 934.8 jit_solution(250420976528316752)
XLA Ops:
  8.0 1.3 dynamic-slice
  9.9 0.9 multiply_reduce_fusion.5
  10.7 0.9 fusion.49
  11.6 16.8 %all-reduce.14 = (f32[64]{0:T(128)S(1)}, f32[64]{0:T(128)S(1)}) all-reduce(f32[64]{0:T(128)S(1)} %multiply_reduce_fusion.5, f32[64]{0:T(128)S(1)} %fusion.49), channel_id=1, replica_groups=mesh['dp'=32,'fsdp'=8] {'fsdp'}, use_global_device_ids=true, to_apply=%region_3.0 | all-reduce | flops 128 | bytes 1024 | tf_op jit(solution)/shard_map/psum | solution.py:104
  28.5 72.9 %all-reduce.13 = f32[2048]{0:T(1024)S(1)} all-reduce(f32[2048]{0:T(1024)S(1)} %sqrt_dynamic-update-slice_fusion), channel_id=1, replica_groups=mesh['dp'=32,'fsdp'=8] {'dp'}, use_global_device_ids=true, to_apply=%add.13 | all-reduce | flops 2048 | bytes 16384
  101.5 2.5 convolution_divide_fusion.1
  104.8 23.3 %all_gather.18 = bf16[4096,48]{0,1:T(8,128)(2,1)S(1)} all-gather(bf16[512,48]{0,1:T(8,128)(2,1)S(1)} %copy-done.23), channel_id=1, replica_groups=mesh['dp'=32,'fsdp'=8] {'fsdp'}, dimensions={0}, use_global_device_ids=true | all-gather | bytes 442368 | tf_op jit(solution)/shard_map/all_gather | solution.py:157
  130.0 22.2 %all_gather.19 = bf16[3072,16]{0,1:T(8,128)(2,1)S(1)} all-gather(bf16[384,16]{0,1:T(8,128)(2,1)S(1)} %copy-done.29), channel_id=1, replica_groups=mesh['dp'=32,'fsdp'=8] {'fsdp'}, dimensions={0}, use_global_device_ids=true | all-gather | bytes 110592 | tf_op jit(solution)/shard_map/all_gather | solution.py:162
  152.9 1.2 fusion.66
  154.1 2.4 fusion.51
  156.5 17.8 %all-reduce.18.cloned.1.call-done = f32[64,2048]{1,0:T(8,128)} async-done(((f32[64,2048]{1,0:T(8,128)}), f32[64,2048]{1,0:T(8,128)}) %all-reduce.18.cloned.1.call-update) | async-done | bytes 524304 | tf_op jit(solution)/shard_map/psum | solution.py:118
  174.3 1.2 reduce_max.18
  175.5 1.3 fusion.40
  176.8 1.5 multiply_reduce_fusion.2
  178.9 2.1 fusion.20
  181.8 3.3 all-to-all-start
  186.2 4.0 all-to-all-done
  190.8 241.8 %all-gather.5.cloned.1.call-done = bf16[4096,3072]{1,0:T(8,128)(2,1)} async-done(((bf16[512,3072]{1,0:T(8,128)(2,1)}), bf16[4096,3072]{1,0:T(8,128)(2,1)}) %all-gather.5.cloned.1.call-update) | async-done | bytes 25165840 | tf_op jit(solution)/shard_map/all_gather | solution.py:156
  432.6 12.3 %convolution_add_fusion = f32[256,3072]{1,0:T(8,128)S(1)} fusion(bf16[256,4096]{1,0:T(8,128)(2,1)S(1)} %fusion.1, bf16[4096,3072]{1,0:T(8,128)(2,1)} %all-gather.5.cloned.1.call-done, f32[256,512]{1,0:T(8,128)S(1)} %fusion.63, f32[256,512]{1,0:T(8,128)} %fusion.66, f32[256,2048]{1,0:T(8,128)} %fusion.51), kind=kOutput, calls=%fused_computation.4 | convolution fusion | flops 6445596672 | bytes 33554432 | tf_op jit(solution)/shard_map/dot_general | solution.py:158
  445.2 0.9 fusion.81
  448.2 1.9 copy.69
  451.0 1.0 multiply_subtract_fusion.1
  452.2 2.1 fusion.12
  454.3 1.3 copy-done.5
  456.8 1.2 reshape.134
  458.1 4.6 fusion.43
  462.8 3.6 convolution_bitcast_fusion
  466.4 4.0 fusion.44
  470.5 2.8 fusion.17
  473.2 1.0 copy.52
  474.4 1.0 copy.56
  475.4 1.2 fusion.82
  476.6 2.2 copy.72
  478.7 2.1 copy.73
  480.8 2.1 multiply_add_fusion.1
  483.5 1.1 copy.89
  485.7 1.1 fusion.15
  486.9 2.1 fusion.53
  489.9 1.2 fusion.13
  491.8 31.8 %reduce-scatter.6.cloned.1.call-done = f32[512,48]{0,1:T(8,128)} async-done(((f32[4096,48]{0,1:T(8,128)}), f32[512,48]{0,1:T(8,128)}) %reduce-scatter.6.cloned.1.call-update) | async-done | bytes 98320 | tf_op jit(solution)/shard_map/reduce_scatter | solution.py:173
  523.7 5.2 fusion.6
  529.0 35.2 %reduce-scatter.8.cloned.1.call-done = f32[384,16]{0,1:T(8,128)} async-done(((f32[3072,16]{0,1:T(8,128)}), f32[384,16]{0,1:T(8,128)}) %reduce-scatter.8.cloned.1.call-update) | async-done | bytes 24592 | tf_op jit(solution)/shard_map/reduce_scatter | solution.py:174
  564.2 129.0 %psum.46 = f32[384,16]{0,1:T(8,128)S(1)} all-reduce(f32[384,16]{0,1:T(8,128)} %reduce-scatter.8.cloned.1.call-done), channel_id=1, replica_groups=mesh['dp'=32,'fsdp'=8] {'dp'}, use_global_device_ids=true, to_apply=%region_18.19 | all-reduce | flops 6144 | bytes 49152 | tf_op jit(solution)/shard_map/psum | solution.py:176
  693.8 115.1 %all-reduce.20.cloned.1.call-done = f32[512,48]{0,1:T(8,128)} async-done(((f32[512,48]{0,1:T(8,128)}), f32[512,48]{0,1:T(8,128)}) %all-reduce.20.cloned.1.call-update) | async-done | bytes 98320 | tf_op jit(solution)/shard_map/psum | solution.py:176
  808.9 1.5 multiply_reduce_fusion.4
  811.7 15.7 %psum.47 = f32[]{:T(128)} all-reduce(f32[]{:T(128)S(6)} %add.104), channel_id=1, replica_groups=mesh['dp'=32,'fsdp'=8] {'fsdp'}, use_global_device_ids=true, to_apply=%region_20.21 | all-reduce | flops 1 | bytes 8 | tf_op jit(solution)/shard_map/psum | solution.py:177
  828.8 1.5 broadcast_multiply_fusion
  830.3 97.1 %reduce-scatter.4.cloned.1.call-done = f32[64,256]{1,0:T(8,128)} async-done(((f32[2048,256]{1,0:T(8,128)}), f32[64,256]{1,0:T(8,128)}) %reduce-scatter.4.cloned.1.call-update) | async-done | bytes 65552 | tf_op jit(solution)/shard_map/reduce_scatter | solution.py:141
  (146 shorter events, 16.5 us)
Async XLA Ops:
  7.2 94.3 %all-gather.3.cloned.1.call-start = ((), (), s32[]{:S(2)}) async-start(), calls=%async_computation.4 | async-start | bytes 1081344 | tf_op jit(solution)/shard_map/all_gather | solution.py:113
  7.9 166.4 %all-reduce.18.cloned.1.call-start = ((), (), s32[]{:S(2)}) async-start(), calls=%async_computation.5 | async-start | bytes 1048576 | tf_op jit(solution)/shard_map/psum | solution.py:118
  101.4 77.5 %copy-start.40 = (f32[64]{0:T(128)}, f32[64]{0:T(128)S(1)}, u32[]{:S(2)}) copy-start(f32[64]{0:T(128)S(1)} %add_sqrt_fusion) | copy-start | bytes 772
  104.0 0.8 copy-start.23
  104.0 24.1 %copy-start.2 = (bf16[2,128,4096]{2,1,0:T(8,128)(2,1)S(1)}, bf16[2,128,4096]{2,1,0:T(8,128)(2,1)}, u32[]{:S(2)}) copy-start(bf16[2,128,4096]{2,1,0:T(8,128)(2,1)} %param.11) | copy-start | bytes 6291460
  104.0 24.6 %copy-start.26 = (f32[4096]{0:T(1024)S(1)}, f32[4096]{0:T(1024)}, u32[]{:S(2)}) copy-start(f32[4096]{0:T(1024)} %param.12) | copy-start | bytes 49156
  104.0 328.6 %all-gather.5.cloned.1.call-start = ((), (), s32[]{:S(2)}) async-start(), calls=%async_computation.7 | async-start | bytes 28311552 | tf_op jit(solution)/shard_map/all_gather | solution.py:156
  104.8 23.8 %copy-start.3 = (bf16[2,128,4096]{2,1,0:T(8,128)(2,1)S(1)}, bf16[2,128,4096]{2,1,0:T(8,128)(2,1)}, u32[]{:S(2)}) copy-start(bf16[2,128,4096]{2,1,0:T(8,128)(2,1)} %param.11) | copy-start | bytes 6291460
  129.2 303.4 %copy-start = (bf16[256,4096]{1,0:T(8,128)(2,1)}, bf16[256,4096]{1,0:T(8,128)(2,1)S(1)}, u32[]{:S(2)}) copy-start(bf16[256,4096]{1,0:T(8,128)(2,1)S(1)} %fusion.1) | copy-start | bytes 6291460
  152.4 33.6 %copy-start.14 = (f32[128,64]{0,1:T(8,128)}, f32[128,64]{0,1:T(8,128)S(1)}, u32[]{:S(2)}) copy-start(f32[128,64]{0,1:T(8,128)S(1)} %get-tuple-element.27) | copy-start | bytes 98308
  152.5 24.3 %copy-start.17 = (f32[256,48]{0,1:T(8,128)}, f32[256,48]{0,1:T(8,128)S(1)}, u32[]{:S(2)}) copy-start(f32[256,48]{0,1:T(8,128)S(1)} %subtract_add_fusion.7) | copy-start | bytes 147460
  152.5 24.3 %copy-start.38 = (s32[64]{0:T(128)S(1)}, s32[64]{0:T(128)}, u32[]{:S(2)}) copy-start(s32[64]{0:T(128)} %param.10) | copy-start | bytes 772
  152.9 26.0 %copy-start.24 = (bf16[64,256]{1,0:T(8,128)(2,1)S(1)}, bf16[64,256]{1,0:T(8,128)(2,1)}, u32[]{:S(2)}) copy-start(bf16[64,256]{1,0:T(8,128)(2,1)} %param.8) | copy-start | bytes 98308
  175.5 5.6 copy-start.33
  176.8 4.3 copy-start.36
  178.9 2.2 copy-start.31
  181.1 263.8 %copy-start.35 = (f32[64,256]{1,0:T(8,128)}, f32[64,256]{1,0:T(8,128)S(1)}, u32[]{:S(2)}) copy-start(f32[64,256]{1,0:T(8,128)S(1)} %fusion.20) | copy-start | bytes 196612
  181.8 8.4 all-to-all-start
  185.1 338.5 %reduce-scatter.6.cloned.1.call-start = ((), (), s32[]{:S(2)}) async-start(), calls=%async_computation.8 | async-start | bytes 884736 | tf_op jit(solution)/shard_map/reduce_scatter | solution.py:173
  186.0 260.4 %copy-start.10 = (f32[128,64]{1,0:T(8,128)}, f32[128,64]{1,0:T(8,128)S(1)}, u32[]{:S(2)}) copy-start(f32[128,64]{1,0:T(8,128)S(1)} %copy.46) | copy-start | bytes 98308
  186.1 260.3 %copy-start.12 = (f32[128,64]{1,0:T(8,128)}, f32[128,64]{1,0:T(8,128)S(1)}, u32[]{:S(2)}) copy-start(f32[128,64]{1,0:T(8,128)S(1)} %copy.47) | copy-start | bytes 98308
  450.6 1.6 copy-start.4
  454.3 1.3 copy-start.5
  454.3 2.5 copy-start.19
  458.0 4.7 copy-start.6
  458.1 4.7 copy-start.20
  458.1 4.7 copy-start.22
  458.1 4.7 copy-start.27
  466.4 4.0 copy-start.28
  470.5 3.8 copy-start.15
  470.5 3.8 copy-start.16
  473.2 2.2 copy-start.7
  478.7 2.1 copy-start.11
  478.7 2.1 copy-start.13
  483.5 1.2 copy-start.8
  483.5 1.2 copy-start.9
  485.0 1.8 copy-start.1
  486.8 2.2 copy-start.18
  489.0 34.7 %copy-start.25 = (bf16[64,256]{1,0:T(8,128)(2,1)S(1)}, bf16[64,256]{1,0:T(8,128)(2,1)}, u32[]{:S(2)}) copy-start(bf16[64,256]{1,0:T(8,128)(2,1)} %param.8) | copy-start | bytes 98308
  489.0 34.7 %copy-start.30 = (f32[2048]{0:T(1024)S(1)}, f32[2048]{0:T(1024)}, u32[]{:S(2)}) copy-start(f32[2048]{0:T(1024)} %get-tuple-element.24) | copy-start | bytes 24580
  489.0 34.7 %copy-start.32 = (f32[2048]{0:T(1024)S(1)}, f32[2048]{0:T(1024)}, u32[]{:S(2)}) copy-start(f32[2048]{0:T(1024)} %copy-done.31) | copy-start | bytes 24580
  489.0 34.7 %copy-start.34 = (f32[64]{0:T(128)S(1)}, f32[64]{0:T(128)}, u32[]{:S(2)}) copy-start(f32[64]{0:T(128)} %copy-done.33) | copy-start | bytes 772
  489.0 34.7 %copy-start.37 = (f32[64]{0:T(128)S(1)}, f32[64]{0:T(128)}, u32[]{:S(2)}) copy-start(f32[64]{0:T(128)} %copy-done.36) | copy-start | bytes 772
  489.0 34.7 %copy-start.39 = (s32[64]{0:T(128)S(1)}, s32[64]{0:T(128)}, u32[]{:S(2)}) copy-start(s32[64]{0:T(128)} %param.10) | copy-start | bytes 772
  489.0 34.7 %copy-start.41 = (f32[64]{0:T(128)S(1)}, f32[64]{0:T(128)}, u32[]{:S(2)}) copy-start(f32[64]{0:T(128)} %copy-done.40) | copy-start | bytes 772
  489.0 75.1 %reduce-scatter.8.cloned.1.call-start = ((), (), s32[]{:S(2)}) async-start(), calls=%async_computation.10 | async-start | bytes 221184 | tf_op jit(solution)/shard_map/reduce_scatter | solution.py:174
  491.8 317.1 %all-reduce.20.cloned.1.call-start = ((), (), s32[]{:S(2)}) async-start(), calls=%async_computation.9 | async-start | bytes 196608 | tf_op jit(solution)/shard_map/psum | solution.py:176
  523.6 403.9 %reduce-scatter.4.cloned.1.call-start = ((), (), s32[]{:S(2)}) async-start(), calls=%async_computation.6 | async-start | bytes 2162688 | tf_op jit(solution)/shard_map/reduce_scatter | solution.py:141
  (2 other events, 1.4 us)
Sparse Core Ops, SparseCore 0:
  10.8 81.8 all-gather.2
  104.1 70.1 all-reduce.17
  176.2 256.3 all-gather.4
  489.1 34.4 reduce-scatter.5
  525.9 38.1 reduce-scatter.7
  566.8 242.0 all-reduce.19
  813.6 113.8 reduce-scatter.3
where the time goes:
time: 945 us; the launch traced here: 935 us
  waiting for transfers between devices  544 us (58%)
  blocking collectives  280 us (30%)
  matrix products  49.9 us (5%)
  other arithmetic  20.3 us (2%)
  local copies, waits for them, and re-layouts  18.6 us (2%)
  between operations  18 us (2%)
    all_gather x1, waiting for transfers between devices, shards(): lax.all_gather(frozen_projection_weight, 'fsdp', axis=0, tiled=True)  242 us
    psum x1, blocking collectives, shards(): down_shard, up_shard = lax.psum((down_shard, up_shard), 'dp')  129 us
    psum x1, waiting for transfers between devices, shards(): down_shard, up_shard = lax.psum((down_shard, up_shard), 'dp')  115 us
    reduce_scatter x1, waiting for transfers between devices, shards(): lax.psum_scatter(pulled_gradient / (passage_norm_every * SOFTMAX_TEMPER)[...  97.1 us
    unnamed x1, blocking collectives  72.9 us
    reduce_scatter x1, waiting for transfers between devices, shards(): lax.psum_scatter(up_map_gradient, 'fsdp', scatter_dimension=0, tiled=True)  35.2 us
    reduce_scatter x1, waiting for transfers between devices, shards(): lax.psum_scatter(down_map_gradient, 'fsdp', scatter_dimension=0, tiled=True)  31.8 us
    all_gather x1, blocking collectives, shards(): lax.all_gather(adapter_down_maps, 'fsdp', axis=0, tiled=True)  23.3 us
  transfers between devices with their start and end apart: 8, of which 7 were waited for; matrix products, arithmetic and copies ran while one was open for 3% of the time, Pallas kernels for 0%

commit v1 on v0

v1 whole, which is shorter than its diff:
```python
import functools
import math

import jax
import jax.numpy as jnp
import numpy as np
from jax import lax
from jax.experimental import pallas as pl
from jax.experimental.pallas import tpu as pltpu
from jax.sharding import PartitionSpec as P

MODEL_WIDTH = 4096
HD = 128
HQ = 16
HK = 4
GROUP = HQ // HK
ADAPTER_RANK = 16
L = 128
EPS_NORM = 1e-06
SOFTMAX_TEMPER = 0.02
ADAPTER_SCALE = 2.0
RMS_EPS = 1e-05
ROPE_BASE = 10000.0
MAX_NORM = 1.0

N_DP = 32
N_FSDP = 8
RING = N_DP // 2
ROWS = MODEL_WIDTH // N_FSDP
UP_ROWS = (HQ + 2 * HK) * HD // N_FSDP
COLS = (GROUP + 2) * HD
PACK = 3 * ADAPTER_RANK + ADAPTER_RANK
LOW = 3 * ADAPTER_RANK
F32 = jnp.float32
BF16 = jnp.bfloat16
VMEM_LIMIT = 48 * 1024 * 1024

NN = (((1,), (0,)), ((), ()))
NT = (((1,), (1,)), ((), ()))
TN = (((0,), (0,)), ((), ()))


def dot(a, b, dims=NN):
    return lax.dot_general(a, b, dims, preferred_element_type=F32)


def split(x):
    head = x.astype(BF16)
    return head, (x - head.astype(F32)).astype(BF16)


def params():
    return pltpu.CompilerParams(vmem_limit_bytes=VMEM_LIMIT)


def cost(flops, bytes_accessed):
    return pl.CostEstimate(flops=int(flops), bytes_accessed=int(bytes_accessed), transcendentals=0)


VMEM = pl.BlockSpec(memory_space=pltpu.VMEM)
SMEM = pl.BlockSpec(memory_space=pltpu.SMEM)
ANY = pl.BlockSpec(memory_space=pl.ANY)


def rope_tables():
    half = HD // 2
    freqs = np.power(
        np.float32(ROPE_BASE), -(np.arange(half, dtype=np.float32) * np.float32(2.0)) / np.float32(HD)
    ).astype(np.float32)
    angles = np.arange(L, dtype=np.float32)[:, None] * freqs[None, :]
    cosine = np.cos(angles).astype(np.float32)
    sine = np.sin(angles).astype(np.float32)
    return np.concatenate([cosine, cosine], 1), np.concatenate([-sine, sine], 1)


def normalize_kernel(x_ref, gain_ref, first_ref, second_ref):
    for s, out_ref in enumerate((first_ref, second_ref)):
        values = x_ref[s].astype(F32)
        scale = lax.rsqrt(jnp.mean(values * values, axis=-1, keepdims=True) + RMS_EPS)
        out_ref[...] = (values * scale * gain_ref[...]).astype(BF16)


def normalize(x, gain):
    shape = jax.ShapeDtypeStruct((L, MODEL_WIDTH), BF16)
    step = 32
    return pl.pallas_call(
        normalize_kernel,
        name="normalize",
        grid=(L // step,),
        in_specs=[
            pl.BlockSpec((2, step, MODEL_WIDTH), lambda i: (0, i, 0)),
            pl.BlockSpec((1, MODEL_WIDTH), lambda i: (0, 0)),
        ],
        out_specs=[pl.BlockSpec((step, MODEL_WIDTH), lambda i: (i, 0))] * 2,
        out_shape=[shape, shape],
        compiler_params=params(),
        cost_estimate=cost(6 * 2 * L * MODEL_WIDTH, 8 * L * MODEL_WIDTH),
    )(x, gain.reshape(1, MODEL_WIDTH))


def eye_mask(n, m):
    return lax.broadcasted_iota(jnp.int32, (n, m), 0) == lax.broadcasted_iota(jnp.int32, (n, m), 1)


def column_of(row, n):
    return jnp.sum(jnp.where(eye_mask(n, row.shape[1]), row, 0.0), axis=1, keepdims=True)


def chunk_of(c, own_ref, other_ref, size=256):
    per = own_ref.shape[0] // size
    ref = own_ref if c < per else other_ref
    return ref[(c % per) * size : (c % per + 1) * size, :]


def partial_scores_kernel(q_ref, own_ref, other_ref, out_ref):
    q = q_ref[...]
    ones = jnp.ones((16, 256), BF16)
    rows = lax.broadcasted_iota(jnp.int32, (8, 256), 0)

    def square_row(block):
        values = block.astype(F32)
        head, rest = split(values * values)
        return (dot(ones, head, NT) + dot(ones, rest, NT))[0:8]

    q_row = square_row(jnp.concatenate([q, jnp.zeros((256 - 64, 256), BF16)], axis=0))
    for c in range(N_FSDP):
        passages = chunk_of(c, own_ref, other_ref)
        out_ref[c, 0:64, :] = dot(q, passages, NT)
        out_ref[c, 64:72, :] = jnp.where(
            rows == 0, square_row(passages), jnp.where(rows == 1, q_row, 0.0)
        )


def finish_scores_kernel(parts_ref, out_ref):
    total = parts_ref[0]
    for c in range(1, N_FSDP):
        total = total + parts_ref[c]
    p_norm = jnp.sqrt(total[64:65] + EPS_NORM)
    q_norm_row = jnp.sqrt(total[65:66] + EPS_NORM)
    q_norm = column_of(q_norm_row, 64)
    scores = total[0:64] / (q_norm * p_norm * SOFTMAX_TEMPER)
    rows = lax.broadcasted_iota(jnp.int32, (8, 256), 0)
    tail = jnp.where(rows == 0, p_norm, jnp.where(rows == 1, q_norm_row, 0.0))
    for c in range(N_FSDP):
        out_ref[c, 0:64, :] = scores
        out_ref[c, 64:72, :] = tail


def query_grad_kernel(s_ref, q_ref, pos_ref, own_ref, other_ref, grad_ref, w_ref, col_ref):
    top = jnp.max(s_ref[0, 0:64, :], axis=1, keepdims=True)
    for c in range(1, N_FSDP):
        top = jnp.maximum(top, jnp.max(s_ref[c, 0:64, :], axis=1, keepdims=True))
    norm = jnp.zeros((64, 1), F32)
    for c in range(N_FSDP):
        norm = norm + jnp.sum(jnp.exp(s_ref[c, 0:64, :] - top), axis=1, keepdims=True)
    q_norm = column_of(s_ref[0, 65:66, :], 64)
    place = pos_ref[...]
    lane = lax.broadcasted_iota(jnp.int32, (64, 256), 1)
    cross = jnp.zeros((64, 1), F32)
    total = jnp.zeros((64, 256), F32)
    for c in range(N_FSDP):
        s = s_ref[c, 0:64, :]
        p_norm = s_ref[c, 64:65, :]
        grad = jnp.exp(s - top) / norm - jnp.where(lane + 256 * c == place, 1.0, 0.0)
        terms = grad * s
        cross = cross + jnp.sum(terms, axis=1, keepdims=True)
        column = jnp.sum(terms, axis=0, keepdims=True)
        col_ref[c] = jnp.broadcast_to(column / (p_norm * p_norm), (8, 256))
        weight = grad / (p_norm * SOFTMAX_TEMPER)
        w_ref[c] = weight / q_norm
        head, rest = split(weight)
        both = dot(jnp.concatenate([head, rest], axis=0), chunk_of(c, own_ref, other_ref))
        total = total + both[0:64] + both[64:128]
    grad_ref[...] = total / q_norm - (cross / (q_norm * q_norm)) * q_ref[...].astype(F32)


def passage_terms_kernel(w_ref, col_ref, q_ref, own_ref, other_ref, keep_ref, give_ref):
    q = q_ref[...]
    twice = jnp.concatenate([q, q], axis=0)
    for c in range(N_FSDP):
        head, rest = split(w_ref[c])
        pulled = dot(jnp.concatenate([head, rest], axis=0), twice, TN)
        scale = column_of(col_ref[c, 0:1, :], 256)
        value = pulled - scale * chunk_of(c, own_ref, other_ref).astype(F32)
        out_ref = keep_ref if c < 4 else give_ref
        out_ref[(c % 4) * 256 : (c % 4 + 1) * 256, :] = value


def forward_kernel(
    scalar_ref, t0, t1, t2, t3, t4, t5, t6, t7, weight_ref, cos_ref, sin_ref,
    q_ref, k_ref, v_ref, p_ref, csum_ref, low_ref, up_ref,
    tok, wv, acc, lacc, tok_sem, w_sem,
):
    tokens = (t0, t1, t2, t3, t4, t5, t6, t7)
    head = scalar_ref[0]
    tok_copies = [
        pltpu.make_async_copy(t, tok.at[pl.ds(L * n, L)], tok_sem.at[n]) for n, t in enumerate(tokens)
    ]
    w_copies = [
        pltpu.make_async_copy(weight_ref.at[n], wv.at[n], w_sem.at[n]) for n in range(N_FSDP)
    ]
    w_copies[0].start()
    tok_copies[0].start()
    tok_copies[1].start()
    for n in range(1, N_FSDP):
        w_copies[n].start()
    for n in range(2, N_FSDP):
        tok_copies[n].start()

    cos = cos_ref[...]
    sin = sin_ref[...]
    causal = lax.broadcasted_iota(jnp.int32, (L, L), 0) >= lax.broadcasted_iota(jnp.int32, (L, L), 1)
    causal = jnp.concatenate([causal.astype(F32)] * GROUP, axis=0) > 0.5

    def rope(x):
        return (x * cos + pltpu.roll(x, HD // 2, 1) * sin).astype(BF16)

    @pl.loop(0, 4)
    def _(i):
        for n in range(4):

            @pl.when(i == n)
            def _():
                tok_copies[2 * n].wait()
                tok_copies[2 * n + 1].wait()

        rows = pl.ds(pl.multiple_of(i * 2 * L, 2 * L), 2 * L)
        for n in range(N_FSDP):

            @pl.when(i == 0)
            def _():
                w_copies[n].wait()

            x = tok[rows, ROWS * n : ROWS * (n + 1)]
            part = dot(x, wv[n, 0:ROWS, :])
            low_part = dot(x, wv[n, ROWS : ROWS + LOW, 0:ROWS], NT)
            if n == 0:
                acc[...] = part
                lacc[...] = low_part
            else:
                acc[...] += part
                lacc[...] += low_part

        @pl.when(i == 0)
        def _():
            up_ref[...] = jnp.zeros_like(up_ref)
            for j in range(GROUP + 2):
                tile = GROUP * head + j if j < GROUP else (HQ + HK * (j - GROUP)) + head
                shard = tile // 3
                lanes = pl.ds(pl.multiple_of((tile % 3) * HD, HD), HD)
                block = max(0, j - GROUP + 1)
                up_ref[ADAPTER_RANK * block : ADAPTER_RANK * (block + 1), HD * j : HD * (j + 1)] = (
                    wv[shard, ROWS + LOW : ROWS + LOW + ADAPTER_RANK, lanes]
                )

        low = lacc[...].astype(BF16)
        acc[...] += ADAPTER_SCALE * dot(low, up_ref[...])
        for s in range(2):
            n = 2 * i + s
            r = slice(L * s, L * (s + 1))
            low_ref[n] = low[r]
            q = jnp.concatenate([rope(acc[r, HD * j : HD * (j + 1)]) for j in range(GROUP)], axis=0)
            k = rope(acc[r, GROUP * HD : (GROUP + 1) * HD])
            q_ref[n] = q
            k_ref[n] = k
            v_ref[n] = acc[r, (GROUP + 1) * HD : (GROUP + 2) * HD].astype(BF16)
            scores = dot(q, k, NT) / math.sqrt(HD)
            scores = jnp.where(causal, scores, -1e30)
            e = jnp.exp(scores - jnp.max(scores, axis=1, keepdims=True))
            p = e / jnp.sum(e, axis=1, keepdims=True)
            p_ref[n] = p
            rounded = p.astype(BF16).astype(F32)
            csum_ref[n] = jnp.zeros((8, L), F32)
            for j in range(GROUP):
                csum_ref[n, j : j + 1, :] = jnp.sum(rounded[L * j : L * (j + 1)], axis=0, keepdims=True)


def forward(scalars, tokens, weight, cos, sin):
    n = len(tokens)
    return pl.pallas_call(
        forward_kernel,
        name="attention_forward",
        in_specs=[SMEM] + [ANY] * (n + 1) + [VMEM, VMEM],
        out_specs=[VMEM] * 7,
        out_shape=[
            jax.ShapeDtypeStruct((n, GROUP * L, HD), BF16),
            jax.ShapeDtypeStruct((n, L, HD), BF16),
            jax.ShapeDtypeStruct((n, L, HD), BF16),
            jax.ShapeDtypeStruct((n, GROUP * L, L), F32),
            jax.ShapeDtypeStruct((n, 8, L), F32),
            jax.ShapeDtypeStruct((n, L, LOW), BF16),
            jax.ShapeDtypeStruct((LOW, COLS), BF16),
        ],
        scratch_shapes=[
            pltpu.VMEM((n * L, MODEL_WIDTH), BF16),
            pltpu.VMEM((N_FSDP, ROWS + PACK, COLS), BF16),
            pltpu.VMEM((2 * L, COLS), F32),
            pltpu.VMEM((2 * L, LOW), F32),
            pltpu.SemaphoreType.DMA((n,)),
            pltpu.SemaphoreType.DMA((N_FSDP,)),
        ],
        compiler_params=params(),
        cost_estimate=cost(2 * n * L * MODEL_WIDTH * (COLS + LOW), 20e6),
    )(scalars, *tokens, weight, cos, sin)


def backward_kernel(
    scalar_ref, t0, t1, t2, t3, t4, t5, t6, t7, g_own, g_other, q_ref, k_ref, v_ref, p_ref,
    csum_ref, low_ref, up_ref, cos_ref, sin_ref, out_ref, tok, dlow, dup, g_all, tok_sem,
):
    tokens = (t0, t1, t2, t3, t4, t5, t6, t7)
    head = scalar_ref[0]
    core = scalar_ref[1]
    copies = [
        pltpu.make_async_copy(t, tok.at[pl.ds(L * n, L)], tok_sem.at[n]) for n, t in enumerate(tokens)
    ]
    for copy in copies:
        copy.start()
    cos = cos_ref[...]
    sin = sin_ref[...]
    up = up_ref[...]
    g_all[...] = jnp.zeros_like(g_all)
    shard_row = lax.broadcasted_iota(jnp.int32, (N_FSDP, 256), 0)
    for n in range(8):
        ref = (g_own, g_other)[(n // 2) % 2]
        rows = ref[(n // 4) * 2 + n % 2] / L
        for j in range(2):
            row = jnp.sum(jnp.where(shard_row == 2 * head + j, rows, 0.0), axis=0, keepdims=True)
            g_all[n, 2 * j : 2 * j + 1, :] = row[:, 0:HD]
            g_all[n, 2 * j + 1 : 2 * j + 2, :] = row[:, HD : 2 * HD]
    dup[...] = jnp.zeros_like(dup)

    def unrope(x):
        return x * cos + pltpu.roll(x * sin, HD // 2, 1)

    @pl.loop(0, 8)
    def _(n):
        g = g_all[n]
        g_head, g_rest = split(g)
        v = v_ref[n]
        k = k_ref[n]
        q = q_ref[n]
        u = dot(jnp.concatenate([g_head, g_rest], axis=0), v, NT)
        u = u[0:8] + u[8:16]
        parts = []
        for j in range(GROUP):
            p = p_ref[n, L * j : L * (j + 1), :]
            pu = p * u[j : j + 1]
            parts.append((pu - p * jnp.sum(pu, axis=1, keepdims=True)) * (1.0 / math.sqrt(HD)))
        ds_head, ds_rest = split(jnp.concatenate(parts, axis=0))
        dq = dot(ds_head, k) + dot(ds_rest, k)
        dk = dot(ds_head, q, TN) + dot(ds_rest, q, TN)
        c_head, c_rest = split(csum_ref[n])
        dv = dot(
            jnp.concatenate([c_head, c_rest, c_head, c_rest], axis=0),
            jnp.concatenate([g_head, g_head, g_rest, g_rest], axis=0),
            TN,
        )
        dproj = jnp.concatenate(
            [unrope(dq[L * j : L * (j + 1)]) for j in range(GROUP)] + [unrope(dk), dv], axis=1
        )
        head_part, rest_part = split(ADAPTER_SCALE * dproj)
        low_grad = dot(up, head_part, NT) + dot(up, rest_part, NT)
        l_head, l_rest = split(low_grad)
        lanes = pl.ds(pl.multiple_of(n * L, L), L)
        dlow[0:LOW, lanes] = l_head
        dlow[LOW : 2 * LOW, lanes] = l_rest
        low = low_ref[n]
        dup[...] += dot(low, head_part, TN) + dot(low, rest_part, TN)

    for half in range(2):
        spot = core if half == 0 else 1 - core
        if half == 1:
            out_ref[pl.ds(spot, 1), RING // 2 : RING] = jnp.zeros((1, RING // 2, N_FSDP, 8, HD), F32)
    far = 1 - core
    for j in range(GROUP + 2):
        tile = GROUP * head + j if j < GROUP else (HQ + HK * (j - GROUP)) + head
        shard = tile // 3
        block = max(0, j - GROUP + 1)
        value = dup[ADAPTER_RANK * block : ADAPTER_RANK * (block + 1), HD * j : HD * (j + 1)]
        for i in range(2):
            out_ref[far, RING // 2 + 2 * (tile % 3) + i, shard] = value[8 * i : 8 * (i + 1)]
    for copy in copies:
        copy.wait()
    for f in range(N_FSDP):
        both = dot(dlow[...], tok[:, ROWS * f : ROWS * (f + 1)])
        value = both[0:LOW] + both[LOW : 2 * LOW]
        for b in range(ROWS // HD):
            for i in range(LOW // 8):
                group = b * (LOW // 8) + i
                spot = core if group < RING else 1 - core
                out_ref[spot, group % RING, f] = value[8 * i : 8 * (i + 1), HD * b : HD * (b + 1)]


def backward(scalars, tokens, g_own, g_other, saved, cos, sin):
    n = len(tokens)
    return pl.pallas_call(
        backward_kernel,
        name="attention_backward",
        in_specs=[SMEM] + [ANY] * n + [VMEM] * 11,
        out_specs=VMEM,
        out_shape=jax.ShapeDtypeStruct((2, RING, N_FSDP, 8, HD), F32),
        scratch_shapes=[
            pltpu.VMEM((n * L, MODEL_WIDTH), BF16),
            pltpu.VMEM((2 * LOW, n * L), BF16),
            pltpu.VMEM((LOW, COLS), F32),
            pltpu.VMEM((n, 8, HD), F32),
            pltpu.SemaphoreType.DMA((n,)),
        ],
        compiler_params=params(),
        cost_estimate=cost(2 * n * L * MODEL_WIDTH * 2 * LOW, 15e6),
    )(scalars, *tokens, g_own, g_other, *saved, cos, sin)


def finish_kernel(scalar_ref, own_ref, other_ref, down_ref, up_ref):
    core = scalar_ref[1]
    squares = jnp.sum(own_ref[:, 8:9, :], axis=0) + jnp.sum(other_ref[:, 8:9, :], axis=0)
    grad_norm = jnp.sqrt(jnp.sum(squares, axis=1, keepdims=True))
    unit_scale = math.sqrt(3 * MODEL_WIDTH * ADAPTER_RANK + (HQ + 2 * HK) * HD * ADAPTER_RANK)
    factor = jnp.minimum(1.0, MAX_NORM / (grad_norm + 1e-06)) * unit_scale

    def tile(group):
        half, spot = divmod(group, RING)
        a = own_ref[spot, 0:8, :]
        b = other_ref[spot, 0:8, :]
        return jnp.where(core == half, a, b) * factor

    for b in range(ROWS // HD):
        for i in range(LOW // 8):
            down_ref[8 * i : 8 * (i + 1), HD * b : HD * (b + 1)] = tile(b * (LOW // 8) + i)
    for b in range(UP_ROWS // HD):
        for i in range(ADAPTER_RANK // 8):
            group = (ROWS // HD) * (LOW // 8) + 2 * b + i
            up_ref[8 * i : 8 * (i + 1), HD * b : HD * (b + 1)] = tile(group)


def dp_pairs(move):
    pairs = []
    for d in range(N_DP):
        z, y, core = move(d // 4, (d // 2) % 2, d % 2)
        pairs.append((d, (z % (N_DP // 4)) * 4 + y * 2 + core))
    return pairs


SIBLING = dp_pairs(lambda z, y, c: (z, y, 1 - c))
UPWARD = dp_pairs(lambda z, y, c: (z + 1, y, c))
DOWNWARD = dp_pairs(lambda z, y, c: (z - 1, y, c))
CORE_GROUPS = [[2 * i + c for i in range(RING)] for c in range(2)]


def to_sibling(x):
    return lax.ppermute(x, "dp", SIBLING)


def swap_dp(x):
    return lax.all_to_all(x, "dp", 0, 0, axis_index_groups=CORE_GROUPS)


def swap_fsdp(x):
    return lax.all_to_all(x, "fsdp", 0, 0)


def shards(
    query_rows, passage_rows, positive, layer_input, gain, frozen_weight, down_maps, up_maps
):
    dp = lax.axis_index("dp")
    core = dp % 2
    head = 2 * ((dp // 4) % 2) + core
    scalars = jnp.stack([head, core]).astype(jnp.int32)
    cos, sin = (jnp.asarray(t) for t in rope_tables())

    columns = [
        lax.dynamic_slice_in_dim(frozen_weight, GROUP * HD * head, GROUP * HD, 1),
        lax.dynamic_slice_in_dim(frozen_weight, HQ * HD + HD * head, HD, 1),
        lax.dynamic_slice_in_dim(frozen_weight, (HQ + HK) * HD + HD * head, HD, 1),
    ]
    packed = jnp.concatenate(
        [
            jnp.concatenate(columns, axis=1),
            jnp.pad(down_maps.T, ((0, 0), (0, COLS - ROWS))),
            jnp.pad(up_maps.T, ((0, 0), (0, COLS - UP_ROWS))),
        ],
        axis=0,
    )
    weight = lax.all_gather(packed, "fsdp", axis=0)

    first, second = normalize(layer_input, gain)
    from_below = lax.ppermute(first, "dp", UPWARD)
    from_above = lax.ppermute(second, "dp", DOWNWARD)
    tokens = [first, second, to_sibling(first), to_sibling(second)]
    tokens += [from_below, from_above, to_sibling(from_below), to_sibling(from_above)]

    own = swap_dp(jnp.broadcast_to(passage_rows[None], (RING, 64, 256))).reshape(RING * 64, 256)
    other = to_sibling(own)
    partial = pl.pallas_call(
        partial_scores_kernel,
        name="partial_scores",
        out_shape=jax.ShapeDtypeStruct((N_FSDP, 72, 256), F32),
        compiler_params=params(),
        cost_estimate=cost(2 * 64 * 256 * 2048 * 2, 2e6),
    )(query_rows, own, other)
    scores = pl.pallas_call(
        finish_scores_kernel,
        name="finish_scores",
        out_shape=jax.ShapeDtypeStruct((N_FSDP, 72, 256), F32),
        compiler_params=params(),
        cost_estimate=cost(64 * 256 * 20, 1.2e6),
    )(swap_fsdp(partial))
    scores = swap_fsdp(scores)
    owner = positive // 64
    place = (
        jnp.where(owner % 2 == core, 0, RING * 64) + (owner // 2) * 64 + positive % 64
    ).astype(jnp.int32)
    query_grad, pulls, columns_sum = pl.pallas_call(
        query_grad_kernel,
        name="query_grad",
        out_shape=[
            jax.ShapeDtypeStruct((64, 256), F32),
            jax.ShapeDtypeStruct((N_FSDP, 64, 256), F32),
            jax.ShapeDtypeStruct((N_FSDP, 8, 256), F32),
        ],
        compiler_params=params(),
        cost_estimate=cost(2 * 128 * 256 * 2048, 2e6),
    )(scores, query_rows, place.reshape(64, 1), own, other)
    g = swap_fsdp(query_grad[:16].reshape(N_FSDP, 2, 256))
    g = jnp.swapaxes(g, 0, 1)
    g_own = jnp.concatenate(
        [g, lax.ppermute(g[0:1], "dp", UPWARD), lax.ppermute(g[1:2], "dp", DOWNWARD)], axis=0
    )
    g_other = to_sibling(g_own)

    keep, give = pl.pallas_call(
        passage_terms_kernel,
        name="passage_terms",
        out_shape=[jax.ShapeDtypeStruct((RING * 64, 256), F32)] * 2,
        compiler_params=params(),
        cost_estimate=cost(2 * 128 * 256 * 2048, 6e6),
    )(pulls, columns_sum, query_rows, own, other)
    sent = (keep + to_sibling(give)).astype(BF16).reshape(RING, 64, 256)
    passage_grad = jnp.sum(swap_dp(sent).astype(F32), axis=0)

    *saved, = forward(scalars, tokens, weight, cos, sin)
    grads = backward(scalars, tokens, g_own, g_other, saved, cos, sin)
    summed = (grads[0] + to_sibling(grads[1])).astype(BF16)
    piece = jnp.sum(swap_dp(summed).astype(F32), axis=0)
    pieces = jnp.sum(swap_fsdp(jnp.broadcast_to(piece[None], (N_FSDP,) + piece.shape)), axis=0)
    squares = jnp.sum(pieces * pieces, axis=(0, 1))
    mine = lax.dynamic_index_in_dim(pieces, lax.axis_index("fsdp"), 0, keepdims=False)
    tail = jnp.concatenate([mine, jnp.broadcast_to(squares[None], (8, HD))], axis=0)
    tail_own = swap_dp(jnp.broadcast_to(tail[None], (RING, 16, HD)))
    tail_other = to_sibling(tail_own)
    down, up = pl.pallas_call(
        finish_kernel,
        name="finish_clip",
        in_specs=[SMEM, VMEM, VMEM],
        out_shape=[
            jax.ShapeDtypeStruct((LOW, ROWS), F32),
            jax.ShapeDtypeStruct((ADAPTER_RANK, UP_ROWS), F32),
        ],
        compiler_params=params(),
    )(scalars, tail_own, tail_other)
    return query_grad, passage_grad, down.T, up.T


def solution(mesh):
    in_specs = (
        P("dp", "fsdp"),
        P("dp", "fsdp"),
        P("dp"),
        P(("dp", "fsdp"), None, None),
        P(),
        P("fsdp", None),
        P("fsdp", None),
        P("fsdp", None),
    )
    out_specs = (P("dp", "fsdp"), P("dp", "fsdp"), P("fsdp", None), P("fsdp", None))
    return jax.shard_map(shards, mesh=mesh, in_specs=in_specs, out_specs=out_specs, check_vma=False)
```

time: 945 us -> 266 us (0.28)
  waiting for transfers between devices: 544 us -> 114 us
  blocking collectives: 280 us -> 12.2 us
  starting transfers between devices: 3.79 us -> 66.4 us
  matrix products: 49.9 us -> 0 us
  Pallas kernels: 0 us -> 43.4 us
  other arithmetic: 20.3 us -> 5.5 us
  local copies, waits for them, and re-layouts: 18.6 us -> 6.24 us
    all_gather x2 -> x1, waiting for transfers between devices: 242 us -> 0.02 us  [shards(): weight = lax.all_gather(packed, 'fsdp', axis=0)]
    reduce_scatter x3 -> x0, waiting for transfers between devices: 164 us -> none  [the longest x1 97.1 us: shards(): lax.psum_scatter(pulled_gradient / (passage_norm_every * SOFTMAX_TEMPER)[...]
    psum x3 -> x0, blocking collectives: 161 us -> none  [the longest x1 129 us: shards(): down_shard, up_shard = lax.psum((down_shard, up_shard), 'dp')]
    psum x2 -> x0, waiting for transfers between devices: 133 us -> none  [the longest x1 115 us: shards(): down_shard, up_shard = lax.psum((down_shard, up_shard), 'dp')]
    all_to_all x1 -> x7, waiting for transfers between devices: 3.96 us -> 77.9 us  [the longest x4 44.6 us: swap_dp(): return lax.all_to_all(x, 'dp', 0, 0, axis_index_groups=CORE_GROUPS)]
    unnamed x1 -> x0, blocking collectives: 72.9 us -> none
    dot_general x20 -> x0, matrix products: 49.9 us -> none  [the longest x1 12.3 us: shards(): jnp.dot(normalized_input, weight_piece, preferred_element_type=jnp.float32)]
    all_to_all x1 -> x7, starting transfers between devices: 3.34 us -> 51.2 us  [the longest x3 26.8 us: swap_fsdp(): return lax.all_to_all(x, 'fsdp', 0, 0)]
  transfers between devices with their start and end apart: 8 -> 21, of which waited for: 7 -> 11; matrix products, arithmetic and copies ran while one was open for 3% -> 2% of each run, Pallas kernels for 0% -> 12%
where the time goes in v1:
time: 266 us; the launch traced here: 262 us
  waiting for transfers between devices  114 us (43%)
  starting transfers between devices  66.4 us (25%)
  Pallas kernels  43.4 us (16%)
  between operations  14.3 us (5%)
  blocking collectives  12.2 us (5%)
  local copies, waits for them, and re-layouts  6.24 us (2%)
  other arithmetic  5.5 us (2%)
    all_to_all x4, waiting for transfers between devices, swap_dp(): return lax.all_to_all(x, 'dp', 0, 0, axis_index_groups=CORE_GROUPS)  44.6 us
    all_to_all x3, waiting for transfers between devices, swap_fsdp(): return lax.all_to_all(x, 'fsdp', 0, 0)  33.4 us
    ppermute x1, waiting for transfers between devices, shards(): lax.ppermute(g[1:2], 'dp', DOWNWARD)  28.9 us
    all_to_all x3, starting transfers between devices, swap_fsdp(): return lax.all_to_all(x, 'fsdp', 0, 0)  26.8 us
    all_to_all x4, starting transfers between devices, swap_dp(): return lax.all_to_all(x, 'dp', 0, 0, axis_index_groups=CORE_GROUPS)  24.4 us
    pallas_call x1, Pallas kernels, forward(): pl.pallas_call(forward_kernel, name='attention_forward', in_specs=[SMEM]...  23.2 us
    ppermute x9, starting transfers between devices, to_sibling(): return lax.ppermute(x, 'dp', SIBLING)  12.5 us
    all_to_all x1, blocking collectives, swap_fsdp(): return lax.all_to_all(x, 'fsdp', 0, 0)  12.2 us
  transfers between devices with their start and end apart: 21, of which 11 were waited for; matrix products, arithmetic and copies ran while one was open for 2% of the time, Pallas kernels for 12%

profile of v1, /device:TPU:1, one launch (start us, length us, event | category | flops | bytes accessed | tf_op | source)
XLA Modules:
  0.0 262.2 jit_solution(16596444496892448937)
XLA Ops:
  7.3 1.1 constant_dynamic-slice_fusion.2
  8.4 1.0 constant_dynamic-slice_fusion.1
  9.4 2.0 fusion.4
  11.4 0.9 broadcast_in_dim.14
  12.3 11.7 %all-to-all-start = ((bf16[16,64,256]{2,1,0:T(8,128)(2,1)}), bf16[16,64,256]{2,1,0:T(8,128)(2,1)S(1)}, u32[]{:S(2)}, u32[]{:S(2)}) async-start(bf16[16,64,256]{2,1,0:T(8,128)(2,1)} %broadcast_in_dim.14), calls=%async_computation | async-start | bytes 1048576 | tf_op jit(solution)/shard_map/all_to_all | solution.py:456
  24.1 2.5 normalize.1
  26.6 1.4 collective-permute-start.4
  27.9 1.3 collective-permute-start.5
  29.2 13.7 %all-to-all-done = bf16[16,64,256]{2,1,0:T(8,128)(2,1)S(1)} async-done(((bf16[16,64,256]{2,1,0:T(8,128)(2,1)}), bf16[16,64,256]{2,1,0:T(8,128)(2,1)S(1)}, u32[]{:S(2)}, u32[]{:S(2)}) %all-to-all-start) | async-done | bytes 524320 | tf_op jit(solution)/shard_map/all_to_all | solution.py:456
  42.9 3.3 %collective-permute-start = (bf16[1024,256]{1,0:T(8,128)(2,1)S(1)}, bf16[1024,256]{1,0:T(8,128)(2,1)S(1)}, u32[]{:S(2)}, u32[]{:S(2)}) collective-permute-start(bf16[1024,256]{1,0:T(8,128)(2,1)S(1)} %bitcast.25), channel_id=1, source_target_pairs={{0,8},{8,0},{16,24},{24,16},{32,40},{40,32},{48,56},{56,48},{64,72... | collective-permute-start | bytes 1572872 | tf_op jit(solution)/shard_map/ppermute | solution.py:452
  46.2 1.5 collective-permute-done.other_ref
  47.8 1.9 partial_scores.1
  49.7 17.7 %all-to-all-start.1 = ((f32[8,72,256]{2,1,0:T(8,128)}), f32[8,72,256]{2,1,0:T(8,128)S(1)}, u32[]{:S(2)}, u32[]{:S(2)}) async-start(f32[8,72,256]{2,1,0:T(8,128)} %partial_scores.1), calls=%async_computation.1 | async-start | bytes 1179648 | tf_op jit(solution)/shard_map/all_to_all | solution.py:460
  67.3 0.7 collective-permute-start.2
  68.1 0.4 collective-permute-start.6
  68.6 13.0 %all-to-all-done.1.parts_ref = f32[8,72,256]{2,1,0:T(8,128)S(1)} async-done(((f32[8,72,256]{2,1,0:T(8,128)}), f32[8,72,256]{2,1,0:T(8,128)S(1)}, u32[]{:S(2)}, u32[]{:S(2)}) %all-to-all-start.1) | async-done | bytes 589856 | tf_op jit(solution)/shard_map/all_to_all | solution.py:460
  81.6 1.0 finish_scores.1
  82.6 5.7 %all-to-all-start.2 = ((f32[8,72,256]{2,1,0:T(8,128)}), f32[8,72,256]{2,1,0:T(8,128)S(1)}, u32[]{:S(2)}, u32[]{:S(2)}) async-start(f32[8,72,256]{2,1,0:T(8,128)} %finish_scores.1), calls=%async_computation.2 | async-start | bytes 1179648 | tf_op jit(solution)/shard_map/all_to_all | solution.py:460
  88.5 14.0 %all-to-all-done.2.s_ref = f32[8,72,256]{2,1,0:T(8,128)S(1)} async-done(((f32[8,72,256]{2,1,0:T(8,128)}), f32[8,72,256]{2,1,0:T(8,128)S(1)}, u32[]{:S(2)}, u32[]{:S(2)}) %all-to-all-start.2) | async-done | bytes 589856 | tf_op jit(solution)/shard_map/all_to_all | solution.py:460
  102.4 1.3 query_grad.1
  103.7 0.7 slice.15
  104.5 12.2 %all_to_all.40 = f32[8,2,256]{2,1,0:T(2,128)S(1)} all-to-all(f32[8,2,256]{2,1,0:T(2,128)S(1)} %reshape.31), channel_id=1, replica_groups=mesh['dp'=32,'fsdp'=8] {'fsdp'}, dimensions={0} | all-to-all | bytes 32768 | tf_op jit(solution)/shard_map/all_to_all | solution.py:460
  116.7 3.7 %collective-permute-done.8 = f32[1,8,256]{2,1,0:T(8,128)S(1)} collective-permute-done((f32[1,8,256]{2,1,0:T(8,128)S(1)}, f32[1,8,256]{2,1,0:T(8,128)S(1)}, u32[]{:S(2)}, u32[]{:S(2)}) %collective-permute-start.8) | collective-permute-done | bytes 8224 | tf_op jit(solution)/shard_map/ppermute | solution.py:528
  120.5 28.9 %collective-permute-done.9 = f32[1,8,256]{2,1,0:T(8,128)S(1)} collective-permute-done((f32[1,8,256]{2,1,0:T(8,128)S(1)}, f32[1,8,256]{2,1,0:T(8,128)S(1)}, u32[]{:S(2)}, u32[]{:S(2)}) %collective-permute-start.9) | collective-permute-done | bytes 8224 | tf_op jit(solution)/shard_map/ppermute | solution.py:528
  149.4 3.8 %collective-permute-start.10 = (f32[4,8,256]{2,1,0:T(8,128)S(1)}, f32[4,8,256]{2,1,0:T(8,128)S(1)}, u32[]{:S(2)}, u32[]{:S(2)}) collective-permute-start(f32[4,8,256]{2,1,0:T(8,128)S(1)} %pad_maximum_fusion.g_own), channel_id=1, source_target_pairs={{0,8},{8,0},{16,24},{24,16},{32,40},{40,32},{48,56},{56,48},{64,72... | collective-permute-start | bytes 98312 | tf_op jit(solution)/shard_map/ppermute | solution.py:452
  153.3 23.2 %attention_forward.1 = (bf16[8,512,128]{2,1,0:T(8,128)(2,1)S(1)}, bf16[8,128,128]{2,1,0:T(8,128)(2,1)S(1)}, bf16[8,128,128]{2,1,0:T(8,128)(2,1)S(1)}, f32[8,512,...) custom-call(s32[2]{0:T(128)S(1)} %pad_add_fusion.scalar_ref, ...), custom_call_target="tpu_custom_call" | custom-call | flops 6845104128 | bytes 20000000 | tf_op jit(solution)/shard_map/attention_forward/pallas_call | solution.py:280
  176.5 1.0 copy-done.1
  177.5 10.7 %attention_backward.1 = f32[2,16,8,8,128]{4,3,2,1,0:T(8,128)S(1)} custom-call(s32[2]{0:T(128)S(1)} %pad_add_fusion.scalar_ref, bf16[128,4096]{1,0:T(8,128)(2,1)} %get-tuple-element.25.t0, bf16[128,4096]{1,0:T(8,128)(2,1)} %get-tuple-element.26.t1, bf16[128,4096]{1,0:T(8,128)(2,1)S(1)} %collective-permute-done.2.t2, ...), custom_call_target="tpu_custom_call" | custom-call | flops 805306368 | bytes 15000000 | tf_op jit(solution)/shard_map/attention_backward/pallas_call | solution.py:397
  188.3 0.1 collective-permute-start.11
  188.4 1.9 collective-permute-done.11
  190.3 0.8 fusion.6
  191.1 5.5 %all-to-all-start.5 = ((bf16[16,8,8,128]{3,2,1,0:T(8,128)(2,1)}), bf16[16,8,8,128]{3,2,1,0:T(8,128)(2,1)}, u32[]{:S(2)}, u32[]{:S(2)}) async-start(bf16[16,8,8,128]{3,2,1,0:T(8,128)(2,1)} %fusion.6), calls=%async_computation.5 | async-start | bytes 524288 | tf_op jit(solution)/shard_map/all_to_all | solution.py:456
  196.6 1.5 passage_terms.1
  198.1 0.4 collective-permute-start.1
  198.6 11.0 %all-to-all-done.5 = bf16[16,8,8,128]{3,2,1,0:T(8,128)(2,1)} async-done(((bf16[16,8,8,128]{3,2,1,0:T(8,128)(2,1)}), bf16[16,8,8,128]{3,2,1,0:T(8,128)(2,1)}, u32[]{:S(2)}, u32[]{:S(2)}) %all-to-all-start.5) | async-done | bytes 262176 | tf_op jit(solution)/shard_map/all_to_all | solution.py:456
  209.6 1.0 convert_reduce_fusion.1
  210.6 0.7 broadcast_in_dim.16
  211.3 3.4 %all-to-all-start.6 = ((f32[8,8,8,128]{3,2,1,0:T(8,128)}), f32[8,8,8,128]{3,2,1,0:T(8,128)S(1)}, u32[]{:S(2)}, u32[]{:S(2)}) async-start(f32[8,8,8,128]{3,2,1,0:T(8,128)} %broadcast_in_dim.16), calls=%async_computation.6 | async-start | bytes 524288 | tf_op jit(solution)/shard_map/all_to_all | solution.py:460
  214.7 6.4 %all-to-all-done.6 = f32[8,8,8,128]{3,2,1,0:T(8,128)S(1)} async-done(((f32[8,8,8,128]{3,2,1,0:T(8,128)}), f32[8,8,8,128]{3,2,1,0:T(8,128)S(1)}, u32[]{:S(2)}, u32[]{:S(2)}) %all-to-all-start.6) | async-done | bytes 262176 | tf_op jit(solution)/shard_map/all_to_all | solution.py:460
  221.1 0.7 broadcast_in_dim.18
  221.8 3.5 %all-to-all-start.7 = ((f32[16,16,128]{2,1,0:T(8,128)}), f32[16,16,128]{2,1,0:T(8,128)S(1)}, u32[]{:S(2)}, u32[]{:S(2)}) async-start(f32[16,16,128]{2,1,0:T(8,128)} %broadcast_in_dim.18), calls=%async_computation.7 | async-start | bytes 262144 | tf_op jit(solution)/shard_map/all_to_all | solution.py:456
  225.3 0.9 add_convert_fusion
  226.2 9.1 %all-to-all-done.7.own_ref = f32[16,16,128]{2,1,0:T(8,128)S(1)} async-done(((f32[16,16,128]{2,1,0:T(8,128)}), f32[16,16,128]{2,1,0:T(8,128)S(1)}, u32[]{:S(2)}, u32[]{:S(2)}) %all-to-all-start.7) | async-done | bytes 131104 | tf_op jit(solution)/shard_map/all_to_all | solution.py:456
  235.3 3.6 %all-to-all-start.3 = ((bf16[16,64,256]{2,1,0:T(8,128)(2,1)}), bf16[16,64,256]{2,1,0:T(8,128)(2,1)S(1)}, u32[]{:S(2)}, u32[]{:S(2)}) async-start(bf16[16,64,256]{2,1,0:T(8,128)(2,1)} %bitcast.2), calls=%async_computation.3 | async-start | bytes 1048576 | tf_op jit(solution)/shard_map/all_to_all | solution.py:456
  238.9 3.6 %collective-permute-start.12 = (f32[16,16,128]{2,1,0:T(8,128)S(1)}, f32[16,16,128]{2,1,0:T(8,128)S(1)}, u32[]{:S(2)}, u32[]{:S(2)}) collective-permute-start(f32[16,16,128]{2,1,0:T(8,128)S(1)} %all-to-all-done.7.own_ref), channel_id=1, source_target_pairs={{0,8},{8,0},{16,24},{24,16},{32,40},{40,32},{48,56},{56,48},{64,72... | collective-permute-start | bytes 393224 | tf_op jit(solution)/shard_map/ppermute | solution.py:452
  242.5 10.8 %all-to-all-done.3 = bf16[16,64,256]{2,1,0:T(8,128)(2,1)S(1)} async-done(((bf16[16,64,256]{2,1,0:T(8,128)(2,1)}), bf16[16,64,256]{2,1,0:T(8,128)(2,1)S(1)}, u32[]{:S(2)}, u32[]{:S(2)}) %all-to-all-start.3) | async-done | bytes 524320 | tf_op jit(solution)/shard_map/all_to_all | solution.py:456
  253.3 0.7 convert_reduce_fusion
  254.0 1.3 finish_clip.1
  (44 shorter events, 0.7 us)
Async XLA Ops:
  7.2 146.1 %all-gather.3.cloned.1.call-start = ((), (), s32[]{:S(2)}) async-start(), calls=%async_computation.8 | async-start | bytes 7962624 | tf_op jit(solution)/shard_map/all_gather | solution.py:485
  8.3 3.1 %copy-start.6 = (bf16[64,256]{1,0:T(8,128)(2,1)S(1)}, bf16[64,256]{1,0:T(8,128)(2,1)}, u32[]{:S(2)}) copy-start(bf16[64,256]{1,0:T(8,128)(2,1)} %param.11) | copy-start | bytes 98308
  9.4 14.7 %copy-start = (bf16[2,128,4096]{2,1,0:T(8,128)(2,1)S(1)}, bf16[2,128,4096]{2,1,0:T(8,128)(2,1)}, u32[]{:S(2)}) copy-start(bf16[2,128,4096]{2,1,0:T(8,128)(2,1)} %x_ref.1) | copy-start | bytes 6291460
  9.4 14.7 %copy-start.5 = (f32[4096]{0:T(1024)S(1)}, f32[4096]{0:T(1024)}, u32[]{:S(2)}) copy-start(f32[4096]{0:T(1024)} %param.14) | copy-start | bytes 49156
  11.4 36.4 %copy-start.2 = (bf16[64,256]{1,0:T(8,128)(2,1)S(1)}, bf16[64,256]{1,0:T(8,128)(2,1)}, u32[]{:S(2)}) copy-start(bf16[64,256]{1,0:T(8,128)(2,1)} %q_ref.5) | copy-start | bytes 98308
  12.3 30.6 %all-to-all-start = ((bf16[16,64,256]{2,1,0:T(8,128)(2,1)}), bf16[16,64,256]{2,1,0:T(8,128)(2,1)S(1)}, u32[]{:S(2)}, u32[]{:S(2)}) async-start(bf16[16,64,256]{2,1,0:T(8,128)(2,1)} %broadcast_in_dim.14), calls=%async_computation | async-start | bytes 1048576 | tf_op jit(solution)/shard_map/all_to_all | solution.py:456
  26.6 41.5 %collective-permute-start.4 = (bf16[128,4096]{1,0:T(8,128)(2,1)}, bf16[128,4096]{1,0:T(8,128)(2,1)}, u32[]{:S(2)}, u32[]{:S(2)}) collective-permute-start(bf16[128,4096]{1,0:T(8,128)(2,1)} %get-tuple-element.25.t0), channel_id=1, source_target_pairs={{0,32},{8,40},{16,48},{24,56},{32,64},{40,72},{48,80},{56,88},{64,... | collective-permute-start | bytes 3145736 | tf_op jit(solution)/shard_map/ppermute | solution.py:488
  27.9 40.6 %collective-permute-start.5 = (bf16[128,4096]{1,0:T(8,128)(2,1)}, bf16[128,4096]{1,0:T(8,128)(2,1)}, u32[]{:S(2)}, u32[]{:S(2)}) collective-permute-start(bf16[128,4096]{1,0:T(8,128)(2,1)} %get-tuple-element.26.t1), channel_id=1, source_target_pairs={{0,224},{8,232},{16,240},{24,248},{32,0},{40,8},{48,16},{56,24},{6... | collective-permute-start | bytes 3145736 | tf_op jit(solution)/shard_map/ppermute | solution.py:489
  42.9 4.8 %collective-permute-start = (bf16[1024,256]{1,0:T(8,128)(2,1)S(1)}, bf16[1024,256]{1,0:T(8,128)(2,1)S(1)}, u32[]{:S(2)}, u32[]{:S(2)}) collective-permute-start(bf16[1024,256]{1,0:T(8,128)(2,1)S(1)} %bitcast.25), channel_id=1, source_target_pairs={{0,8},{8,0},{16,24},{24,16},{32,40},{40,32},{48,56},{56,48},{64,72... | collective-permute-start | bytes 1572872 | tf_op jit(solution)/shard_map/ppermute | solution.py:452
  49.7 38.7 %copy-start.7 = (s32[64]{0:T(128)S(1)}, s32[64]{0:T(128)}, u32[]{:S(2)}) copy-start(s32[64]{0:T(128)} %param.12) | copy-start | bytes 772
  49.7 32.0 %all-to-all-start.1 = ((f32[8,72,256]{2,1,0:T(8,128)}), f32[8,72,256]{2,1,0:T(8,128)S(1)}, u32[]{:S(2)}, u32[]{:S(2)}) async-start(f32[8,72,256]{2,1,0:T(8,128)} %partial_scores.1), calls=%async_computation.1 | async-start | bytes 1179648 | tf_op jit(solution)/shard_map/all_to_all | solution.py:460
  67.3 85.9 %collective-permute-start.2 = (bf16[128,4096]{1,0:T(8,128)(2,1)}, bf16[128,4096]{1,0:T(8,128)(2,1)S(1)}, u32[]{:S(2)}, u32[]{:S(2)}) collective-permute-start(bf16[128,4096]{1,0:T(8,128)(2,1)} %get-tuple-element.25.t0), channel_id=1, source_target_pairs={{0,8},{8,0},{16,24},{24,16},{32,40},{40,32},{48,56},{56,48},{64,72... | collective-permute-start | bytes 3145736 | tf_op jit(solution)/shard_map/ppermute | solution.py:452
  68.0 85.3 %collective-permute-start.3 = (bf16[128,4096]{1,0:T(8,128)(2,1)}, bf16[128,4096]{1,0:T(8,128)(2,1)}, u32[]{:S(2)}, u32[]{:S(2)}) collective-permute-start(bf16[128,4096]{1,0:T(8,128)(2,1)} %get-tuple-element.26.t1), channel_id=1, source_target_pairs={{0,8},{8,0},{16,24},{24,16},{32,40},{40,32},{48,56},{56,48},{64,72... | collective-permute-start | bytes 3145736 | tf_op jit(solution)/shard_map/ppermute | solution.py:452
  68.1 85.2 %collective-permute-start.6 = (bf16[128,4096]{1,0:T(8,128)(2,1)}, bf16[128,4096]{1,0:T(8,128)(2,1)}, u32[]{:S(2)}, u32[]{:S(2)}) collective-permute-start(bf16[128,4096]{1,0:T(8,128)(2,1)} %collective-permute-done.4.t4), channel_id=1, source_target_pairs={{0,8},{8,0},{16,24},{24,16},{32,40},{40,32},{48,56},{56,48},{64,72... | collective-permute-start | bytes 3145736 | tf_op jit(solution)/shard_map/ppermute | solution.py:452
  68.5 84.8 %collective-permute-start.7 = (bf16[128,4096]{1,0:T(8,128)(2,1)}, bf16[128,4096]{1,0:T(8,128)(2,1)}, u32[]{:S(2)}, u32[]{:S(2)}) collective-permute-start(bf16[128,4096]{1,0:T(8,128)(2,1)} %collective-permute-done.5.t5), channel_id=1, source_target_pairs={{0,8},{8,0},{16,24},{24,16},{32,40},{40,32},{48,56},{56,48},{64,72... | collective-permute-start | bytes 3145736 | tf_op jit(solution)/shard_map/ppermute | solution.py:452
  82.6 70.7 %copy-start.3 = (f32[128,128]{1,0:T(8,128)S(1)}, f32[128,128]{1,0:T(8,128)}, u32[]{:S(2)}) copy-start(f32[128,128]{1,0:T(8,128)} %constant.108.clone.cos_ref) | copy-start | bytes 196612
  82.6 70.7 %copy-start.4 = (f32[128,128]{1,0:T(8,128)S(1)}, f32[128,128]{1,0:T(8,128)}, u32[]{:S(2)}) copy-start(f32[128,128]{1,0:T(8,128)} %constant.109.clone.sin_ref) | copy-start | bytes 196612
  82.6 19.8 %all-to-all-start.2 = ((f32[8,72,256]{2,1,0:T(8,128)}), f32[8,72,256]{2,1,0:T(8,128)S(1)}, u32[]{:S(2)}, u32[]{:S(2)}) async-start(f32[8,72,256]{2,1,0:T(8,128)} %finish_scores.1), calls=%async_computation.2 | async-start | bytes 1179648 | tf_op jit(solution)/shard_map/all_to_all | solution.py:460
  116.7 3.7 %collective-permute-start.8 = (f32[1,8,256]{2,1,0:T(8,128)S(1)}, f32[1,8,256]{2,1,0:T(8,128)S(1)}, u32[]{:S(2)}, u32[]{:S(2)}) collective-permute-start(f32[1,8,256]{2,1,0:T(8,128)S(1)} %get-tuple-element.38), channel_id=1, source_target_pairs={{0,32},{8,40},{16,48},{24,56},{32,64},{40,72},{48,80},{56,88},{64,... | collective-permute-start | bytes 24584 | tf_op jit(solution)/shard_map/ppermute | solution.py:528
  120.4 29.0 %collective-permute-start.9 = (f32[1,8,256]{2,1,0:T(8,128)S(1)}, f32[1,8,256]{2,1,0:T(8,128)S(1)}, u32[]{:S(2)}, u32[]{:S(2)}) collective-permute-start(f32[1,8,256]{2,1,0:T(8,128)S(1)} %get-tuple-element.39), channel_id=1, source_target_pairs={{0,224},{8,232},{16,240},{24,248},{32,0},{40,8},{48,16},{56,24},{6... | collective-permute-start | bytes 24584 | tf_op jit(solution)/shard_map/ppermute | solution.py:528
  149.4 28.1 %collective-permute-start.10 = (f32[4,8,256]{2,1,0:T(8,128)S(1)}, f32[4,8,256]{2,1,0:T(8,128)S(1)}, u32[]{:S(2)}, u32[]{:S(2)}) collective-permute-start(f32[4,8,256]{2,1,0:T(8,128)S(1)} %pad_maximum_fusion.g_own), channel_id=1, source_target_pairs={{0,8},{8,0},{16,24},{24,16},{32,40},{40,32},{48,56},{56,48},{64,72... | collective-permute-start | bytes 98312 | tf_op jit(solution)/shard_map/ppermute | solution.py:452
  176.5 1.0 copy-start.1
  188.3 2.0 collective-permute-start.11
  191.1 18.5 %all-to-all-start.5 = ((bf16[16,8,8,128]{3,2,1,0:T(8,128)(2,1)}), bf16[16,8,8,128]{3,2,1,0:T(8,128)(2,1)}, u32[]{:S(2)}, u32[]{:S(2)}) async-start(bf16[16,8,8,128]{3,2,1,0:T(8,128)(2,1)} %fusion.6), calls=%async_computation.5 | async-start | bytes 524288 | tf_op jit(solution)/shard_map/all_to_all | solution.py:456
  198.1 27.2 %collective-permute-start.1 = (f32[1024,256]{1,0:T(8,128)}, f32[1024,256]{1,0:T(8,128)S(1)}, u32[]{:S(2)}, u32[]{:S(2)}) collective-permute-start(f32[1024,256]{1,0:T(8,128)} %get-tuple-element.24), channel_id=1, source_target_pairs={{0,8},{8,0},{16,24},{24,16},{32,40},{40,32},{48,56},{56,48},{64,72... | collective-permute-start | bytes 3145736 | tf_op jit(solution)/shard_map/ppermute | solution.py:452
  211.3 9.8 %all-to-all-start.6 = ((f32[8,8,8,128]{3,2,1,0:T(8,128)}), f32[8,8,8,128]{3,2,1,0:T(8,128)S(1)}, u32[]{:S(2)}, u32[]{:S(2)}) async-start(f32[8,8,8,128]{3,2,1,0:T(8,128)} %broadcast_in_dim.16), calls=%async_computation.6 | async-start | bytes 524288 | tf_op jit(solution)/shard_map/all_to_all | solution.py:460
  221.8 13.5 %all-to-all-start.7 = ((f32[16,16,128]{2,1,0:T(8,128)}), f32[16,16,128]{2,1,0:T(8,128)S(1)}, u32[]{:S(2)}, u32[]{:S(2)}) async-start(f32[16,16,128]{2,1,0:T(8,128)} %broadcast_in_dim.18), calls=%async_computation.7 | async-start | bytes 262144 | tf_op jit(solution)/shard_map/all_to_all | solution.py:456
  235.3 18.0 %all-to-all-start.3 = ((bf16[16,64,256]{2,1,0:T(8,128)(2,1)}), bf16[16,64,256]{2,1,0:T(8,128)(2,1)S(1)}, u32[]{:S(2)}, u32[]{:S(2)}) async-start(bf16[16,64,256]{2,1,0:T(8,128)(2,1)} %bitcast.2), calls=%async_computation.3 | async-start | bytes 1048576 | tf_op jit(solution)/shard_map/all_to_all | solution.py:456
  238.9 15.1 %collective-permute-start.12 = (f32[16,16,128]{2,1,0:T(8,128)S(1)}, f32[16,16,128]{2,1,0:T(8,128)S(1)}, u32[]{:S(2)}, u32[]{:S(2)}) collective-permute-start(f32[16,16,128]{2,1,0:T(8,128)S(1)} %all-to-all-done.7.own_ref), channel_id=1, source_target_pairs={{0,8},{8,0},{16,24},{24,16},{32,40},{40,32},{48,56},{56,48},{64,72... | collective-permute-start | bytes 393224 | tf_op jit(solution)/shard_map/ppermute | solution.py:452
Sparse Core Ops, SparseCore 0:
  11.5 103.1 all-gather.2

commit v2 on v1

--- a/solution.py
+++ b/solution.py
@@ -146,7 +146,7 @@
         out_ref[c, 64:72, :] = tail
 
 
-def query_grad_kernel(s_ref, q_ref, pos_ref, own_ref, other_ref, grad_ref, w_ref, col_ref):
+def query_grad_kernel(s_ref, q_ref, pos_ref, own_ref, other_ref, grad_ref, w_ref, col_ref, rerun_ref):
     top = jnp.max(s_ref[0, 0:64, :], axis=1, keepdims=True)
     for c in range(1, N_FSDP):
         top = jnp.maximum(top, jnp.max(s_ref[c, 0:64, :], axis=1, keepdims=True))
@@ -171,7 +171,10 @@
         head, rest = split(weight)
         both = dot(jnp.concatenate([head, rest], axis=0), chunk_of(c, own_ref, other_ref))
         total = total + both[0:64] + both[64:128]
-    grad_ref[...] = total / q_norm - (cross / (q_norm * q_norm)) * q_ref[...].astype(F32)
+    query_grad = total / q_norm - (cross / (q_norm * q_norm)) * q_ref[...].astype(F32)
+    grad_ref[...] = query_grad
+    for m in range(N_FSDP):
+        rerun_ref[m] = query_grad[2 * m : 2 * m + 2]
 
 
 def passage_terms_kernel(w_ref, col_ref, q_ref, own_ref, other_ref, keep_ref, give_ref):
@@ -186,9 +189,9 @@
         out_ref[(c % 4) * 256 : (c % 4 + 1) * 256, :] = value
 
 
-def forward_kernel(
+def project_kernel(
     scalar_ref, t0, t1, t2, t3, t4, t5, t6, t7, weight_ref, cos_ref, sin_ref,
-    q_ref, k_ref, v_ref, p_ref, csum_ref, low_ref, up_ref,
+    q_ref, k_ref, v_ref, low_ref, up_ref,
     tok, wv, acc, lacc, tok_sem, w_sem,
 ):
     tokens = (t0, t1, t2, t3, t4, t5, t6, t7)
@@ -209,9 +212,6 @@
 
     cos = cos_ref[...]
     sin = sin_ref[...]
-    causal = lax.broadcasted_iota(jnp.int32, (L, L), 0) >= lax.broadcasted_iota(jnp.int32, (L, L), 1)
-    causal = jnp.concatenate([causal.astype(F32)] * GROUP, axis=0) > 0.5
-
     def rope(x):
         return (x * cos + pltpu.roll(x, HD // 2, 1) * sin).astype(BF16)
 
@@ -264,30 +264,19 @@
             q_ref[n] = q
             k_ref[n] = k
             v_ref[n] = acc[r, (GROUP + 1) * HD : (GROUP + 2) * HD].astype(BF16)
-            scores = dot(q, k, NT) / math.sqrt(HD)
-            scores = jnp.where(causal, scores, -1e30)
-            e = jnp.exp(scores - jnp.max(scores, axis=1, keepdims=True))
-            p = e / jnp.sum(e, axis=1, keepdims=True)
-            p_ref[n] = p
-            rounded = p.astype(BF16).astype(F32)
-            csum_ref[n] = jnp.zeros((8, L), F32)
-            for j in range(GROUP):
-                csum_ref[n, j : j + 1, :] = jnp.sum(rounded[L * j : L * (j + 1)], axis=0, keepdims=True)
-
-
-def forward(scalars, tokens, weight, cos, sin):
+
+
+def project(scalars, tokens, weight, cos, sin):
     n = len(tokens)
     return pl.pallas_call(
-        forward_kernel,
-        name="attention_forward",
+        project_kernel,
+        name="project",
         in_specs=[SMEM] + [ANY] * (n + 1) + [VMEM, VMEM],
-        out_specs=[VMEM] * 7,
+        out_specs=[VMEM] * 5,
         out_shape=[
             jax.ShapeDtypeStruct((n, GROUP * L, HD), BF16),
             jax.ShapeDtypeStruct((n, L, HD), BF16),
             jax.ShapeDtypeStruct((n, L, HD), BF16),
-            jax.ShapeDtypeStruct((n, GROUP * L, L), F32),
-            jax.ShapeDtypeStruct((n, 8, L), F32),
             jax.ShapeDtypeStruct((n, L, LOW), BF16),
             jax.ShapeDtypeStruct((LOW, COLS), BF16),
         ],
@@ -302,6 +291,39 @@
         compiler_params=params(),
         cost_estimate=cost(2 * n * L * MODEL_WIDTH * (COLS + LOW), 20e6),
     )(scalars, *tokens, weight, cos, sin)
+
+
+def attend_kernel(q_ref, k_ref, p_ref, csum_ref):
+    causal = lax.broadcasted_iota(jnp.int32, (L, L), 0) >= lax.broadcasted_iota(jnp.int32, (L, L), 1)
+    causal = jnp.concatenate([causal.astype(F32)] * GROUP, axis=0) > 0.5
+
+    @pl.loop(0, q_ref.shape[0])
+    def _(n):
+        scores = dot(q_ref[n], k_ref[n], NT) / math.sqrt(HD)
+        scores = jnp.where(causal, scores, -1e30)
+        e = jnp.exp(scores - jnp.max(scores, axis=1, keepdims=True))
+        p = e / jnp.sum(e, axis=1, keepdims=True)
+        p_ref[n] = p
+        rounded = p.astype(BF16).astype(F32)
+        csum_ref[n] = jnp.zeros((8, L), F32)
+        for j in range(GROUP):
+            csum_ref[n, j : j + 1, :] = jnp.sum(rounded[L * j : L * (j + 1)], axis=0, keepdims=True)
+
+
+def attend(queries, keys):
+    n = queries.shape[0]
+    return pl.pallas_call(
+        attend_kernel,
+        name="attend",
+        in_specs=[VMEM, VMEM],
+        out_specs=[VMEM, VMEM],
+        out_shape=[
+            jax.ShapeDtypeStruct((n, GROUP * L, L), F32),
+            jax.ShapeDtypeStruct((n, 8, L), F32),
+        ],
+        compiler_params=params(),
+        cost_estimate=cost(2 * n * GROUP * L * L * HD * 10, 4e6),
+    )(queries, keys)
 
 
 def backward_kernel(
@@ -368,18 +390,15 @@
         low = low_ref[n]
         dup[...] += dot(low, head_part, TN) + dot(low, rest_part, TN)
 
-    for half in range(2):
-        spot = core if half == 0 else 1 - core
-        if half == 1:
-            out_ref[pl.ds(spot, 1), RING // 2 : RING] = jnp.zeros((1, RING // 2, N_FSDP, 8, HD), F32)
     far = 1 - core
+    out_ref[pl.ds(far, 1), :, RING // 2 : RING] = jnp.zeros((1, N_FSDP, RING // 2, 8, HD), F32)
     for j in range(GROUP + 2):
         tile = GROUP * head + j if j < GROUP else (HQ + HK * (j - GROUP)) + head
         shard = tile // 3
         block = max(0, j - GROUP + 1)
         value = dup[ADAPTER_RANK * block : ADAPTER_RANK * (block + 1), HD * j : HD * (j + 1)]
         for i in range(2):
-            out_ref[far, RING // 2 + 2 * (tile % 3) + i, shard] = value[8 * i : 8 * (i + 1)]
+            out_ref[far, shard, RING // 2 + 2 * (tile % 3) + i] = value[8 * i : 8 * (i + 1)]
     for copy in copies:
         copy.wait()
     for f in range(N_FSDP):
@@ -389,7 +408,7 @@
             for i in range(LOW // 8):
                 group = b * (LOW // 8) + i
                 spot = core if group < RING else 1 - core
-                out_ref[spot, group % RING, f] = value[8 * i : 8 * (i + 1), HD * b : HD * (b + 1)]
+                out_ref[spot, f, group % RING] = value[8 * i : 8 * (i + 1), HD * b : HD * (b + 1)]
 
 
 def backward(scalars, tokens, g_own, g_other, saved, cos, sin):
@@ -399,7 +418,7 @@
         name="attention_backward",
         in_specs=[SMEM] + [ANY] * n + [VMEM] * 11,
         out_specs=VMEM,
-        out_shape=jax.ShapeDtypeStruct((2, RING, N_FSDP, 8, HD), F32),
+        out_shape=jax.ShapeDtypeStruct((2, N_FSDP, RING, 8, HD), F32),
         scratch_shapes=[
             pltpu.VMEM((n * L, MODEL_WIDTH), BF16),
             pltpu.VMEM((2 * LOW, n * L), BF16),
@@ -412,17 +431,36 @@
     )(scalars, *tokens, g_own, g_other, *saved, cos, sin)
 
 
-def finish_kernel(scalar_ref, own_ref, other_ref, down_ref, up_ref):
+def fold_kernel(parts_ref, out_ref):
+    total = parts_ref[0]
+    for n in range(1, N_FSDP):
+        total = total + parts_ref[n]
+    total = total.astype(BF16)
+    for n in range(RING):
+        out_ref[n] = total
+
+
+def total_kernel(parts_ref, out_ref, squares_ref):
+    total = parts_ref[0].astype(F32)
+    for n in range(1, RING):
+        total = total + parts_ref[n].astype(F32)
+    out_ref[...] = total
+    squares = jnp.broadcast_to(jnp.sum(total * total, axis=0, keepdims=True), (8, HD))
+    for n in range(N_FSDP):
+        squares_ref[n] = squares
+
+
+def finish_kernel(scalar_ref, own_ref, other_ref, squares_ref, squares_other_ref, down_ref, up_ref):
     core = scalar_ref[1]
-    squares = jnp.sum(own_ref[:, 8:9, :], axis=0) + jnp.sum(other_ref[:, 8:9, :], axis=0)
+    squares = jnp.sum(squares_ref[:, 0:1, :], axis=0) + jnp.sum(squares_other_ref[:, 0:1, :], axis=0)
     grad_norm = jnp.sqrt(jnp.sum(squares, axis=1, keepdims=True))
     unit_scale = math.sqrt(3 * MODEL_WIDTH * ADAPTER_RANK + (HQ + 2 * HK) * HD * ADAPTER_RANK)
     factor = jnp.minimum(1.0, MAX_NORM / (grad_norm + 1e-06)) * unit_scale
 
     def tile(group):
         half, spot = divmod(group, RING)
-        a = own_ref[spot, 0:8, :]
-        b = other_ref[spot, 0:8, :]
+        a = own_ref[8 * spot : 8 * spot + 8, :]
+        b = other_ref[8 * spot : 8 * spot + 8, :]
         return jnp.where(core == half, a, b) * factor
 
     for b in range(ROWS // HD):
@@ -452,6 +490,10 @@
     return lax.ppermute(x, "dp", SIBLING)
 
 
+def after(x, *others):
+    return lax.optimization_barrier((x,) + others)[0]
+
+
 def swap_dp(x):
     return lax.all_to_all(x, "dp", 0, 0, axis_index_groups=CORE_GROUPS)
 
@@ -466,9 +508,9 @@
     dp = lax.axis_index("dp")
     core = dp % 2
     head = 2 * ((dp // 4) % 2) + core
+    cos, sin = (jnp.asarray(t) for t in rope_tables())
+
     scalars = jnp.stack([head, core]).astype(jnp.int32)
-    cos, sin = (jnp.asarray(t) for t in rope_tables())
-
     columns = [
         lax.dynamic_slice_in_dim(frozen_weight, GROUP * HD * head, GROUP * HD, 1),
         lax.dynamic_slice_in_dim(frozen_weight, HQ * HD + HD * head, HD, 1),
@@ -482,16 +524,16 @@
         ],
         axis=0,
     )
+    first, second = normalize(layer_input, gain)
+
     weight = lax.all_gather(packed, "fsdp", axis=0)
 
-    first, second = normalize(layer_input, gain)
-    from_below = lax.ppermute(first, "dp", UPWARD)
-    from_above = lax.ppermute(second, "dp", DOWNWARD)
-    tokens = [first, second, to_sibling(first), to_sibling(second)]
-    tokens += [from_below, from_above, to_sibling(from_below), to_sibling(from_above)]
-
     own = swap_dp(jnp.broadcast_to(passage_rows[None], (RING, 64, 256))).reshape(RING * 64, 256)
+    own = after(own, first, second)
     other = to_sibling(own)
+    from_below = lax.ppermute(after(first, own), "dp", UPWARD)
+    from_above = lax.ppermute(after(second, own), "dp", DOWNWARD)
+
     partial = pl.pallas_call(
         partial_scores_kernel,
         name="partial_scores",
@@ -511,23 +553,19 @@
     place = (
         jnp.where(owner % 2 == core, 0, RING * 64) + (owner // 2) * 64 + positive % 64
     ).astype(jnp.int32)
-    query_grad, pulls, columns_sum = pl.pallas_call(
+    query_grad, pulls, columns_sum, rerun = pl.pallas_call(
         query_grad_kernel,
         name="query_grad",
         out_shape=[
             jax.ShapeDtypeStruct((64, 256), F32),
             jax.ShapeDtypeStruct((N_FSDP, 64, 256), F32),
             jax.ShapeDtypeStruct((N_FSDP, 8, 256), F32),
+            jax.ShapeDtypeStruct((N_FSDP, 2, 256), F32),
         ],
         compiler_params=params(),
         cost_estimate=cost(2 * 128 * 256 * 2048, 2e6),
     )(scores, query_rows, place.reshape(64, 1), own, other)
-    g = swap_fsdp(query_grad[:16].reshape(N_FSDP, 2, 256))
-    g = jnp.swapaxes(g, 0, 1)
-    g_own = jnp.concatenate(
-        [g, lax.ppermute(g[0:1], "dp", UPWARD), lax.ppermute(g[1:2], "dp", DOWNWARD)], axis=0
-    )
-    g_other = to_sibling(g_own)
+    g = swap_fsdp(rerun)
 
     keep, give = pl.pallas_call(
         passage_terms_kernel,
@@ -536,29 +574,58 @@
         compiler_params=params(),
         cost_estimate=cost(2 * 128 * 256 * 2048, 6e6),
     )(pulls, columns_sum, query_rows, own, other)
-    sent = (keep + to_sibling(give)).astype(BF16).reshape(RING, 64, 256)
-    passage_grad = jnp.sum(swap_dp(sent).astype(F32), axis=0)
-
-    *saved, = forward(scalars, tokens, weight, cos, sin)
-    grads = backward(scalars, tokens, g_own, g_other, saved, cos, sin)
-    summed = (grads[0] + to_sibling(grads[1])).astype(BF16)
-    piece = jnp.sum(swap_dp(summed).astype(F32), axis=0)
-    pieces = jnp.sum(swap_fsdp(jnp.broadcast_to(piece[None], (N_FSDP,) + piece.shape)), axis=0)
-    squares = jnp.sum(pieces * pieces, axis=(0, 1))
-    mine = lax.dynamic_index_in_dim(pieces, lax.axis_index("fsdp"), 0, keepdims=False)
-    tail = jnp.concatenate([mine, jnp.broadcast_to(squares[None], (8, HD))], axis=0)
-    tail_own = swap_dp(jnp.broadcast_to(tail[None], (RING, 16, HD)))
-    tail_other = to_sibling(tail_own)
+    received = to_sibling(give)
+
+    tokens = [first, second, to_sibling(first), to_sibling(second)]
+    tokens += [from_below, from_above, to_sibling(from_below), to_sibling(from_above)]
+    weight = after(weight, keep)
+    *saved, = project(scalars, tokens, weight, cos, sin)
+    g = after(g, saved[0])
+
+    sent = (keep + received).astype(BF16).reshape(RING, 64, 256)
+    arrived = swap_dp(sent)
+    passage_grad = jnp.sum(arrived.astype(F32), axis=0)
+
+    g = jnp.swapaxes(g, 0, 1)
+    below, above = lax.ppermute(g[0:1], "dp", UPWARD), lax.ppermute(g[1:2], "dp", DOWNWARD)
+    queries, keys = after(saved[0], g, sent), saved[1]
+    weights, sums = attend(queries, keys)
+    below = after(below, weights)
+    g_own = jnp.concatenate([g, below, above], axis=0)
+    g_other = to_sibling(g_own)
+    grads = backward(
+        scalars, tokens, g_own, g_other, [queries, keys, saved[2], weights, sums, *saved[3:]], cos, sin
+    )
+    grads = after(grads, arrived)
+
+    summed = grads[0] + to_sibling(grads[1])
+    shared = pl.pallas_call(
+        fold_kernel,
+        name="fold_fsdp",
+        out_shape=jax.ShapeDtypeStruct((RING, RING * 8, HD), BF16),
+        compiler_params=params(),
+    )(swap_fsdp(summed.reshape(N_FSDP, RING * 8, HD)))
+    total, squares = pl.pallas_call(
+        total_kernel,
+        name="total_dp",
+        out_shape=[
+            jax.ShapeDtypeStruct((RING * 8, HD), F32),
+            jax.ShapeDtypeStruct((N_FSDP, 8, HD), F32),
+        ],
+        compiler_params=params(),
+    )(swap_dp(shared))
+    total_other = to_sibling(total)
+    squares = swap_fsdp(squares)
     down, up = pl.pallas_call(
         finish_kernel,
         name="finish_clip",
-        in_specs=[SMEM, VMEM, VMEM],
+        in_specs=[SMEM] + [VMEM] * 4,
         out_shape=[
             jax.ShapeDtypeStruct((LOW, ROWS), F32),
             jax.ShapeDtypeStruct((ADAPTER_RANK, UP_ROWS), F32),
         ],
         compiler_params=params(),
-    )(scalars, tail_own, tail_other)
+    )(scalars, total, total_other, squares, to_sibling(squares))
     return query_grad, passage_grad, down.T, up.T
 
 

time: 266 us -> 228 us (0.86); the launches traced: 262 us -> 227 us
  waiting for transfers between devices: 114 us -> 60.9 us
  blocking collectives: 12.2 us -> 38.9 us
  starting transfers between devices: 66.4 us -> 58.5 us
    ppermute x1, waiting for transfers between devices: 28.9 us -> 0.01 us  [shards(): lax.ppermute(g[1:2], 'dp', DOWNWARD)]
    all_to_all x4 -> x2, waiting for transfers between devices: 44.6 us -> 16 us  [swap_dp(): return lax.all_to_all(x, 'dp', 0, 0, axis_index_groups=CORE_GROUPS)]
    all_to_all x0 -> x1, blocking collectives: none -> 26.3 us  [swap_dp(): return lax.all_to_all(x, 'dp', 0, 0, axis_index_groups=CORE_GROUPS)]
    all_gather x1, waiting for transfers between devices: 0.02 us -> 12.7 us  [shards(): weight = lax.all_gather(packed, 'fsdp', axis=0)]
    all_to_all x3 -> x4, starting transfers between devices: 26.8 us -> 18.9 us  [swap_fsdp(): return lax.all_to_all(x, 'fsdp', 0, 0)]
    all_to_all x3 -> x4, waiting for transfers between devices: 33.4 us -> 28 us  [swap_fsdp(): return lax.all_to_all(x, 'fsdp', 0, 0)]
    ppermute x1, waiting for transfers between devices: 3.71 us -> 0.01 us  [shards(): lax.ppermute(g[0:1], 'dp', UPWARD)]
    all_to_all x4 -> x2, starting transfers between devices: 24.4 us -> 20.7 us  [swap_dp(): return lax.all_to_all(x, 'dp', 0, 0, axis_index_groups=CORE_GROUPS)]
  transfers between devices with their start and end apart: 21 -> 21, of which waited for: 11 -> 9; matrix products, arithmetic and copies ran while one was open for 2% -> 2% of each run, Pallas kernels for 12% -> 18%
where the time goes in v2:
time: 228 us; the launch traced here: 227 us
  waiting for transfers between devices  60.9 us (27%)
  starting transfers between devices  58.5 us (26%)
  Pallas kernels  43.5 us (19%)
  blocking collectives  38.9 us (17%)
  between operations  14.4 us (6%)
  local copies, waits for them, and re-layouts  5.46 us (2%)
  other arithmetic  5.3 us (2%)
    all_to_all x4, waiting for transfers between devices, swap_fsdp(): return lax.all_to_all(x, 'fsdp', 0, 0)  28 us
    all_to_all x1, blocking collectives, swap_dp(): return lax.all_to_all(x, 'dp', 0, 0, axis_index_groups=CORE_GROUPS)  26.3 us
    all_to_all x2, starting transfers between devices, swap_dp(): return lax.all_to_all(x, 'dp', 0, 0, axis_index_groups=CORE_GROUPS)  20.7 us
    pallas_call x1, Pallas kernels, project(): pl.pallas_call(project_kernel, name='project', in_specs=[SMEM] + [ANY] *...  19.4 us
    all_to_all x4, starting transfers between devices, swap_fsdp(): return lax.all_to_all(x, 'fsdp', 0, 0)  18.9 us
    all_to_all x2, waiting for transfers between devices, swap_dp(): return lax.all_to_all(x, 'dp', 0, 0, axis_index_groups=CORE_GROUPS)  16 us
    ppermute x10, starting transfers between devices, to_sibling(): return lax.ppermute(x, 'dp', SIBLING)  13.2 us
    all_gather x1, waiting for transfers between devices, shards(): weight = lax.all_gather(packed, 'fsdp', axis=0)  12.7 us
  transfers between devices with their start and end apart: 21, of which 9 were waited for; matrix products, arithmetic and copies ran while one was open for 2% of the time, Pallas kernels for 18%

profile of v2, /device:TPU:1, one launch (start us, length us, event | category | flops | bytes accessed | tf_op | source)
XLA Modules:
  0.0 226.9 jit_solution(8305474725623332929)
XLA Ops:
  7.3 1.1 constant_dynamic-slice_fusion.2
  8.4 1.0 constant_dynamic-slice_fusion.1
  9.4 2.0 fusion.4
  11.4 0.8 broadcast_in_dim.12
  12.2 11.7 %all-to-all-start = ((bf16[16,64,256]{2,1,0:T(8,128)(2,1)}), bf16[16,64,256]{2,1,0:T(8,128)(2,1)S(1)}, u32[]{:S(2)}, u32[]{:S(2)}) async-start(bf16[16,64,256]{2,1,0:T(8,128)(2,1)} %broadcast_in_dim.12), calls=%async_computation | async-start | bytes 1048576 | tf_op jit(solution)/shard_map/all_to_all | solution.py:498
  24.0 2.4 %normalize.1 = (bf16[128,4096]{1,0:T(8,128)(2,1)S(1)}, bf16[128,4096]{1,0:T(8,128)(2,1)}) custom-call(bf16[2,128,4096]{2,1,0:T(8,128)(2,1)S(1)} %copy-done, f32[1,4096]{1,0:T(1,128)S(1)} %bitcast.27), custom_call_target="tpu_custom_call" | custom-call | flops 6291456 | bytes 4194304 | tf_op jit(solution)/shard_map/normalize/pallas_call | solution.py:86
  26.4 1.0 copy-done.2
  27.4 16.0 %all-to-all-done = bf16[16,64,256]{2,1,0:T(8,128)(2,1)S(1)} async-done(((bf16[16,64,256]{2,1,0:T(8,128)(2,1)}), bf16[16,64,256]{2,1,0:T(8,128)(2,1)S(1)}, u32[]{:S(2)}, u32[]{:S(2)}) %all-to-all-start) | async-done | bytes 524320 | tf_op jit(solution)/shard_map/all_to_all | solution.py:498
  43.4 2.1 collective-permute-start
  45.5 1.5 collective-permute-done.other_ref
  47.0 1.9 partial_scores.1
  48.9 4.0 %all-to-all-start.1 = ((f32[8,72,256]{2,1,0:T(8,128)}), f32[8,72,256]{2,1,0:T(8,128)S(1)}, u32[]{:S(2)}, u32[]{:S(2)}) async-start(f32[8,72,256]{2,1,0:T(8,128)} %partial_scores.1), calls=%async_computation.1 | async-start | bytes 1179648 | tf_op jit(solution)/shard_map/all_to_all | solution.py:502
  52.9 0.2 collective-permute-start.4
  53.1 2.6 %collective-permute-start.5 = (bf16[128,4096]{1,0:T(8,128)(2,1)}, bf16[128,4096]{1,0:T(8,128)(2,1)}, u32[]{:S(2)}, u32[]{:S(2)}) collective-permute-start(bf16[128,4096]{1,0:T(8,128)(2,1)} %get-tuple-element.40.t1), channel_id=1, source_target_pairs={{0,224},{8,232},{16,240},{24,248},{32,0},{40,8},{48,16},{56,24},{6... | collective-permute-start | bytes 3145736 | tf_op jit(solution)/shard_map/ppermute | solution.py:535
  55.7 11.5 %all-to-all-done.1.parts_ref = f32[8,72,256]{2,1,0:T(8,128)S(1)} async-done(((f32[8,72,256]{2,1,0:T(8,128)}), f32[8,72,256]{2,1,0:T(8,128)S(1)}, u32[]{:S(2)}, u32[]{:S(2)}) %all-to-all-start.1) | async-done | bytes 589856 | tf_op jit(solution)/shard_map/all_to_all | solution.py:502
  67.2 1.0 finish_scores.1
  68.2 5.6 %all-to-all-start.2 = ((f32[8,72,256]{2,1,0:T(8,128)}), f32[8,72,256]{2,1,0:T(8,128)S(1)}, u32[]{:S(2)}, u32[]{:S(2)}) async-start(f32[8,72,256]{2,1,0:T(8,128)} %finish_scores.1), calls=%async_computation.2 | async-start | bytes 1179648 | tf_op jit(solution)/shard_map/all_to_all | solution.py:502
  73.8 0.1 copy.16.pos_ref
  73.9 14.0 %all-to-all-done.2.s_ref = f32[8,72,256]{2,1,0:T(8,128)S(1)} async-done(((f32[8,72,256]{2,1,0:T(8,128)}), f32[8,72,256]{2,1,0:T(8,128)S(1)}, u32[]{:S(2)}, u32[]{:S(2)}) %all-to-all-start.2) | async-done | bytes 589856 | tf_op jit(solution)/shard_map/all_to_all | solution.py:502
  87.8 1.3 query_grad.1
  89.1 1.5 passage_terms.1
  90.6 1.8 collective-permute-start.1
  92.5 0.5 collective-permute-start.3
  93.0 0.5 collective-permute-start.6
  93.6 6.0 %all-to-all-start.4 = ((f32[8,2,256]{2,1,0:T(2,128)}), f32[8,2,256]{2,1,0:T(2,128)S(1)}, u32[]{:S(2)}, u32[]{:S(2)}) async-start(f32[8,2,256]{2,1,0:T(2,128)} %get-tuple-element.41), calls=%async_computation.4 | async-start | bytes 32768 | tf_op jit(solution)/shard_map/all_to_all | solution.py:502
  99.6 2.5 %add_convert_fusion = bf16[1024,256]{1,0:T(8,128)(2,1)} fusion(f32[1024,256]{1,0:T(8,128)} %copy-done.7, f32[1024,256]{1,0:T(8,128)} %collective-permute-done.1), kind=kLoop, calls=%fused_computation.7 | loop fusion | flops 524288 | bytes 2621440 | tf_op jit(solution)/shard_map/convert_element_type | solution.py:585
  102.1 12.7 %all-gather.3.cloned.1.call-done = bf16[4608,768]{1,0:T(8,128)(2,1)} async-done(((bf16[576,768]{1,0:T(8,128)(2,1)}), bf16[4608,768]{1,0:T(8,128)(2,1)}) %all-gather.3.cloned.1.call-update) | async-done | bytes 7077904 | tf_op jit(solution)/shard_map/all_gather | solution.py:529
  114.8 8.9 %all-to-all-start.3 = ((bf16[16,64,256]{2,1,0:T(8,128)(2,1)}), bf16[16,64,256]{2,1,0:T(8,128)(2,1)S(1)}, u32[]{:S(2)}, u32[]{:S(2)}) async-start(bf16[16,64,256]{2,1,0:T(8,128)(2,1)} %bitcast.3), calls=%async_computation.3 | async-start | bytes 1048576 | tf_op jit(solution)/shard_map/all_to_all | solution.py:498
  123.8 19.4 %project.1 = (bf16[8,512,128]{2,1,0:T(8,128)(2,1)S(1)}, bf16[8,128,128]{2,1,0:T(8,128)(2,1)S(1)}, bf16[8,128,128]{2,1,0:T(8,128)(2,1)S(1)}, bf16[8,128,48]{2,1,0:T(8,128)(2,1)S(1)}, bf16[48,768]{1,0:T(8,128)(2,1)S(1)}) custom-call(s32[2]{0:T(128)S(1)} %pad_add_fusion.scalar_ref, bf16[128,4096]{1,0:T(8,128)(2,1)S(1)} %copy-done.3, ...), custom_call_target="tpu_custom_call" | custom-call | flops 6845104128 | bytes 20000000 | tf_op jit(solution)/shard_map/project/pallas_call | solution.py:271
  143.3 1.6 collective-permute-start.8
  144.9 1.3 collective-permute-start.9
  146.2 3.2 %attend.1 = (f32[8,512,128]{2,1,0:T(8,128)S(1)}, f32[8,8,128]{2,1,0:T(8,128)S(1)}) custom-call(bf16[8,512,128]{2,1,0:T(8,128)(2,1)S(1)} %get-tuple-element.45.q_ref, bf16[8,128,128]{2,1,0:T(8,128)(2,1)S(1)} %get-tuple-element.46.k_ref), custom_call_target="tpu_custom_call" | custom-call | flops 1342177280 | bytes 4000000 | tf_op jit(solution)/shard_map/attend/pallas_call | solution.py:315
  149.5 1.3 copy-done.1
  150.8 1.7 collective-permute-start.10
  152.4 0.9 collective-permute-done.10.g_other
  153.3 10.8 %attention_backward.1 = f32[2,8,16,8,128]{4,3,2,1,0:T(8,128)S(1)} custom-call(s32[2]{0:T(128)S(1)} %pad_add_fusion.scalar_ref, bf16[128,4096]{1,0:T(8,128)(2,1)S(1)} %copy-done.3, bf16[128,4096]{1,0:T(8,128)(2,1)} %get-tuple-element.40.t1, bf16[128,4096]{1,0:T(8,128)(2,1)S(1)} %copy-done.5, bf16[128,4096]{1,0:T(8,128)(2,1)} %collective-permute-done.3.t3, ...), custom_call_target="tpu_custom_call" | custom-call | flops 805306368 | bytes 15000000 | tf_op jit(solution)/shard_map/attention_backward/pallas_call | solution.py:416
  164.2 0.4 collective-permute-start.11
  164.6 1.6 collective-permute-done.11
  166.2 12.6 %all_to_all.40.parts_ref = f32[8,128,128]{2,1,0:T(8,128)S(1)} all-to-all(f32[8,128,128]{2,1,0:T(8,128)S(1)} %fusion.5), channel_id=1, replica_groups=mesh['dp'=32,'fsdp'=8] {'fsdp'}, dimensions={0} | all-to-all | bytes 1048576 | tf_op jit(solution)/shard_map/all_to_all | solution.py:502
  178.9 26.3 %all_to_all.41.parts_ref = bf16[16,128,128]{2,1,0:T(8,128)(2,1)S(1)} all-to-all(bf16[16,128,128]{2,1,0:T(8,128)(2,1)S(1)} %fold_fsdp.1), channel_id=1, replica_groups={{0,16,32,48,64,80,96,112,128,144,160,176,192,208,224,240},{8,24,40,56,7..., dimensions={0} | all-to-all | bytes 1048576 | tf_op jit(solution)/shard_map/all_to_all | solution.py:498
  205.2 0.7 total_dp.1
  205.9 3.3 %all-to-all-start.7 = ((f32[8,8,128]{2,1,0:T(8,128)}), f32[8,8,128]{2,1,0:T(8,128)S(1)}, u32[]{:S(2)}, u32[]{:S(2)}) async-start(f32[8,8,128]{2,1,0:T(8,128)} %get-tuple-element.55), calls=%async_computation.7 | async-start | bytes 65536 | tf_op jit(solution)/shard_map/all_to_all | solution.py:502
  209.3 2.6 %collective-permute-start.12 = (f32[128,128]{1,0:T(8,128)S(1)}, f32[128,128]{1,0:T(8,128)S(1)}, u32[]{:S(2)}, u32[]{:S(2)}) collective-permute-start(f32[128,128]{1,0:T(8,128)S(1)} %get-tuple-element.54.own_ref), channel_id=1, source_target_pairs={{0,8},{8,0},{16,24},{24,16},{32,40},{40,32},{48,56},{56,48},{64,72... | collective-permute-start | bytes 196616 | tf_op jit(solution)/shard_map/ppermute | solution.py:490
  211.8 2.5 %all-to-all-done.7.squares_ref = f32[8,8,128]{2,1,0:T(8,128)S(1)} async-done(((f32[8,8,128]{2,1,0:T(8,128)}), f32[8,8,128]{2,1,0:T(8,128)S(1)}, u32[]{:S(2)}, u32[]{:S(2)}) %all-to-all-start.7) | async-done | bytes 32800 | tf_op jit(solution)/shard_map/all_to_all | solution.py:502
  214.3 3.6 %collective-permute-start.13 = (f32[8,8,128]{2,1,0:T(8,128)S(1)}, f32[8,8,128]{2,1,0:T(8,128)S(1)}, u32[]{:S(2)}, u32[]{:S(2)}) collective-permute-start(f32[8,8,128]{2,1,0:T(8,128)S(1)} %all-to-all-done.7.squares_ref), channel_id=1, source_target_pairs={{0,8},{8,0},{16,24},{24,16},{32,40},{40,32},{48,56},{56,48},{64,72... | collective-permute-start | bytes 98312 | tf_op jit(solution)/shard_map/ppermute | solution.py:490
  217.9 0.7 convert_reduce_fusion
  218.6 0.2 collective-permute-done.13.squares_other_ref
  218.8 1.3 finish_clip.1
  (50 shorter events, 0.5 us)
Async XLA Ops:
  7.2 107.6 %all-gather.3.cloned.1.call-start = ((), (), s32[]{:S(2)}) async-start(), calls=%async_computation.8 | async-start | bytes 7962624 | tf_op jit(solution)/shard_map/all_gather | solution.py:529
  8.3 3.0 %copy-start.12 = (bf16[64,256]{1,0:T(8,128)(2,1)S(1)}, bf16[64,256]{1,0:T(8,128)(2,1)}, u32[]{:S(2)}) copy-start(bf16[64,256]{1,0:T(8,128)(2,1)} %param.11) | copy-start | bytes 98308
  9.4 14.6 %copy-start = (bf16[2,128,4096]{2,1,0:T(8,128)(2,1)S(1)}, bf16[2,128,4096]{2,1,0:T(8,128)(2,1)}, u32[]{:S(2)}) copy-start(bf16[2,128,4096]{2,1,0:T(8,128)(2,1)} %x_ref.1) | copy-start | bytes 6291460
  9.4 14.6 %copy-start.11 = (f32[4096]{0:T(1024)S(1)}, f32[4096]{0:T(1024)}, u32[]{:S(2)}) copy-start(f32[4096]{0:T(1024)} %param.14) | copy-start | bytes 49156
  11.4 35.7 %copy-start.8 = (bf16[64,256]{1,0:T(8,128)(2,1)S(1)}, bf16[64,256]{1,0:T(8,128)(2,1)}, u32[]{:S(2)}) copy-start(bf16[64,256]{1,0:T(8,128)(2,1)} %q_ref.5) | copy-start | bytes 98308
  12.2 31.2 %all-to-all-start = ((bf16[16,64,256]{2,1,0:T(8,128)(2,1)}), bf16[16,64,256]{2,1,0:T(8,128)(2,1)S(1)}, u32[]{:S(2)}, u32[]{:S(2)}) async-start(bf16[16,64,256]{2,1,0:T(8,128)(2,1)} %broadcast_in_dim.12), calls=%async_computation | async-start | bytes 1048576 | tf_op jit(solution)/shard_map/all_to_all | solution.py:498
  26.3 1.0 copy-start.2
  43.4 9.5 %copy-start.3 = (bf16[128,4096]{1,0:T(8,128)(2,1)S(1)}, bf16[128,4096]{1,0:T(8,128)(2,1)}, u32[]{:S(2)}) copy-start(bf16[128,4096]{1,0:T(8,128)(2,1)} %copy-done.2) | copy-start | bytes 3145732
  43.4 3.6 %collective-permute-start = (bf16[1024,256]{1,0:T(8,128)(2,1)S(1)}, bf16[1024,256]{1,0:T(8,128)(2,1)S(1)}, u32[]{:S(2)}, u32[]{:S(2)}) collective-permute-start(bf16[1024,256]{1,0:T(8,128)(2,1)S(1)} %bitcast.23), channel_id=1, source_target_pairs={{0,8},{8,0},{16,24},{24,16},{32,40},{40,32},{48,56},{56,48},{64,72... | collective-permute-start | bytes 1572872 | tf_op jit(solution)/shard_map/ppermute | solution.py:490
  48.9 24.8 %copy-start.13 = (s32[64]{0:T(128)S(1)}, s32[64]{0:T(128)}, u32[]{:S(2)}) copy-start(s32[64]{0:T(128)} %param.12) | copy-start | bytes 772
  48.9 18.3 %all-to-all-start.1 = ((f32[8,72,256]{2,1,0:T(8,128)}), f32[8,72,256]{2,1,0:T(8,128)S(1)}, u32[]{:S(2)}, u32[]{:S(2)}) async-start(f32[8,72,256]{2,1,0:T(8,128)} %partial_scores.1), calls=%async_computation.1 | async-start | bytes 1179648 | tf_op jit(solution)/shard_map/all_to_all | solution.py:502
  52.9 40.1 %collective-permute-start.4 = (bf16[128,4096]{1,0:T(8,128)(2,1)S(1)}, bf16[128,4096]{1,0:T(8,128)(2,1)}, u32[]{:S(2)}, u32[]{:S(2)}) collective-permute-start(bf16[128,4096]{1,0:T(8,128)(2,1)S(1)} %copy-done.3), channel_id=1, source_target_pairs={{0,32},{8,40},{16,48},{24,56},{32,64},{40,72},{48,80},{56,88},{64,... | collective-permute-start | bytes 3145736 | tf_op jit(solution)/shard_map/ppermute | solution.py:534
  53.1 40.3 %collective-permute-start.5 = (bf16[128,4096]{1,0:T(8,128)(2,1)}, bf16[128,4096]{1,0:T(8,128)(2,1)}, u32[]{:S(2)}, u32[]{:S(2)}) collective-permute-start(bf16[128,4096]{1,0:T(8,128)(2,1)} %get-tuple-element.40.t1), channel_id=1, source_target_pairs={{0,224},{8,232},{16,240},{24,248},{32,0},{40,8},{48,16},{56,24},{6... | collective-permute-start | bytes 3145736 | tf_op jit(solution)/shard_map/ppermute | solution.py:535
  68.2 19.6 %all-to-all-start.2 = ((f32[8,72,256]{2,1,0:T(8,128)}), f32[8,72,256]{2,1,0:T(8,128)S(1)}, u32[]{:S(2)}, u32[]{:S(2)}) async-start(f32[8,72,256]{2,1,0:T(8,128)} %finish_scores.1), calls=%async_computation.2 | async-start | bytes 1179648 | tf_op jit(solution)/shard_map/all_to_all | solution.py:502
  90.6 2.4 %copy-start.7 = (f32[1024,256]{1,0:T(8,128)}, f32[1024,256]{1,0:T(8,128)S(1)}, u32[]{:S(2)}) copy-start(f32[1024,256]{1,0:T(8,128)S(1)} %get-tuple-element.37) | copy-start | bytes 3145732
  90.6 8.9 %collective-permute-start.1 = (f32[1024,256]{1,0:T(8,128)}, f32[1024,256]{1,0:T(8,128)}, u32[]{:S(2)}, u32[]{:S(2)}) collective-permute-start(f32[1024,256]{1,0:T(8,128)} %get-tuple-element.38), channel_id=1, source_target_pairs={{0,8},{8,0},{16,24},{24,16},{32,40},{40,32},{48,56},{56,48},{64,72... | collective-permute-start | bytes 3145736 | tf_op jit(solution)/shard_map/ppermute | solution.py:490
  92.5 31.3 %collective-permute-start.2 = (bf16[128,4096]{1,0:T(8,128)(2,1)S(1)}, bf16[128,4096]{1,0:T(8,128)(2,1)S(1)}, u32[]{:S(2)}, u32[]{:S(2)}) collective-permute-start(bf16[128,4096]{1,0:T(8,128)(2,1)S(1)} %copy-done.3), channel_id=1, source_target_pairs={{0,8},{8,0},{16,24},{24,16},{32,40},{40,32},{48,56},{56,48},{64,72... | collective-permute-start | bytes 3145736 | tf_op jit(solution)/shard_map/ppermute | solution.py:490
  92.5 31.3 %collective-permute-start.3 = (bf16[128,4096]{1,0:T(8,128)(2,1)}, bf16[128,4096]{1,0:T(8,128)(2,1)}, u32[]{:S(2)}, u32[]{:S(2)}) collective-permute-start(bf16[128,4096]{1,0:T(8,128)(2,1)} %get-tuple-element.40.t1), channel_id=1, source_target_pairs={{0,8},{8,0},{16,24},{24,16},{32,40},{40,32},{48,56},{56,48},{64,72... | collective-permute-start | bytes 3145736 | tf_op jit(solution)/shard_map/ppermute | solution.py:490
  93.0 30.8 %collective-permute-start.6 = (bf16[128,4096]{1,0:T(8,128)(2,1)}, bf16[128,4096]{1,0:T(8,128)(2,1)}, u32[]{:S(2)}, u32[]{:S(2)}) collective-permute-start(bf16[128,4096]{1,0:T(8,128)(2,1)} %collective-permute-done.4.t4), channel_id=1, source_target_pairs={{0,8},{8,0},{16,24},{24,16},{32,40},{40,32},{48,56},{56,48},{64,72... | collective-permute-start | bytes 3145736 | tf_op jit(solution)/shard_map/ppermute | solution.py:490
  93.5 30.3 %collective-permute-start.7 = (bf16[128,4096]{1,0:T(8,128)(2,1)}, bf16[128,4096]{1,0:T(8,128)(2,1)}, u32[]{:S(2)}, u32[]{:S(2)}) collective-permute-start(bf16[128,4096]{1,0:T(8,128)(2,1)} %collective-permute-done.5.t5), channel_id=1, source_target_pairs={{0,8},{8,0},{16,24},{24,16},{32,40},{40,32},{48,56},{56,48},{64,72... | collective-permute-start | bytes 3145736 | tf_op jit(solution)/shard_map/ppermute | solution.py:490
  93.6 21.2 %all-to-all-start.4 = ((f32[8,2,256]{2,1,0:T(2,128)}), f32[8,2,256]{2,1,0:T(2,128)S(1)}, u32[]{:S(2)}, u32[]{:S(2)}) async-start(f32[8,2,256]{2,1,0:T(2,128)} %get-tuple-element.41), calls=%async_computation.4 | async-start | bytes 32768 | tf_op jit(solution)/shard_map/all_to_all | solution.py:502
  99.6 24.3 %copy-start.9 = (f32[128,128]{1,0:T(8,128)S(1)}, f32[128,128]{1,0:T(8,128)}, u32[]{:S(2)}) copy-start(f32[128,128]{1,0:T(8,128)} %constant.101.clone.sin_ref) | copy-start | bytes 196612
  99.6 24.2 %copy-start.10 = (f32[128,128]{1,0:T(8,128)S(1)}, f32[128,128]{1,0:T(8,128)}, u32[]{:S(2)}) copy-start(f32[128,128]{1,0:T(8,128)} %constant.100.clone.cos_ref) | copy-start | bytes 196612
  114.8 49.3 %all-to-all-start.3 = ((bf16[16,64,256]{2,1,0:T(8,128)(2,1)}), bf16[16,64,256]{2,1,0:T(8,128)(2,1)S(1)}, u32[]{:S(2)}, u32[]{:S(2)}) async-start(bf16[16,64,256]{2,1,0:T(8,128)(2,1)} %bitcast.3), calls=%async_computation.3 | async-start | bytes 1048576 | tf_op jit(solution)/shard_map/all_to_all | solution.py:498
  123.8 19.5 %copy-start.4 = (bf16[128,4096]{1,0:T(8,128)(2,1)}, bf16[128,4096]{1,0:T(8,128)(2,1)S(1)}, u32[]{:S(2)}) copy-start(bf16[128,4096]{1,0:T(8,128)(2,1)S(1)} %collective-permute-done.2.t2) | copy-start | bytes 3145732
  143.2 6.2 %copy-start.6 = (bf16[8,512,128]{2,1,0:T(8,128)(2,1)}, bf16[8,512,128]{2,1,0:T(8,128)(2,1)S(1)}, u32[]{:S(2)}) copy-start(bf16[8,512,128]{2,1,0:T(8,128)(2,1)S(1)} %get-tuple-element.45.q_ref) | copy-start | bytes 3145732
  143.3 7.5 %collective-permute-start.8 = (f32[1,8,256]{2,1,0:T(8,128)S(1)}, f32[1,8,256]{2,1,0:T(8,128)S(1)}, u32[]{:S(2)}, u32[]{:S(2)}) collective-permute-start(f32[1,8,256]{2,1,0:T(8,128)S(1)} %get-tuple-element.60), channel_id=1, source_target_pairs={{0,32},{8,40},{16,48},{24,56},{32,64},{40,72},{48,80},{56,88},{64,... | collective-permute-start | bytes 24584 | tf_op jit(solution)/shard_map/ppermute | solution.py:590
  144.9 5.9 %collective-permute-start.9 = (f32[1,8,256]{2,1,0:T(8,128)S(1)}, f32[1,8,256]{2,1,0:T(8,128)S(1)}, u32[]{:S(2)}, u32[]{:S(2)}) collective-permute-start(f32[1,8,256]{2,1,0:T(8,128)S(1)} %get-tuple-element.61), channel_id=1, source_target_pairs={{0,224},{8,232},{16,240},{24,248},{32,0},{40,8},{48,16},{56,24},{6... | collective-permute-start | bytes 24584 | tf_op jit(solution)/shard_map/ppermute | solution.py:590
  146.2 7.1 %copy-start.5 = (bf16[128,4096]{1,0:T(8,128)(2,1)S(1)}, bf16[128,4096]{1,0:T(8,128)(2,1)}, u32[]{:S(2)}) copy-start(bf16[128,4096]{1,0:T(8,128)(2,1)} %copy-done.4) | copy-start | bytes 3145732
  149.5 1.3 copy-start.1
  150.8 2.5 %collective-permute-start.10 = (f32[4,8,256]{2,1,0:T(8,128)S(1)}, f32[4,8,256]{2,1,0:T(8,128)S(1)}, u32[]{:S(2)}, u32[]{:S(2)}) collective-permute-start(f32[4,8,256]{2,1,0:T(8,128)S(1)} %pad_maximum_fusion.g_own), channel_id=1, source_target_pairs={{0,8},{8,0},{16,24},{24,16},{32,40},{40,32},{48,56},{56,48},{64,72... | collective-permute-start | bytes 98312 | tf_op jit(solution)/shard_map/ppermute | solution.py:490
  164.2 2.0 collective-permute-start.11
  205.9 8.4 %all-to-all-start.7 = ((f32[8,8,128]{2,1,0:T(8,128)}), f32[8,8,128]{2,1,0:T(8,128)S(1)}, u32[]{:S(2)}, u32[]{:S(2)}) async-start(f32[8,8,128]{2,1,0:T(8,128)} %get-tuple-element.55), calls=%async_computation.7 | async-start | bytes 65536 | tf_op jit(solution)/shard_map/all_to_all | solution.py:502
  209.3 9.5 %collective-permute-start.12 = (f32[128,128]{1,0:T(8,128)S(1)}, f32[128,128]{1,0:T(8,128)S(1)}, u32[]{:S(2)}, u32[]{:S(2)}) collective-permute-start(f32[128,128]{1,0:T(8,128)S(1)} %get-tuple-element.54.own_ref), channel_id=1, source_target_pairs={{0,8},{8,0},{16,24},{24,16},{32,40},{40,32},{48,56},{56,48},{64,72... | collective-permute-start | bytes 196616 | tf_op jit(solution)/shard_map/ppermute | solution.py:490
  214.3 4.5 %collective-permute-start.13 = (f32[8,8,128]{2,1,0:T(8,128)S(1)}, f32[8,8,128]{2,1,0:T(8,128)S(1)}, u32[]{:S(2)}, u32[]{:S(2)}) collective-permute-start(f32[8,8,128]{2,1,0:T(8,128)S(1)} %all-to-all-done.7.squares_ref), channel_id=1, source_target_pairs={{0,8},{8,0},{16,24},{24,16},{32,40},{40,32},{48,56},{56,48},{64,72... | collective-permute-start | bytes 98312 | tf_op jit(solution)/shard_map/ppermute | solution.py:490
Sparse Core Ops, SparseCore 0:
  11.5 103.2 all-gather.2

commit v3 on v2

--- a/solution.py
+++ b/solution.py
@@ -29,11 +29,12 @@
 ROWS = MODEL_WIDTH // N_FSDP
 UP_ROWS = (HQ + 2 * HK) * HD // N_FSDP
 COLS = (GROUP + 2) * HD
-PACK = 3 * ADAPTER_RANK + ADAPTER_RANK
+MAP = 2 * ADAPTER_RANK
 LOW = 3 * ADAPTER_RANK
 F32 = jnp.float32
 BF16 = jnp.bfloat16
-VMEM_LIMIT = 48 * 1024 * 1024
+VMEM_LIMIT = 16 * 1024 * 1024
+LARGE_VMEM = 40 * 1024 * 1024
 
 NN = (((1,), (0,)), ((), ()))
 NT = (((1,), (1,)), ((), ()))
@@ -49,12 +50,12 @@
     return head, (x - head.astype(F32)).astype(BF16)
 
 
-def params():
-    return pltpu.CompilerParams(vmem_limit_bytes=VMEM_LIMIT)
+def params(limit=VMEM_LIMIT):
+    return pltpu.CompilerParams(vmem_limit_bytes=limit)
 
 
 def cost(flops, bytes_accessed):
-    return pl.CostEstimate(flops=int(flops), bytes_accessed=int(bytes_accessed), transcendentals=0)
+    return pl.CostEstimate(flops=1, bytes_accessed=1, transcendentals=0)
 
 
 VMEM = pl.BlockSpec(memory_space=pltpu.VMEM)
@@ -177,7 +178,7 @@
         rerun_ref[m] = query_grad[2 * m : 2 * m + 2]
 
 
-def passage_terms_kernel(w_ref, col_ref, q_ref, own_ref, other_ref, keep_ref, give_ref):
+def passage_terms_kernel(scalar_ref, w_ref, col_ref, q_ref, own_ref, other_ref, keep_ref, give_ref):
     q = q_ref[...]
     twice = jnp.concatenate([q, q], axis=0)
     for c in range(N_FSDP):
@@ -186,92 +187,79 @@
         scale = column_of(col_ref[c, 0:1, :], 256)
         value = pulled - scale * chunk_of(c, own_ref, other_ref).astype(F32)
         out_ref = keep_ref if c < 4 else give_ref
-        out_ref[(c % 4) * 256 : (c % 4 + 1) * 256, :] = value
+        for b in range(4):
+            place = (c % 4) * 256 + (b // 2) * 128 + (scalar_ref[2] + b % 2) % 2 * 64
+            out_ref[pl.ds(pl.multiple_of(place, 64), 64), :] = value[64 * b : 64 * (b + 1)]
 
 
 def project_kernel(
-    scalar_ref, t0, t1, t2, t3, t4, t5, t6, t7, weight_ref, cos_ref, sin_ref,
+    scalar_ref, t0, t1, t2, t3, t4, t5, t6, t7, weight_ref, maps_ref, cos_ref, sin_ref,
     q_ref, k_ref, v_ref, low_ref, up_ref,
-    tok, wv, acc, lacc, tok_sem, w_sem,
+    tok, wv, maps, acc, lacc, tok_sem, w_sem,
 ):
     tokens = (t0, t1, t2, t3, t4, t5, t6, t7)
     head = scalar_ref[0]
     tok_copies = [
         pltpu.make_async_copy(t, tok.at[pl.ds(L * n, L)], tok_sem.at[n]) for n, t in enumerate(tokens)
     ]
+    core = scalar_ref[1]
     w_copies = [
-        pltpu.make_async_copy(weight_ref.at[n], wv.at[n], w_sem.at[n]) for n in range(N_FSDP)
+        pltpu.make_async_copy(weight_ref.at[n, pl.ds(0, ROWS)], wv.at[n], w_sem.at[n])
+        for n in range(N_FSDP)
     ]
-    w_copies[0].start()
-    tok_copies[0].start()
-    tok_copies[1].start()
-    for n in range(1, N_FSDP):
-        w_copies[n].start()
-    for n in range(2, N_FSDP):
-        tok_copies[n].start()
+    map_copies = [
+        pltpu.make_async_copy(weight_ref.at[:, pl.ds(ROWS, MAP)], maps.at[core], w_sem.at[N_FSDP]),
+        pltpu.make_async_copy(maps_ref, maps.at[1 - core], w_sem.at[N_FSDP + 1]),
+    ]
+    for copy in tok_copies[:2] + w_copies[:2] + map_copies + w_copies[2:] + tok_copies[2:]:
+        copy.start()
 
     cos = cos_ref[...]
     sin = sin_ref[...]
     def rope(x):
         return (x * cos + pltpu.roll(x, HD // 2, 1) * sin).astype(BF16)
 
-    @pl.loop(0, 4)
-    def _(i):
-        for n in range(4):
-
-            @pl.when(i == n)
-            def _():
-                tok_copies[2 * n].wait()
-                tok_copies[2 * n + 1].wait()
-
-        rows = pl.ds(pl.multiple_of(i * 2 * L, 2 * L), 2 * L)
+    for copy in map_copies:
+        copy.wait()
+    up_ref[...] = jnp.zeros_like(up_ref)
+    for j in range(GROUP + 2):
+        tile = GROUP * head + j if j < GROUP else (HQ + HK * (j - GROUP)) + head
+        lanes = pl.ds(pl.multiple_of((tile % 3) * HD, HD), HD)
+        block = max(0, j - GROUP + 1)
+        up_ref[ADAPTER_RANK * block : ADAPTER_RANK * (block + 1), HD * j : HD * (j + 1)] = (
+            maps[1, tile // 3, ADAPTER_RANK : 2 * ADAPTER_RANK, lanes]
+        )
+    for i in range(4):
+        tok_copies[2 * i].wait()
+        tok_copies[2 * i + 1].wait()
+        rows = slice(2 * L * i, 2 * L * (i + 1))
         for n in range(N_FSDP):
-
-            @pl.when(i == 0)
-            def _():
+            if i == 0:
                 w_copies[n].wait()
-
             x = tok[rows, ROWS * n : ROWS * (n + 1)]
-            part = dot(x, wv[n, 0:ROWS, :])
-            low_part = dot(x, wv[n, ROWS : ROWS + LOW, 0:ROWS], NT)
-            if n == 0:
-                acc[...] = part
-                lacc[...] = low_part
-            else:
-                acc[...] += part
-                lacc[...] += low_part
-
-        @pl.when(i == 0)
-        def _():
-            up_ref[...] = jnp.zeros_like(up_ref)
-            for j in range(GROUP + 2):
-                tile = GROUP * head + j if j < GROUP else (HQ + HK * (j - GROUP)) + head
-                shard = tile // 3
-                lanes = pl.ds(pl.multiple_of((tile % 3) * HD, HD), HD)
-                block = max(0, j - GROUP + 1)
-                up_ref[ADAPTER_RANK * block : ADAPTER_RANK * (block + 1), HD * j : HD * (j + 1)] = (
-                    wv[shard, ROWS + LOW : ROWS + LOW + ADAPTER_RANK, lanes]
-                )
-
-        low = lacc[...].astype(BF16)
-        acc[...] += ADAPTER_SCALE * dot(low, up_ref[...])
+            part = dot(x, wv[n])
+            down = jnp.concatenate([maps[0, n, :, 0:ROWS], maps[1, n, 0:ADAPTER_RANK, 0:ROWS]], axis=0)
+            low_part = dot(x, down, NT)
+            total = part if n == 0 else total + part
+            low_sum = low_part if n == 0 else low_sum + low_part
+
+        low = low_sum.astype(BF16)
+        acc[...] = total + ADAPTER_SCALE * dot(low, up_ref[...])
         for s in range(2):
             n = 2 * i + s
             r = slice(L * s, L * (s + 1))
             low_ref[n] = low[r]
-            q = jnp.concatenate([rope(acc[r, HD * j : HD * (j + 1)]) for j in range(GROUP)], axis=0)
-            k = rope(acc[r, GROUP * HD : (GROUP + 1) * HD])
-            q_ref[n] = q
-            k_ref[n] = k
+            q_ref[n] = jnp.concatenate([rope(acc[r, HD * j : HD * (j + 1)]) for j in range(GROUP)], axis=0)
+            k_ref[n] = rope(acc[r, GROUP * HD : (GROUP + 1) * HD])
             v_ref[n] = acc[r, (GROUP + 1) * HD : (GROUP + 2) * HD].astype(BF16)
 
 
-def project(scalars, tokens, weight, cos, sin):
+def project(scalars, tokens, weight, maps, cos, sin):
     n = len(tokens)
     return pl.pallas_call(
         project_kernel,
         name="project",
-        in_specs=[SMEM] + [ANY] * (n + 1) + [VMEM, VMEM],
+        in_specs=[SMEM] + [ANY] * (n + 2) + [VMEM, VMEM],
         out_specs=[VMEM] * 5,
         out_shape=[
             jax.ShapeDtypeStruct((n, GROUP * L, HD), BF16),
@@ -282,22 +270,23 @@
         ],
         scratch_shapes=[
             pltpu.VMEM((n * L, MODEL_WIDTH), BF16),
-            pltpu.VMEM((N_FSDP, ROWS + PACK, COLS), BF16),
+            pltpu.VMEM((N_FSDP, ROWS, COLS), BF16),
+            pltpu.VMEM((2, N_FSDP, MAP, COLS), BF16),
             pltpu.VMEM((2 * L, COLS), F32),
             pltpu.VMEM((2 * L, LOW), F32),
             pltpu.SemaphoreType.DMA((n,)),
-            pltpu.SemaphoreType.DMA((N_FSDP,)),
-        ],
-        compiler_params=params(),
+            pltpu.SemaphoreType.DMA((N_FSDP + 2,)),
+        ],
+        compiler_params=params(LARGE_VMEM),
         cost_estimate=cost(2 * n * L * MODEL_WIDTH * (COLS + LOW), 20e6),
-    )(scalars, *tokens, weight, cos, sin)
+    )(scalars, *tokens, weight, maps, cos, sin)
 
 
 def attend_kernel(q_ref, k_ref, p_ref, csum_ref):
     causal = lax.broadcasted_iota(jnp.int32, (L, L), 0) >= lax.broadcasted_iota(jnp.int32, (L, L), 1)
     causal = jnp.concatenate([causal.astype(F32)] * GROUP, axis=0) > 0.5
 
-    @pl.loop(0, q_ref.shape[0])
+    @pl.loop(0, q_ref.shape[0], unroll=4)
     def _(n):
         scores = dot(q_ref[n], k_ref[n], NT) / math.sqrt(HD)
         scores = jnp.where(causal, scores, -1e30)
@@ -328,7 +317,7 @@
 
 def backward_kernel(
     scalar_ref, t0, t1, t2, t3, t4, t5, t6, t7, g_own, g_other, q_ref, k_ref, v_ref, p_ref,
-    csum_ref, low_ref, up_ref, cos_ref, sin_ref, out_ref, tok, dlow, dup, g_all, tok_sem,
+    csum_ref, low_ref, up_ref, cos_ref, sin_ref, keep_ref, give_ref, tok, dlow, dup, g_all, sums, tok_sem,
 ):
     tokens = (t0, t1, t2, t3, t4, t5, t6, t7)
     head = scalar_ref[0]
@@ -355,7 +344,7 @@
     def unrope(x):
         return x * cos + pltpu.roll(x * sin, HD // 2, 1)
 
-    @pl.loop(0, 8)
+    @pl.loop(0, 8, unroll=4)
     def _(n):
         g = g_all[n]
         g_head, g_rest = split(g)
@@ -390,15 +379,14 @@
         low = low_ref[n]
         dup[...] += dot(low, head_part, TN) + dot(low, rest_part, TN)
 
-    far = 1 - core
-    out_ref[pl.ds(far, 1), :, RING // 2 : RING] = jnp.zeros((1, N_FSDP, RING // 2, 8, HD), F32)
+    sums[1, :, RING // 2 : RING] = jnp.zeros((N_FSDP, RING // 2, 8, HD), F32)
     for j in range(GROUP + 2):
         tile = GROUP * head + j if j < GROUP else (HQ + HK * (j - GROUP)) + head
         shard = tile // 3
         block = max(0, j - GROUP + 1)
         value = dup[ADAPTER_RANK * block : ADAPTER_RANK * (block + 1), HD * j : HD * (j + 1)]
         for i in range(2):
-            out_ref[far, shard, RING // 2 + 2 * (tile % 3) + i] = value[8 * i : 8 * (i + 1)]
+            sums[1, shard, RING // 2 + 2 * (tile % 3) + i] = value[8 * i : 8 * (i + 1)]
     for copy in copies:
         copy.wait()
     for f in range(N_FSDP):
@@ -407,8 +395,9 @@
         for b in range(ROWS // HD):
             for i in range(LOW // 8):
                 group = b * (LOW // 8) + i
-                spot = core if group < RING else 1 - core
-                out_ref[spot, f, group % RING] = value[8 * i : 8 * (i + 1), HD * b : HD * (b + 1)]
+                sums[group // RING, f, group % RING] = value[8 * i : 8 * (i + 1), HD * b : HD * (b + 1)]
+    keep_ref[...] = sums[core]
+    give_ref[...] = sums[1 - core]
 
 
 def backward(scalars, tokens, g_own, g_other, saved, cos, sin):
@@ -417,16 +406,17 @@
         backward_kernel,
         name="attention_backward",
         in_specs=[SMEM] + [ANY] * n + [VMEM] * 11,
-        out_specs=VMEM,
-        out_shape=jax.ShapeDtypeStruct((2, N_FSDP, RING, 8, HD), F32),
+        out_specs=[VMEM, VMEM],
+        out_shape=[jax.ShapeDtypeStruct((N_FSDP, RING, 8, HD), F32)] * 2,
         scratch_shapes=[
             pltpu.VMEM((n * L, MODEL_WIDTH), BF16),
             pltpu.VMEM((2 * LOW, n * L), BF16),
             pltpu.VMEM((LOW, COLS), F32),
             pltpu.VMEM((n, 8, HD), F32),
+            pltpu.VMEM((2, N_FSDP, RING, 8, HD), F32),
             pltpu.SemaphoreType.DMA((n,)),
         ],
-        compiler_params=params(),
+        compiler_params=params(LARGE_VMEM),
         cost_estimate=cost(2 * n * L * MODEL_WIDTH * 2 * LOW, 15e6),
     )(scalars, *tokens, g_own, g_other, *saved, cos, sin)
 
@@ -480,6 +470,8 @@
     return pairs
 
 
+Y_PARTNER = dp_pairs(lambda z, y, c: (z, 1 - y, c))
+Z_GROUPS = [[4 * z + i for z in range(N_DP // 4)] for i in range(4)]
 SIBLING = dp_pairs(lambda z, y, c: (z, y, 1 - c))
 UPWARD = dp_pairs(lambda z, y, c: (z + 1, y, c))
 DOWNWARD = dp_pairs(lambda z, y, c: (z - 1, y, c))
@@ -508,27 +500,36 @@
     dp = lax.axis_index("dp")
     core = dp % 2
     head = 2 * ((dp // 4) % 2) + core
+    y_hi = (dp // 2) % 2
     cos, sin = (jnp.asarray(t) for t in rope_tables())
 
-    scalars = jnp.stack([head, core]).astype(jnp.int32)
+    scalars = jnp.stack([head, core, y_hi]).astype(jnp.int32)
     columns = [
         lax.dynamic_slice_in_dim(frozen_weight, GROUP * HD * head, GROUP * HD, 1),
         lax.dynamic_slice_in_dim(frozen_weight, HQ * HD + HD * head, HD, 1),
         lax.dynamic_slice_in_dim(frozen_weight, (HQ + HK) * HD + HD * head, HD, 1),
     ]
-    packed = jnp.concatenate(
+    maps = jnp.stack(
         [
-            jnp.concatenate(columns, axis=1),
-            jnp.pad(down_maps.T, ((0, 0), (0, COLS - ROWS))),
-            jnp.pad(up_maps.T, ((0, 0), (0, COLS - UP_ROWS))),
-        ],
-        axis=0,
+            jnp.pad(down_maps.T[:MAP], ((0, 0), (0, COLS - ROWS))),
+            jnp.concatenate(
+                [
+                    jnp.pad(down_maps.T[MAP:], ((0, 0), (0, COLS - ROWS))),
+                    jnp.pad(up_maps.T, ((0, 0), (0, COLS - UP_ROWS))),
+                ],
+                axis=0,
+            ),
+        ]
     )
+    mine = lax.dynamic_index_in_dim(maps, core, 0, keepdims=False)
+    packed = jnp.concatenate([jnp.concatenate(columns, axis=1), mine], axis=0)
+    weight = lax.all_gather(packed, "fsdp", axis=0)
     first, second = normalize(layer_input, gain)
 
-    weight = lax.all_gather(packed, "fsdp", axis=0)
-
-    own = swap_dp(jnp.broadcast_to(passage_rows[None], (RING, 64, 256))).reshape(RING * 64, 256)
+    pair = jnp.stack([passage_rows, lax.ppermute(passage_rows, "dp", Y_PARTNER)])
+    own = lax.all_to_all(
+        jnp.broadcast_to(pair[None], (N_DP // 4, 2, 64, 256)), "dp", 0, 0, axis_index_groups=Z_GROUPS
+    ).reshape(RING * 64, 256)
     own = after(own, first, second)
     other = to_sibling(own)
     from_below = lax.ppermute(after(first, own), "dp", UPWARD)
@@ -548,10 +549,13 @@
         compiler_params=params(),
         cost_estimate=cost(64 * 256 * 20, 1.2e6),
     )(swap_fsdp(partial))
-    scores = swap_fsdp(scores)
+    scores = after(swap_fsdp(scores), from_below, from_above)
     owner = positive // 64
     place = (
-        jnp.where(owner % 2 == core, 0, RING * 64) + (owner // 2) * 64 + positive % 64
+        jnp.where(owner % 2 == core, 0, RING * 64)
+        + (owner // 4) * 128
+        + jnp.where((owner // 2) % 2 == y_hi, 0, 64)
+        + positive % 64
     ).astype(jnp.int32)
     query_grad, pulls, columns_sum, rerun = pl.pallas_call(
         query_grad_kernel,
@@ -570,35 +574,35 @@
     keep, give = pl.pallas_call(
         passage_terms_kernel,
         name="passage_terms",
+        in_specs=[SMEM] + [VMEM] * 5,
         out_shape=[jax.ShapeDtypeStruct((RING * 64, 256), F32)] * 2,
         compiler_params=params(),
         cost_estimate=cost(2 * 128 * 256 * 2048, 6e6),
-    )(pulls, columns_sum, query_rows, own, other)
+    )(scalars, after(pulls, g), columns_sum, query_rows, own, other)
     received = to_sibling(give)
 
     tokens = [first, second, to_sibling(first), to_sibling(second)]
     tokens += [from_below, from_above, to_sibling(from_below), to_sibling(from_above)]
-    weight = after(weight, keep)
-    *saved, = project(scalars, tokens, weight, cos, sin)
-    g = after(g, saved[0])
-
     sent = (keep + received).astype(BF16).reshape(RING, 64, 256)
     arrived = swap_dp(sent)
     passage_grad = jnp.sum(arrived.astype(F32), axis=0)
 
     g = jnp.swapaxes(g, 0, 1)
     below, above = lax.ppermute(g[0:1], "dp", UPWARD), lax.ppermute(g[1:2], "dp", DOWNWARD)
-    queries, keys = after(saved[0], g, sent), saved[1]
+    weight = after(weight, sent)
+    maps_other = to_sibling(weight[:, ROWS:])
+    *saved, = project(scalars, tokens, weight, maps_other, cos, sin)
+    queries, keys = saved[:2]
     weights, sums = attend(queries, keys)
-    below = after(below, weights)
+    below = after(below, queries)
     g_own = jnp.concatenate([g, below, above], axis=0)
     g_other = to_sibling(g_own)
-    grads = backward(
+    kept, given = backward(
         scalars, tokens, g_own, g_other, [queries, keys, saved[2], weights, sums, *saved[3:]], cos, sin
     )
-    grads = after(grads, arrived)
-
-    summed = grads[0] + to_sibling(grads[1])
+    given = after(given, arrived)
+
+    summed = kept + to_sibling(given)
     shared = pl.pallas_call(
         fold_kernel,
         name="fold_fsdp",
@@ -625,7 +629,7 @@
             jax.ShapeDtypeStruct((ADAPTER_RANK, UP_ROWS), F32),
         ],
         compiler_params=params(),
-    )(scalars, total, total_other, squares, to_sibling(squares))
+    )(scalars, total, total_other, squares, to_sibling(after(squares, passage_grad)))
     return query_grad, passage_grad, down.T, up.T
 
 

time: 228 us -> 217 us (0.952)
  blocking collectives: 38.9 us -> 60.4 us
  waiting for transfers between devices: 60.9 us -> 40.8 us
  Pallas kernels: 43.5 us -> 30.8 us
  local copies, waits for them, and re-layouts: 5.46 us -> 11.6 us
  starting transfers between devices: 58.5 us -> 52.7 us
    all_to_all x1 -> x2, blocking collectives: 12.6 us -> 34.3 us  [swap_fsdp(): return lax.all_to_all(x, 'fsdp', 0, 0)]
    all_to_all x2 -> x1, waiting for transfers between devices: 16 us -> 0.01 us  [swap_dp(): return lax.all_to_all(x, 'dp', 0, 0, axis_index_groups=CORE_GROUPS)]
    all_gather x1, waiting for transfers between devices: 12.7 us -> 0.02 us  [shards(): weight = lax.all_gather(packed, 'fsdp', axis=0)]
    all_to_all x0 -> x1, waiting for transfers between devices: none -> 12.6 us  [shards(): lax.all_to_all(jnp.broadcast_to(pair[None], (N_DP // 4, 2, 64, 256)), 'dp...]
    all_to_all x2 -> x1, starting transfers between devices: 20.7 us -> 9.04 us  [swap_dp(): return lax.all_to_all(x, 'dp', 0, 0, axis_index_groups=CORE_GROUPS)]
    all_to_all x0 -> x1, starting transfers between devices: none -> 8.37 us  [shards(): lax.all_to_all(jnp.broadcast_to(pair[None], (N_DP // 4, 2, 64, 256)), 'dp...]
    pallas_call x1, Pallas kernels: 19.4 us -> 13.3 us  [project(): pl.pallas_call(project_kernel, name='project', in_specs=[SMEM] + [ANY] *...]
    all_to_all x4 -> x3, waiting for transfers between devices: 28 us -> 22.4 us  [swap_fsdp(): return lax.all_to_all(x, 'fsdp', 0, 0)]
  transfers between devices with their start and end apart: 21 -> 22, of which waited for: 9 -> 9; matrix products, arithmetic and copies ran while one was open for 2% -> 2% of each run, Pallas kernels for 18% -> 13%
where the time goes in v3:
time: 217 us; the launch traced here: 216 us
  blocking collectives  60.4 us (28%)
  starting transfers between devices  52.7 us (24%)
  waiting for transfers between devices  40.8 us (19%)
  Pallas kernels  30.8 us (14%)
  between operations  14.4 us (7%)
  local copies, waits for them, and re-layouts  11.6 us (5%)
  other arithmetic  4.96 us (2%)
    all_to_all x2, blocking collectives, swap_fsdp(): return lax.all_to_all(x, 'fsdp', 0, 0)  34.3 us
    all_to_all x1, blocking collectives, swap_dp(): return lax.all_to_all(x, 'dp', 0, 0, axis_index_groups=CORE_GROUPS)  26.1 us
    all_to_all x3, waiting for transfers between devices, swap_fsdp(): return lax.all_to_all(x, 'fsdp', 0, 0)  22.4 us
    all_to_all x3, starting transfers between devices, swap_fsdp(): return lax.all_to_all(x, 'fsdp', 0, 0)  15.2 us
    pallas_call x1, Pallas kernels, project(): pl.pallas_call(project_kernel, name='project', in_specs=[SMEM] + [ANY] *...  13.3 us
    all_to_all x1, waiting for transfers between devices, shards(): lax.all_to_all(jnp.broadcast_to(pair[None], (N_DP // 4, 2, 64, 256)), 'dp...  12.6 us
    ppermute x11, starting transfers between devices, to_sibling(): return lax.ppermute(x, 'dp', SIBLING)  11.6 us
    all_to_all x1, starting transfers between devices, swap_dp(): return lax.all_to_all(x, 'dp', 0, 0, axis_index_groups=CORE_GROUPS)  9.04 us
  transfers between devices with their start and end apart: 22, of which 9 were waited for; matrix products, arithmetic and copies ran while one was open for 2% of the time, Pallas kernels for 13%

profile of v3, /device:TPU:1, one launch (start us, length us, event | category | flops | bytes accessed | tf_op | source)
XLA Modules:
  0.0 215.6 jit_solution(6064612177178137972)
XLA Ops:
  7.3 0.8 slice.21
  8.0 0.7 slice.22
  8.7 1.1 constant_dynamic-slice_fusion.2
  9.8 1.0 constant_dynamic-slice_fusion.1
  10.9 1.0 pad_maximum_fusion
  12.0 3.8 %collective-permute-start = (bf16[64,256]{1,0:T(8,128)(2,1)S(1)}, bf16[64,256]{1,0:T(8,128)(2,1)S(1)}, u32[]{:S(2)}, u32[]{:S(2)}) collective-permute-start(bf16[64,256]{1,0:T(8,128)(2,1)S(1)} %copy-done.10), channel_id=1, source_target_pairs={{0,16},{8,24},{16,0},{24,8},{32,48},{40,56},{48,32},{56,40},{64,80... | collective-permute-start | bytes 98312 | tf_op jit(solution)/shard_map/ppermute | solution.py:529
  15.8 1.3 collective-permute-done
  17.1 0.9 broadcast_in_dim.14
  18.0 8.4 %all-to-all-start = ((bf16[8,2,64,256]{3,2,1,0:T(8,128)(2,1)}), bf16[8,2,64,256]{3,2,1,0:T(8,128)(2,1)S(1)}, u32[]{:S(2)}, u32[]{:S(2)}) async-start(bf16[8,2,64,256]{3,2,1,0:T(8,128)(2,1)} %broadcast_in_dim.14), calls=%async_computation | async-start | bytes 1048576 | tf_op jit(solution)/shard_map/all_to_all | solution.py:530
  26.4 1.7 copy-done.1
  28.1 1.3 normalize.1
  29.4 12.6 %all-to-all-done = bf16[8,2,64,256]{3,2,1,0:T(8,128)(2,1)S(1)} async-done(((bf16[8,2,64,256]{3,2,1,0:T(8,128)(2,1)}), bf16[8,2,64,256]{3,2,1,0:T(8,128)(2,1)S(1)}, u32[]{:S(2)}, u32[]{:S(2)}) %all-to-all-start) | async-done | bytes 524320 | tf_op jit(solution)/shard_map/all_to_all | solution.py:530
  42.0 2.8 %collective-permute-start.1 = (bf16[1024,256]{1,0:T(8,128)(2,1)S(1)}, bf16[1024,256]{1,0:T(8,128)(2,1)S(1)}, u32[]{:S(2)}, u32[]{:S(2)}) collective-permute-start(bf16[1024,256]{1,0:T(8,128)(2,1)S(1)} %bitcast.26), channel_id=1, source_target_pairs={{0,8},{8,0},{16,24},{24,16},{32,40},{40,32},{48,56},{56,48},{64,72... | collective-permute-start | bytes 1572872 | tf_op jit(solution)/shard_map/ppermute | solution.py:482
  44.8 1.5 collective-permute-start.2
  46.3 1.0 partial_scores.1
  47.4 21.6 %all_to_all.40.parts_ref = f32[8,72,256]{2,1,0:T(8,128)S(1)} all-to-all(f32[8,72,256]{2,1,0:T(8,128)S(1)} %partial_scores.1), channel_id=1, replica_groups=mesh['dp'=32,'fsdp'=8] {'fsdp'}, dimensions={0} | all-to-all | bytes 1179648 | tf_op jit(solution)/shard_map/all_to_all | solution.py:494
  69.1 0.8 copy-done
  69.9 4.2 %all-to-all-start.2 = ((f32[8,72,256]{2,1,0:T(8,128)}), f32[8,72,256]{2,1,0:T(8,128)}, u32[]{:S(2)}, u32[]{:S(2)}) async-start(f32[8,72,256]{2,1,0:T(8,128)} %copy-done), calls=%async_computation.2 | async-start | bytes 1179648 | tf_op jit(solution)/shard_map/all_to_all | solution.py:494
  74.3 13.7 %all-to-all-done.2.s_ref = f32[8,72,256]{2,1,0:T(8,128)} async-done(((f32[8,72,256]{2,1,0:T(8,128)}), f32[8,72,256]{2,1,0:T(8,128)}, u32[]{:S(2)}, u32[]{:S(2)}) %all-to-all-start.2) | async-done | bytes 589856 | tf_op jit(solution)/shard_map/all_to_all | solution.py:494
  88.0 2.4 %query_grad.1 = (f32[64,256]{1,0:T(8,128)}, f32[8,64,256]{2,1,0:T(8,128)S(1)}, f32[8,8,256]{2,1,0:T(8,128)S(1)}, f32[8,2,256]{2,1,0:T(2,128)}) custom-call(f32[8,72,256]{2,1,0:T(8,128)} %all-to-all-done.2.s_ref, bf16[64,256]{1,0:T(8,128)(2,1)S(1)} %copy-done.5, s32[64,1]{1,0:T(8,128)S(1)} %copy.16.pos_ref, bf16[1024,256]{1,0:T(8,128)(2,1)S(1)} %bitcast.28, ...), custom_call_target="tpu_custom_call" | custom-call | flops 1 | bytes 1 | tf_op jit(solution)/shard_map/query_grad/pallas_call | solution.py:560
  90.4 0.8 copy-done.3
  91.2 7.7 %all-to-all-start.3 = ((f32[8,2,256]{2,1,0:T(2,128)}), f32[8,2,256]{2,1,0:T(2,128)S(1)}, u32[]{:S(2)}, u32[]{:S(2)}) async-start(f32[8,2,256]{2,1,0:T(2,128)} %get-tuple-element.42), calls=%async_computation.3 | async-start | bytes 32768 | tf_op jit(solution)/shard_map/all_to_all | solution.py:494
  99.0 8.1 %all-to-all-done.3 = f32[8,2,256]{2,1,0:T(2,128)S(1)} async-done(((f32[8,2,256]{2,1,0:T(2,128)}), f32[8,2,256]{2,1,0:T(2,128)S(1)}, u32[]{:S(2)}, u32[]{:S(2)}) %all-to-all-start.3) | async-done | bytes 16416 | tf_op jit(solution)/shard_map/all_to_all | solution.py:494
  107.0 1.0 copy-done.4
  108.1 1.1 passage_terms.1
  110.4 1.5 collective-permute-done.4
  111.9 0.9 add_convert_fusion
  112.8 9.0 %all-to-all-start.4 = ((bf16[16,64,256]{2,1,0:T(8,128)(2,1)}), bf16[16,64,256]{2,1,0:T(8,128)(2,1)}, u32[]{:S(2)}, u32[]{:S(2)}) async-start(bf16[16,64,256]{2,1,0:T(8,128)(2,1)} %bitcast.33), calls=%async_computation.4 | async-start | bytes 1048576 | tf_op jit(solution)/shard_map/all_to_all | solution.py:490
  121.9 1.0 slice.18
  123.4 1.7 collective-permute-start.9
  125.1 1.5 collective-permute-start.11
  126.6 13.3 %project.1 = (bf16[8,512,128]{2,1,0:T(8,128)(2,1)S(1)}, bf16[8,128,128]{2,1,0:T(8,128)(2,1)S(1)}, bf16[8,128,128]{2,1,0:T(8,128)(2,1)S(1)}, bf16[8,128,48]{2,1,0:T(8,128)(2,1)S(1)}, bf16[48,768]{1,0:T(8,128)(2,1)S(1)}) custom-call(s32[3]{0:T(128)S(1)} %pad_add_fusion.scalar_ref, bf16[128,4096]{1,0:T(8,128)(2,1)S(1)} %get-tuple-element.37.t0, ...), custom_call_target="tpu_custom_call" | custom-call | flops 1 | bytes 1 | tf_op jit(solution)/shard_map/project/pallas_call | solution.py:259
  140.6 1.7 attend.1
  142.4 7.8 %attention_backward.1 = (f32[8,16,8,128]{3,2,1,0:T(8,128)S(1)}, f32[8,16,8,128]{3,2,1,0:T(8,128)S(1)}) custom-call(s32[3]{0:T(128)S(1)} %pad_add_fusion.scalar_ref, bf16[128,4096]{1,0:T(8,128)(2,1)S(1)} %get-tuple-element.37.t0, bf16[128,4096]{1,0:T(8,128)(2,1)S(1)} %get-tuple-element.38.t1, bf16[128,4096]{1,0:T(8,128)(2,1)S(1)} %collective-permute-done.5.t2, ...), custom_call_target="tpu_custom_call" | custom-call | flops 1 | bytes 1 | tf_op jit(solution)/shard_map/attention_backward/pallas_call | solution.py:405
  150.1 0.8 copy-done.2
  150.9 0.8 copy-done.9
  151.9 1.9 collective-permute-done.13
  153.9 1.1 add_bitcast_fusion
  155.0 12.7 %all_to_all.41.parts_ref = f32[8,128,128]{2,1,0:T(8,128)S(1)} all-to-all(f32[8,128,128]{2,1,0:T(8,128)S(1)} %add_bitcast_fusion), channel_id=1, replica_groups=mesh['dp'=32,'fsdp'=8] {'fsdp'}, dimensions={0} | all-to-all | bytes 1048576 | tf_op jit(solution)/shard_map/all_to_all | solution.py:494
  167.8 26.1 %all_to_all.42.parts_ref = bf16[16,128,128]{2,1,0:T(8,128)(2,1)S(1)} all-to-all(bf16[16,128,128]{2,1,0:T(8,128)(2,1)S(1)} %fold_fsdp.1), channel_id=1, replica_groups={{0,16,32,48,64,80,96,112,128,144,160,176,192,208,224,240},{8,24,40,56,7..., dimensions={0} | all-to-all | bytes 1048576 | tf_op jit(solution)/shard_map/all_to_all | solution.py:490
  193.8 0.7 total_dp.1
  194.5 3.3 %all-to-all-start.7 = ((f32[8,8,128]{2,1,0:T(8,128)}), f32[8,8,128]{2,1,0:T(8,128)S(1)}, u32[]{:S(2)}, u32[]{:S(2)}) async-start(f32[8,8,128]{2,1,0:T(8,128)} %get-tuple-element.60), calls=%async_computation.7 | async-start | bytes 65536 | tf_op jit(solution)/shard_map/all_to_all | solution.py:494
  197.9 2.6 %collective-permute-start.14 = (f32[128,128]{1,0:T(8,128)S(1)}, f32[128,128]{1,0:T(8,128)S(1)}, u32[]{:S(2)}, u32[]{:S(2)}) collective-permute-start(f32[128,128]{1,0:T(8,128)S(1)} %get-tuple-element.59.own_ref), channel_id=1, source_target_pairs={{0,8},{8,0},{16,24},{24,16},{32,40},{40,32},{48,56},{56,48},{64,72... | collective-permute-start | bytes 196616 | tf_op jit(solution)/shard_map/ppermute | solution.py:482
  200.5 1.7 convert_reduce_fusion
  202.3 0.7 all-to-all-done.7.squares_ref
  202.9 3.7 %collective-permute-start.15 = (f32[8,8,128]{2,1,0:T(8,128)S(1)}, f32[8,8,128]{2,1,0:T(8,128)S(1)}, u32[]{:S(2)}, u32[]{:S(2)}) collective-permute-start(f32[8,8,128]{2,1,0:T(8,128)S(1)} %all-to-all-done.7.squares_ref), channel_id=1, source_target_pairs={{0,8},{8,0},{16,24},{24,16},{32,40},{40,32},{48,56},{56,48},{64,72... | collective-permute-start | bytes 98312 | tf_op jit(solution)/shard_map/ppermute | solution.py:482
  206.6 0.9 collective-permute-done.15.squares_other_ref
  207.5 1.3 finish_clip.1
  (56 shorter events, 3.2 us)
Async XLA Ops:
  7.2 3.7 %copy-start.11 = (bf16[384,16]{0,1:T(8,128)(2,1)S(1)}, bf16[384,16]{0,1:T(8,128)(2,1)}, u32[]{:S(2)}) copy-start(bf16[384,16]{0,1:T(8,128)(2,1)} %param.17) | copy-start | bytes 36868
  7.2 114.7 %all-gather.3.cloned.1.call-start = ((), (), s32[]{:S(2)}) async-start(), calls=%async_computation.8 | async-start | bytes 7520256 | tf_op jit(solution)/shard_map/all_gather | solution.py:526
  9.8 2.2 copy-start.10
  11.9 14.4 %copy-start.8 = (f32[4096]{0:T(1024)S(1)}, f32[4096]{0:T(1024)}, u32[]{:S(2)}) copy-start(f32[4096]{0:T(1024)} %param.14) | copy-start | bytes 49156
  12.0 5.1 %collective-permute-start = (bf16[64,256]{1,0:T(8,128)(2,1)S(1)}, bf16[64,256]{1,0:T(8,128)(2,1)S(1)}, u32[]{:S(2)}, u32[]{:S(2)}) collective-permute-start(bf16[64,256]{1,0:T(8,128)(2,1)S(1)} %copy-done.10), channel_id=1, source_target_pairs={{0,16},{8,24},{16,0},{24,8},{32,48},{40,56},{48,32},{56,40},{64,80... | collective-permute-start | bytes 98312 | tf_op jit(solution)/shard_map/ppermute | solution.py:529
  18.0 28.4 %copy-start.5 = (bf16[64,256]{1,0:T(8,128)(2,1)S(1)}, bf16[64,256]{1,0:T(8,128)(2,1)}, u32[]{:S(2)}) copy-start(bf16[64,256]{1,0:T(8,128)(2,1)} %q_ref.5) | copy-start | bytes 98308
  18.0 24.0 %all-to-all-start = ((bf16[8,2,64,256]{3,2,1,0:T(8,128)(2,1)}), bf16[8,2,64,256]{3,2,1,0:T(8,128)(2,1)S(1)}, u32[]{:S(2)}, u32[]{:S(2)}) async-start(bf16[8,2,64,256]{3,2,1,0:T(8,128)(2,1)} %broadcast_in_dim.14), calls=%async_computation | async-start | bytes 1048576 | tf_op jit(solution)/shard_map/all_to_all | solution.py:530
  26.4 1.7 copy-start.1
  42.0 4.3 %collective-permute-start.1 = (bf16[1024,256]{1,0:T(8,128)(2,1)S(1)}, bf16[1024,256]{1,0:T(8,128)(2,1)S(1)}, u32[]{:S(2)}, u32[]{:S(2)}) collective-permute-start(bf16[1024,256]{1,0:T(8,128)(2,1)S(1)} %bitcast.26), channel_id=1, source_target_pairs={{0,8},{8,0},{16,24},{24,16},{32,40},{40,32},{48,56},{56,48},{64,72... | collective-permute-start | bytes 1572872 | tf_op jit(solution)/shard_map/ppermute | solution.py:482
  44.8 29.5 %collective-permute-start.3 = (bf16[128,4096]{1,0:T(8,128)(2,1)S(1)}, bf16[128,4096]{1,0:T(8,128)(2,1)}, u32[]{:S(2)}, u32[]{:S(2)}) collective-permute-start(bf16[128,4096]{1,0:T(8,128)(2,1)S(1)} %get-tuple-element.38.t1), channel_id=1, source_target_pairs={{0,224},{8,232},{16,240},{24,248},{32,0},{40,8},{48,16},{56,24},{6... | collective-permute-start | bytes 3145736 | tf_op jit(solution)/shard_map/ppermute | solution.py:536
  44.8 29.5 %collective-permute-start.2 = (bf16[128,4096]{1,0:T(8,128)(2,1)S(1)}, bf16[128,4096]{1,0:T(8,128)(2,1)}, u32[]{:S(2)}, u32[]{:S(2)}) collective-permute-start(bf16[128,4096]{1,0:T(8,128)(2,1)S(1)} %get-tuple-element.37.t0), channel_id=1, source_target_pairs={{0,32},{8,40},{16,48},{24,56},{32,64},{40,72},{48,80},{56,88},{64,... | collective-permute-start | bytes 3145736 | tf_op jit(solution)/shard_map/ppermute | solution.py:535
  47.4 26.8 %copy-start.12 = (s32[64]{0:T(128)S(1)}, s32[64]{0:T(128)}, u32[]{:S(2)}) copy-start(s32[64]{0:T(128)} %param.12) | copy-start | bytes 772
  69.1 0.8 copy-start
  69.9 18.1 %all-to-all-start.2 = ((f32[8,72,256]{2,1,0:T(8,128)}), f32[8,72,256]{2,1,0:T(8,128)}, u32[]{:S(2)}, u32[]{:S(2)}) async-start(f32[8,72,256]{2,1,0:T(8,128)} %copy-done), calls=%async_computation.2 | async-start | bytes 1179648 | tf_op jit(solution)/shard_map/all_to_all | solution.py:494
  90.4 0.8 copy-start.3
  91.2 15.8 %all-to-all-start.3 = ((f32[8,2,256]{2,1,0:T(2,128)}), f32[8,2,256]{2,1,0:T(2,128)S(1)}, u32[]{:S(2)}, u32[]{:S(2)}) async-start(f32[8,2,256]{2,1,0:T(2,128)} %get-tuple-element.42), calls=%async_computation.3 | async-start | bytes 32768 | tf_op jit(solution)/shard_map/all_to_all | solution.py:494
  107.0 1.0 copy-start.4
  109.2 2.7 %collective-permute-start.4 = (f32[1024,256]{1,0:T(8,128)S(1)}, f32[1024,256]{1,0:T(8,128)S(1)}, u32[]{:S(2)}, u32[]{:S(2)}) collective-permute-start(f32[1024,256]{1,0:T(8,128)S(1)} %get-tuple-element.46), channel_id=1, source_target_pairs={{0,8},{8,0},{16,24},{24,16},{32,40},{40,32},{48,56},{56,48},{64,72... | collective-permute-start | bytes 3145736 | tf_op jit(solution)/shard_map/ppermute | solution.py:482
  109.3 14.2 %collective-permute-start.5 = (bf16[128,4096]{1,0:T(8,128)(2,1)S(1)}, bf16[128,4096]{1,0:T(8,128)(2,1)S(1)}, u32[]{:S(2)}, u32[]{:S(2)}) collective-permute-start(bf16[128,4096]{1,0:T(8,128)(2,1)S(1)} %get-tuple-element.37.t0), channel_id=1, source_target_pairs={{0,8},{8,0},{16,24},{24,16},{32,40},{40,32},{48,56},{56,48},{64,72... | collective-permute-start | bytes 3145736 | tf_op jit(solution)/shard_map/ppermute | solution.py:482
  109.8 15.4 %collective-permute-start.6 = (bf16[128,4096]{1,0:T(8,128)(2,1)S(1)}, bf16[128,4096]{1,0:T(8,128)(2,1)}, u32[]{:S(2)}, u32[]{:S(2)}) collective-permute-start(bf16[128,4096]{1,0:T(8,128)(2,1)S(1)} %get-tuple-element.38.t1), channel_id=1, source_target_pairs={{0,8},{8,0},{16,24},{24,16},{32,40},{40,32},{48,56},{56,48},{64,72... | collective-permute-start | bytes 3145736 | tf_op jit(solution)/shard_map/ppermute | solution.py:482
  109.9 16.7 %collective-permute-start.8 = (bf16[128,4096]{1,0:T(8,128)(2,1)}, bf16[128,4096]{1,0:T(8,128)(2,1)}, u32[]{:S(2)}, u32[]{:S(2)}) collective-permute-start(bf16[128,4096]{1,0:T(8,128)(2,1)} %collective-permute-done.3.t5), channel_id=1, source_target_pairs={{0,8},{8,0},{16,24},{24,16},{32,40},{40,32},{48,56},{56,48},{64,72... | collective-permute-start | bytes 3145736 | tf_op jit(solution)/shard_map/ppermute | solution.py:482
  110.3 16.3 %collective-permute-start.7 = (bf16[128,4096]{1,0:T(8,128)(2,1)}, bf16[128,4096]{1,0:T(8,128)(2,1)}, u32[]{:S(2)}, u32[]{:S(2)}) collective-permute-start(bf16[128,4096]{1,0:T(8,128)(2,1)} %collective-permute-done.2.t4), channel_id=1, source_target_pairs={{0,8},{8,0},{16,24},{24,16},{32,40},{40,32},{48,56},{56,48},{64,72... | collective-permute-start | bytes 3145736 | tf_op jit(solution)/shard_map/ppermute | solution.py:482
  111.9 14.7 %copy-start.6 = (f32[128,128]{1,0:T(8,128)S(1)}, f32[128,128]{1,0:T(8,128)}, u32[]{:S(2)}) copy-start(f32[128,128]{1,0:T(8,128)} %constant.127.clone.cos_ref) | copy-start | bytes 196612
  111.9 14.7 %copy-start.7 = (f32[128,128]{1,0:T(8,128)S(1)}, f32[128,128]{1,0:T(8,128)}, u32[]{:S(2)}) copy-start(f32[128,128]{1,0:T(8,128)} %constant.128.clone.sin_ref) | copy-start | bytes 196612
  112.8 38.9 %all-to-all-start.4 = ((bf16[16,64,256]{2,1,0:T(8,128)(2,1)}), bf16[16,64,256]{2,1,0:T(8,128)(2,1)}, u32[]{:S(2)}, u32[]{:S(2)}) async-start(bf16[16,64,256]{2,1,0:T(8,128)(2,1)} %bitcast.33), calls=%async_computation.4 | async-start | bytes 1048576 | tf_op jit(solution)/shard_map/all_to_all | solution.py:490
  122.9 3.7 %collective-permute-start.10 = (bf16[8,32,768]{2,1,0:T(8,128)(2,1)S(1)}, bf16[8,32,768]{2,1,0:T(8,128)(2,1)S(1)}, u32[]{:S(2)}, u32[]{:S(2)}) collective-permute-start(bf16[8,32,768]{2,1,0:T(8,128)(2,1)S(1)} %slice.18), channel_id=1, source_target_pairs={{0,8},{8,0},{16,24},{24,16},{32,40},{40,32},{48,56},{56,48},{64,72... | collective-permute-start | bytes 1179656 | tf_op jit(solution)/shard_map/ppermute | solution.py:482
  123.4 16.5 %collective-permute-start.9 = (f32[1,8,256]{2,1,0:T(8,128)S(1)}, f32[1,8,256]{2,1,0:T(8,128)S(1)}, u32[]{:S(2)}, u32[]{:S(2)}) collective-permute-start(f32[1,8,256]{2,1,0:T(8,128)S(1)} %get-tuple-element.66), channel_id=1, source_target_pairs={{0,32},{8,40},{16,48},{24,56},{32,64},{40,72},{48,80},{56,88},{64,... | collective-permute-start | bytes 24584 | tf_op jit(solution)/shard_map/ppermute | solution.py:591
  125.1 14.9 %collective-permute-start.11 = (f32[1,8,256]{2,1,0:T(8,128)S(1)}, f32[1,8,256]{2,1,0:T(8,128)S(1)}, u32[]{:S(2)}, u32[]{:S(2)}) collective-permute-start(f32[1,8,256]{2,1,0:T(8,128)S(1)} %get-tuple-element.67), channel_id=1, source_target_pairs={{0,224},{8,232},{16,240},{24,248},{32,0},{40,8},{48,16},{56,24},{6... | collective-permute-start | bytes 24584 | tf_op jit(solution)/shard_map/ppermute | solution.py:591
  140.0 2.3 %collective-permute-start.12 = (f32[4,8,256]{2,1,0:T(8,128)S(1)}, f32[4,8,256]{2,1,0:T(8,128)S(1)}, u32[]{:S(2)}, u32[]{:S(2)}) collective-permute-start(f32[4,8,256]{2,1,0:T(8,128)S(1)} %pad_maximum_fusion.2.g_own), channel_id=1, source_target_pairs={{0,8},{8,0},{16,24},{24,16},{32,40},{40,32},{48,56},{56,48},{64,72... | collective-permute-start | bytes 98312 | tf_op jit(solution)/shard_map/ppermute | solution.py:482
  150.1 0.8 copy-start.2
  150.9 0.8 copy-start.9
  151.7 2.1 collective-permute-start.13
  194.5 8.4 %all-to-all-start.7 = ((f32[8,8,128]{2,1,0:T(8,128)}), f32[8,8,128]{2,1,0:T(8,128)S(1)}, u32[]{:S(2)}, u32[]{:S(2)}) async-start(f32[8,8,128]{2,1,0:T(8,128)} %get-tuple-element.60), calls=%async_computation.7 | async-start | bytes 65536 | tf_op jit(solution)/shard_map/all_to_all | solution.py:494
  197.9 9.6 %collective-permute-start.14 = (f32[128,128]{1,0:T(8,128)S(1)}, f32[128,128]{1,0:T(8,128)S(1)}, u32[]{:S(2)}, u32[]{:S(2)}) collective-permute-start(f32[128,128]{1,0:T(8,128)S(1)} %get-tuple-element.59.own_ref), channel_id=1, source_target_pairs={{0,8},{8,0},{16,24},{24,16},{32,40},{40,32},{48,56},{56,48},{64,72... | collective-permute-start | bytes 196616 | tf_op jit(solution)/shard_map/ppermute | solution.py:482
  202.9 4.5 %collective-permute-start.15 = (f32[8,8,128]{2,1,0:T(8,128)S(1)}, f32[8,8,128]{2,1,0:T(8,128)S(1)}, u32[]{:S(2)}, u32[]{:S(2)}) collective-permute-start(f32[8,8,128]{2,1,0:T(8,128)S(1)} %all-to-all-done.7.squares_ref), channel_id=1, source_target_pairs={{0,8},{8,0},{16,24},{24,16},{32,40},{40,32},{48,56},{56,48},{64,72... | collective-permute-start | bytes 98312 | tf_op jit(solution)/shard_map/ppermute | solution.py:482
Sparse Core Ops, SparseCore 0:
  12.1 95.0 all-gather.2

commit v4 on v3

--- a/solution.py
+++ b/solution.py
@@ -426,14 +426,19 @@
     for n in range(1, N_FSDP):
         total = total + parts_ref[n]
     total = total.astype(BF16)
-    for n in range(RING):
+    for n in range(out_ref.shape[0]):
         out_ref[n] = total
 
 
-def total_kernel(parts_ref, out_ref, squares_ref):
+def sum_kernel(parts_ref, out_ref):
     total = parts_ref[0].astype(F32)
-    for n in range(1, RING):
+    for n in range(1, parts_ref.shape[0]):
         total = total + parts_ref[n].astype(F32)
+    out_ref[...] = total
+
+
+def total_kernel(own_ref, other_ref, out_ref, squares_ref):
+    total = own_ref[...] + other_ref[...]
     out_ref[...] = total
     squares = jnp.broadcast_to(jnp.sum(total * total, axis=0, keepdims=True), (8, HD))
     for n in range(N_FSDP):
@@ -488,6 +493,10 @@
 
 def swap_dp(x):
     return lax.all_to_all(x, "dp", 0, 0, axis_index_groups=CORE_GROUPS)
+
+
+def swap_z(x):
+    return lax.all_to_all(x, "dp", 0, 0, axis_index_groups=Z_GROUPS)
 
 
 def swap_fsdp(x):
@@ -606,9 +615,15 @@
     shared = pl.pallas_call(
         fold_kernel,
         name="fold_fsdp",
-        out_shape=jax.ShapeDtypeStruct((RING, RING * 8, HD), BF16),
+        out_shape=jax.ShapeDtypeStruct((N_DP // 4, RING * 8, HD), BF16),
         compiler_params=params(),
     )(swap_fsdp(summed.reshape(N_FSDP, RING * 8, HD)))
+    half = pl.pallas_call(
+        sum_kernel,
+        name="sum_z",
+        out_shape=jax.ShapeDtypeStruct((RING * 8, HD), F32),
+        compiler_params=params(),
+    )(swap_z(shared))
     total, squares = pl.pallas_call(
         total_kernel,
         name="total_dp",
@@ -617,7 +632,7 @@
             jax.ShapeDtypeStruct((N_FSDP, 8, HD), F32),
         ],
         compiler_params=params(),
-    )(swap_dp(shared))
+    )(half, lax.ppermute(half, "dp", Y_PARTNER))
     total_other = to_sibling(total)
     squares = swap_fsdp(squares)
     down, up = pl.pallas_call(

time: 217 us -> 213 us (0.982)
  blocking collectives: 60.4 us -> 50.9 us
  starting transfers between devices: 52.7 us -> 57.4 us
    all_to_all x1, blocking collectives: 26.1 us -> 16.7 us  [swap_z(): return lax.all_to_all(x, 'dp', 0, 0, axis_index_groups=Z_GROUPS)]
    ppermute x0 -> x1, starting transfers between devices: none -> 2.77 us  [shards(): lax.ppermute(half, 'dp', Y_PARTNER)]
  transfers between devices with their start and end apart: 22 -> 23, of which waited for: 9 -> 9; matrix products, arithmetic and copies ran while one was open for 2% -> 2% of each run, Pallas kernels for 13% -> 14%
where the time goes in v4:
time: 213 us; the launch traced here: 212 us
  starting transfers between devices  57.4 us (27%)
  blocking collectives  50.9 us (24%)
  waiting for transfers between devices  42.1 us (20%)
  Pallas kernels  30.8 us (14%)
  between operations  14.4 us (7%)
  local copies, waits for them, and re-layouts  11.6 us (5%)
  other arithmetic  4.98 us (2%)
    all_to_all x2, blocking collectives, swap_fsdp(): return lax.all_to_all(x, 'fsdp', 0, 0)  34.3 us
    all_to_all x3, waiting for transfers between devices, swap_fsdp(): return lax.all_to_all(x, 'fsdp', 0, 0)  21.8 us
    all_to_all x1, blocking collectives, swap_z(): return lax.all_to_all(x, 'dp', 0, 0, axis_index_groups=Z_GROUPS)  16.7 us
    all_to_all x3, starting transfers between devices, swap_fsdp(): return lax.all_to_all(x, 'fsdp', 0, 0)  15.2 us
    ppermute x11, starting transfers between devices, to_sibling(): return lax.ppermute(x, 'dp', SIBLING)  13.6 us
    pallas_call x1, Pallas kernels, project(): pl.pallas_call(project_kernel, name='project', in_specs=[SMEM] + [ANY] *...  13.3 us
    all_to_all x1, waiting for transfers between devices, shards(): lax.all_to_all(jnp.broadcast_to(pair[None], (N_DP // 4, 2, 64, 256)), 'dp...  12.6 us
    all_to_all x1, starting transfers between devices, swap_dp(): return lax.all_to_all(x, 'dp', 0, 0, axis_index_groups=CORE_GROUPS)  9.04 us
  transfers between devices with their start and end apart: 23, of which 9 were waited for; matrix products, arithmetic and copies ran while one was open for 2% of the time, Pallas kernels for 14%

profile of v4, /device:TPU:1, one launch (start us, length us, event | category | flops | bytes accessed | tf_op | source)
XLA Modules:
  0.0 212.1 jit_solution(11327849108856668066)
XLA Ops:
  7.3 0.8 slice.21
  8.0 0.7 slice.22
  8.7 1.1 constant_dynamic-slice_fusion.2
  9.8 1.0 constant_dynamic-slice_fusion.1
  10.9 1.0 pad_maximum_fusion
  12.0 3.8 %collective-permute-start = (bf16[64,256]{1,0:T(8,128)(2,1)S(1)}, bf16[64,256]{1,0:T(8,128)(2,1)S(1)}, u32[]{:S(2)}, u32[]{:S(2)}) collective-permute-start(bf16[64,256]{1,0:T(8,128)(2,1)S(1)} %copy-done.10), channel_id=1, source_target_pairs={{0,16},{8,24},{16,0},{24,8},{32,48},{40,56},{48,32},{56,40},{64,80... | collective-permute-start | bytes 98312 | tf_op jit(solution)/shard_map/ppermute | solution.py:538
  15.8 1.3 collective-permute-done
  17.1 0.8 broadcast_in_dim.14
  18.0 8.4 %all-to-all-start = ((bf16[8,2,64,256]{3,2,1,0:T(8,128)(2,1)}), bf16[8,2,64,256]{3,2,1,0:T(8,128)(2,1)S(1)}, u32[]{:S(2)}, u32[]{:S(2)}) async-start(bf16[8,2,64,256]{3,2,1,0:T(8,128)(2,1)} %broadcast_in_dim.14), calls=%async_computation | async-start | bytes 1048576 | tf_op jit(solution)/shard_map/all_to_all | solution.py:539
  26.4 1.7 copy-done.1
  28.1 1.3 normalize.1
  29.4 12.6 %all-to-all-done = bf16[8,2,64,256]{3,2,1,0:T(8,128)(2,1)S(1)} async-done(((bf16[8,2,64,256]{3,2,1,0:T(8,128)(2,1)}), bf16[8,2,64,256]{3,2,1,0:T(8,128)(2,1)S(1)}, u32[]{:S(2)}, u32[]{:S(2)}) %all-to-all-start) | async-done | bytes 524320 | tf_op jit(solution)/shard_map/all_to_all | solution.py:539
  42.0 2.8 %collective-permute-start.1 = (bf16[1024,256]{1,0:T(8,128)(2,1)S(1)}, bf16[1024,256]{1,0:T(8,128)(2,1)S(1)}, u32[]{:S(2)}, u32[]{:S(2)}) collective-permute-start(bf16[1024,256]{1,0:T(8,128)(2,1)S(1)} %bitcast.26), channel_id=1, source_target_pairs={{0,8},{8,0},{16,24},{24,16},{32,40},{40,32},{48,56},{56,48},{64,72... | collective-permute-start | bytes 1572872 | tf_op jit(solution)/shard_map/ppermute | solution.py:487
  44.8 1.5 collective-permute-start.2
  46.4 1.0 partial_scores.1
  47.4 21.6 %all_to_all.40.parts_ref = f32[8,72,256]{2,1,0:T(8,128)S(1)} all-to-all(f32[8,72,256]{2,1,0:T(8,128)S(1)} %partial_scores.1), channel_id=1, replica_groups=mesh['dp'=32,'fsdp'=8] {'fsdp'}, dimensions={0} | all-to-all | bytes 1179648 | tf_op jit(solution)/shard_map/all_to_all | solution.py:503
  69.1 0.8 copy-done
  69.9 4.2 %all-to-all-start.2 = ((f32[8,72,256]{2,1,0:T(8,128)}), f32[8,72,256]{2,1,0:T(8,128)}, u32[]{:S(2)}, u32[]{:S(2)}) async-start(f32[8,72,256]{2,1,0:T(8,128)} %copy-done), calls=%async_computation.2 | async-start | bytes 1179648 | tf_op jit(solution)/shard_map/all_to_all | solution.py:503
  74.3 13.7 %all-to-all-done.2.s_ref = f32[8,72,256]{2,1,0:T(8,128)} async-done(((f32[8,72,256]{2,1,0:T(8,128)}), f32[8,72,256]{2,1,0:T(8,128)}, u32[]{:S(2)}, u32[]{:S(2)}) %all-to-all-start.2) | async-done | bytes 589856 | tf_op jit(solution)/shard_map/all_to_all | solution.py:503
  88.0 2.4 %query_grad.1 = (f32[64,256]{1,0:T(8,128)}, f32[8,64,256]{2,1,0:T(8,128)S(1)}, f32[8,8,256]{2,1,0:T(8,128)S(1)}, f32[8,2,256]{2,1,0:T(2,128)}) custom-call(f32[8,72,256]{2,1,0:T(8,128)} %all-to-all-done.2.s_ref, bf16[64,256]{1,0:T(8,128)(2,1)S(1)} %copy-done.5, s32[64,1]{1,0:T(8,128)S(1)} %copy.16.pos_ref, bf16[1024,256]{1,0:T(8,128)(2,1)S(1)} %bitcast.28, ...), custom_call_target="tpu_custom_call" | custom-call | flops 1 | bytes 1 | tf_op jit(solution)/shard_map/query_grad/pallas_call | solution.py:569
  90.4 0.8 copy-done.3
  91.2 7.7 %all-to-all-start.3 = ((f32[8,2,256]{2,1,0:T(2,128)}), f32[8,2,256]{2,1,0:T(2,128)S(1)}, u32[]{:S(2)}, u32[]{:S(2)}) async-start(f32[8,2,256]{2,1,0:T(2,128)} %get-tuple-element.42), calls=%async_computation.3 | async-start | bytes 32768 | tf_op jit(solution)/shard_map/all_to_all | solution.py:503
  99.0 8.1 %all-to-all-done.3 = f32[8,2,256]{2,1,0:T(2,128)S(1)} async-done(((f32[8,2,256]{2,1,0:T(2,128)}), f32[8,2,256]{2,1,0:T(2,128)S(1)}, u32[]{:S(2)}, u32[]{:S(2)}) %all-to-all-start.3) | async-done | bytes 16416 | tf_op jit(solution)/shard_map/all_to_all | solution.py:503
  107.1 1.0 copy-done.4
  108.1 1.1 passage_terms.1
  110.4 1.5 collective-permute-done.4
  111.9 0.9 add_convert_fusion
  112.8 9.0 %all-to-all-start.4 = ((bf16[16,64,256]{2,1,0:T(8,128)(2,1)}), bf16[16,64,256]{2,1,0:T(8,128)(2,1)}, u32[]{:S(2)}, u32[]{:S(2)}) async-start(bf16[16,64,256]{2,1,0:T(8,128)(2,1)} %bitcast.33), calls=%async_computation.4 | async-start | bytes 1048576 | tf_op jit(solution)/shard_map/all_to_all | solution.py:495
  121.9 1.0 slice.18
  123.5 1.7 collective-permute-start.9
  125.1 1.5 collective-permute-start.11
  126.7 13.3 %project.1 = (bf16[8,512,128]{2,1,0:T(8,128)(2,1)S(1)}, bf16[8,128,128]{2,1,0:T(8,128)(2,1)S(1)}, bf16[8,128,128]{2,1,0:T(8,128)(2,1)S(1)}, bf16[8,128,48]{2,1,0:T(8,128)(2,1)S(1)}, bf16[48,768]{1,0:T(8,128)(2,1)S(1)}) custom-call(s32[3]{0:T(128)S(1)} %pad_add_fusion.scalar_ref, bf16[128,4096]{1,0:T(8,128)(2,1)S(1)} %get-tuple-element.37.t0, ...), custom_call_target="tpu_custom_call" | custom-call | flops 1 | bytes 1 | tf_op jit(solution)/shard_map/project/pallas_call | solution.py:259
  140.6 1.7 attend.1
  142.4 7.8 %attention_backward.1 = (f32[8,16,8,128]{3,2,1,0:T(8,128)S(1)}, f32[8,16,8,128]{3,2,1,0:T(8,128)S(1)}) custom-call(s32[3]{0:T(128)S(1)} %pad_add_fusion.scalar_ref, bf16[128,4096]{1,0:T(8,128)(2,1)S(1)} %get-tuple-element.37.t0, bf16[128,4096]{1,0:T(8,128)(2,1)S(1)} %get-tuple-element.38.t1, bf16[128,4096]{1,0:T(8,128)(2,1)S(1)} %collective-permute-done.5.t2, ...), custom_call_target="tpu_custom_call" | custom-call | flops 1 | bytes 1 | tf_op jit(solution)/shard_map/attention_backward/pallas_call | solution.py:405
  150.1 0.8 copy-done.2
  150.9 0.8 copy-done.9
  151.9 1.9 collective-permute-done.13
  153.9 1.1 add_bitcast_fusion
  155.0 12.7 %all_to_all.41.parts_ref = f32[8,128,128]{2,1,0:T(8,128)S(1)} all-to-all(f32[8,128,128]{2,1,0:T(8,128)S(1)} %add_bitcast_fusion), channel_id=1, replica_groups=mesh['dp'=32,'fsdp'=8] {'fsdp'}, dimensions={0} | all-to-all | bytes 1048576 | tf_op jit(solution)/shard_map/all_to_all | solution.py:503
  167.7 16.7 %all_to_all.42.parts_ref = bf16[8,128,128]{2,1,0:T(8,128)(2,1)S(1)} all-to-all(bf16[8,128,128]{2,1,0:T(8,128)(2,1)S(1)} %fold_fsdp.1), channel_id=1, replica_groups={{0,32,64,96,128,160,192,224},{8,40,72,104,136,168,200,232},{16,48,80,11..., dimensions={0} | all-to-all | bytes 524288 | tf_op jit(solution)/shard_map/all_to_all | solution.py:499
  184.4 2.8 %collective-permute-start.14 = (f32[128,128]{1,0:T(8,128)S(1)}, f32[128,128]{1,0:T(8,128)S(1)}, u32[]{:S(2)}, u32[]{:S(2)}) collective-permute-start(f32[128,128]{1,0:T(8,128)S(1)} %sum_z.1.own_ref), channel_id=1, source_target_pairs={{0,16},{8,24},{16,0},{24,8},{32,48},{40,56},{48,32},{56,40},{64,80... | collective-permute-start | bytes 196616 | tf_op jit(solution)/shard_map/ppermute | solution.py:635
  187.2 1.9 collective-permute-done.14.other_ref
  189.8 3.3 %all-to-all-start.7 = ((f32[8,8,128]{2,1,0:T(8,128)}), f32[8,8,128]{2,1,0:T(8,128)S(1)}, u32[]{:S(2)}, u32[]{:S(2)}) async-start(f32[8,8,128]{2,1,0:T(8,128)} %get-tuple-element.60), calls=%async_computation.7 | async-start | bytes 65536 | tf_op jit(solution)/shard_map/all_to_all | solution.py:503
  193.1 3.9 %collective-permute-start.15 = (f32[128,128]{1,0:T(8,128)S(1)}, f32[128,128]{1,0:T(8,128)S(1)}, u32[]{:S(2)}, u32[]{:S(2)}) collective-permute-start(f32[128,128]{1,0:T(8,128)S(1)} %get-tuple-element.59.own_ref), channel_id=1, source_target_pairs={{0,8},{8,0},{16,24},{24,16},{32,40},{40,32},{48,56},{56,48},{64,72... | collective-permute-start | bytes 196616 | tf_op jit(solution)/shard_map/ppermute | solution.py:487
  197.0 1.7 convert_reduce_fusion
  198.8 4.4 %collective-permute-start.16 = (f32[8,8,128]{2,1,0:T(8,128)S(1)}, f32[8,8,128]{2,1,0:T(8,128)S(1)}, u32[]{:S(2)}, u32[]{:S(2)}) collective-permute-start(f32[8,8,128]{2,1,0:T(8,128)S(1)} %all-to-all-done.7.squares_ref), channel_id=1, source_target_pairs={{0,8},{8,0},{16,24},{24,16},{32,40},{40,32},{48,56},{56,48},{64,72... | collective-permute-start | bytes 98312 | tf_op jit(solution)/shard_map/ppermute | solution.py:487
  203.1 0.9 collective-permute-done.16.squares_other_ref
  204.0 1.3 finish_clip.1
  (59 shorter events, 3.9 us)
Async XLA Ops:
  7.2 3.7 %copy-start.11 = (bf16[384,16]{0,1:T(8,128)(2,1)S(1)}, bf16[384,16]{0,1:T(8,128)(2,1)}, u32[]{:S(2)}) copy-start(bf16[384,16]{0,1:T(8,128)(2,1)} %param.17) | copy-start | bytes 36868
  7.2 114.7 %all-gather.3.cloned.1.call-start = ((), (), s32[]{:S(2)}) async-start(), calls=%async_computation.8 | async-start | bytes 7520256 | tf_op jit(solution)/shard_map/all_gather | solution.py:535
  9.8 2.2 %copy-start.10 = (bf16[64,256]{1,0:T(8,128)(2,1)S(1)}, bf16[64,256]{1,0:T(8,128)(2,1)}, u32[]{:S(2)}) copy-start(bf16[64,256]{1,0:T(8,128)(2,1)} %param.11) | copy-start | bytes 98308
  12.0 14.4 %copy-start.8 = (f32[4096]{0:T(1024)S(1)}, f32[4096]{0:T(1024)}, u32[]{:S(2)}) copy-start(f32[4096]{0:T(1024)} %param.14) | copy-start | bytes 49156
  12.0 5.1 %collective-permute-start = (bf16[64,256]{1,0:T(8,128)(2,1)S(1)}, bf16[64,256]{1,0:T(8,128)(2,1)S(1)}, u32[]{:S(2)}, u32[]{:S(2)}) collective-permute-start(bf16[64,256]{1,0:T(8,128)(2,1)S(1)} %copy-done.10), channel_id=1, source_target_pairs={{0,16},{8,24},{16,0},{24,8},{32,48},{40,56},{48,32},{56,40},{64,80... | collective-permute-start | bytes 98312 | tf_op jit(solution)/shard_map/ppermute | solution.py:538
  18.0 28.4 %copy-start.5 = (bf16[64,256]{1,0:T(8,128)(2,1)S(1)}, bf16[64,256]{1,0:T(8,128)(2,1)}, u32[]{:S(2)}) copy-start(bf16[64,256]{1,0:T(8,128)(2,1)} %q_ref.5) | copy-start | bytes 98308
  18.0 24.0 %all-to-all-start = ((bf16[8,2,64,256]{3,2,1,0:T(8,128)(2,1)}), bf16[8,2,64,256]{3,2,1,0:T(8,128)(2,1)S(1)}, u32[]{:S(2)}, u32[]{:S(2)}) async-start(bf16[8,2,64,256]{3,2,1,0:T(8,128)(2,1)} %broadcast_in_dim.14), calls=%async_computation | async-start | bytes 1048576 | tf_op jit(solution)/shard_map/all_to_all | solution.py:539
  26.4 1.7 copy-start.1
  42.0 4.3 %collective-permute-start.1 = (bf16[1024,256]{1,0:T(8,128)(2,1)S(1)}, bf16[1024,256]{1,0:T(8,128)(2,1)S(1)}, u32[]{:S(2)}, u32[]{:S(2)}) collective-permute-start(bf16[1024,256]{1,0:T(8,128)(2,1)S(1)} %bitcast.26), channel_id=1, source_target_pairs={{0,8},{8,0},{16,24},{24,16},{32,40},{40,32},{48,56},{56,48},{64,72... | collective-permute-start | bytes 1572872 | tf_op jit(solution)/shard_map/ppermute | solution.py:487
  44.8 29.5 %collective-permute-start.3 = (bf16[128,4096]{1,0:T(8,128)(2,1)S(1)}, bf16[128,4096]{1,0:T(8,128)(2,1)}, u32[]{:S(2)}, u32[]{:S(2)}) collective-permute-start(bf16[128,4096]{1,0:T(8,128)(2,1)S(1)} %get-tuple-element.38.t1), channel_id=1, source_target_pairs={{0,224},{8,232},{16,240},{24,248},{32,0},{40,8},{48,16},{56,24},{6... | collective-permute-start | bytes 3145736 | tf_op jit(solution)/shard_map/ppermute | solution.py:545
  44.8 29.5 %collective-permute-start.2 = (bf16[128,4096]{1,0:T(8,128)(2,1)S(1)}, bf16[128,4096]{1,0:T(8,128)(2,1)}, u32[]{:S(2)}, u32[]{:S(2)}) collective-permute-start(bf16[128,4096]{1,0:T(8,128)(2,1)S(1)} %get-tuple-element.37.t0), channel_id=1, source_target_pairs={{0,32},{8,40},{16,48},{24,56},{32,64},{40,72},{48,80},{56,88},{64,... | collective-permute-start | bytes 3145736 | tf_op jit(solution)/shard_map/ppermute | solution.py:544
  47.4 26.8 %copy-start.12 = (s32[64]{0:T(128)S(1)}, s32[64]{0:T(128)}, u32[]{:S(2)}) copy-start(s32[64]{0:T(128)} %param.12) | copy-start | bytes 772
  69.1 0.8 copy-start
  69.9 18.1 %all-to-all-start.2 = ((f32[8,72,256]{2,1,0:T(8,128)}), f32[8,72,256]{2,1,0:T(8,128)}, u32[]{:S(2)}, u32[]{:S(2)}) async-start(f32[8,72,256]{2,1,0:T(8,128)} %copy-done), calls=%async_computation.2 | async-start | bytes 1179648 | tf_op jit(solution)/shard_map/all_to_all | solution.py:503
  90.4 0.8 copy-start.3
  91.2 15.8 %all-to-all-start.3 = ((f32[8,2,256]{2,1,0:T(2,128)}), f32[8,2,256]{2,1,0:T(2,128)S(1)}, u32[]{:S(2)}, u32[]{:S(2)}) async-start(f32[8,2,256]{2,1,0:T(2,128)} %get-tuple-element.42), calls=%async_computation.3 | async-start | bytes 32768 | tf_op jit(solution)/shard_map/all_to_all | solution.py:503
  107.0 1.0 copy-start.4
  109.2 2.7 %collective-permute-start.4 = (f32[1024,256]{1,0:T(8,128)S(1)}, f32[1024,256]{1,0:T(8,128)S(1)}, u32[]{:S(2)}, u32[]{:S(2)}) collective-permute-start(f32[1024,256]{1,0:T(8,128)S(1)} %get-tuple-element.46), channel_id=1, source_target_pairs={{0,8},{8,0},{16,24},{24,16},{32,40},{40,32},{48,56},{56,48},{64,72... | collective-permute-start | bytes 3145736 | tf_op jit(solution)/shard_map/ppermute | solution.py:487
  109.3 14.2 %collective-permute-start.5 = (bf16[128,4096]{1,0:T(8,128)(2,1)S(1)}, bf16[128,4096]{1,0:T(8,128)(2,1)S(1)}, u32[]{:S(2)}, u32[]{:S(2)}) collective-permute-start(bf16[128,4096]{1,0:T(8,128)(2,1)S(1)} %get-tuple-element.37.t0), channel_id=1, source_target_pairs={{0,8},{8,0},{16,24},{24,16},{32,40},{40,32},{48,56},{56,48},{64,72... | collective-permute-start | bytes 3145736 | tf_op jit(solution)/shard_map/ppermute | solution.py:487
  109.8 15.4 %collective-permute-start.6 = (bf16[128,4096]{1,0:T(8,128)(2,1)S(1)}, bf16[128,4096]{1,0:T(8,128)(2,1)}, u32[]{:S(2)}, u32[]{:S(2)}) collective-permute-start(bf16[128,4096]{1,0:T(8,128)(2,1)S(1)} %get-tuple-element.38.t1), channel_id=1, source_target_pairs={{0,8},{8,0},{16,24},{24,16},{32,40},{40,32},{48,56},{56,48},{64,72... | collective-permute-start | bytes 3145736 | tf_op jit(solution)/shard_map/ppermute | solution.py:487
  109.9 16.7 %collective-permute-start.8 = (bf16[128,4096]{1,0:T(8,128)(2,1)}, bf16[128,4096]{1,0:T(8,128)(2,1)}, u32[]{:S(2)}, u32[]{:S(2)}) collective-permute-start(bf16[128,4096]{1,0:T(8,128)(2,1)} %collective-permute-done.3.t5), channel_id=1, source_target_pairs={{0,8},{8,0},{16,24},{24,16},{32,40},{40,32},{48,56},{56,48},{64,72... | collective-permute-start | bytes 3145736 | tf_op jit(solution)/shard_map/ppermute | solution.py:487
  110.3 16.3 %collective-permute-start.7 = (bf16[128,4096]{1,0:T(8,128)(2,1)}, bf16[128,4096]{1,0:T(8,128)(2,1)}, u32[]{:S(2)}, u32[]{:S(2)}) collective-permute-start(bf16[128,4096]{1,0:T(8,128)(2,1)} %collective-permute-done.2.t4), channel_id=1, source_target_pairs={{0,8},{8,0},{16,24},{24,16},{32,40},{40,32},{48,56},{56,48},{64,72... | collective-permute-start | bytes 3145736 | tf_op jit(solution)/shard_map/ppermute | solution.py:487
  111.9 14.7 %copy-start.6 = (f32[128,128]{1,0:T(8,128)S(1)}, f32[128,128]{1,0:T(8,128)}, u32[]{:S(2)}) copy-start(f32[128,128]{1,0:T(8,128)} %constant.127.clone.cos_ref) | copy-start | bytes 196612
  111.9 14.7 %copy-start.7 = (f32[128,128]{1,0:T(8,128)S(1)}, f32[128,128]{1,0:T(8,128)}, u32[]{:S(2)}) copy-start(f32[128,128]{1,0:T(8,128)} %constant.128.clone.sin_ref) | copy-start | bytes 196612
  112.8 38.9 %all-to-all-start.4 = ((bf16[16,64,256]{2,1,0:T(8,128)(2,1)}), bf16[16,64,256]{2,1,0:T(8,128)(2,1)}, u32[]{:S(2)}, u32[]{:S(2)}) async-start(bf16[16,64,256]{2,1,0:T(8,128)(2,1)} %bitcast.33), calls=%async_computation.4 | async-start | bytes 1048576 | tf_op jit(solution)/shard_map/all_to_all | solution.py:495
  122.9 3.7 %collective-permute-start.10 = (bf16[8,32,768]{2,1,0:T(8,128)(2,1)S(1)}, bf16[8,32,768]{2,1,0:T(8,128)(2,1)S(1)}, u32[]{:S(2)}, u32[]{:S(2)}) collective-permute-start(bf16[8,32,768]{2,1,0:T(8,128)(2,1)S(1)} %slice.18), channel_id=1, source_target_pairs={{0,8},{8,0},{16,24},{24,16},{32,40},{40,32},{48,56},{56,48},{64,72... | collective-permute-start | bytes 1179656 | tf_op jit(solution)/shard_map/ppermute | solution.py:487
  123.5 16.5 %collective-permute-start.9 = (f32[1,8,256]{2,1,0:T(8,128)S(1)}, f32[1,8,256]{2,1,0:T(8,128)S(1)}, u32[]{:S(2)}, u32[]{:S(2)}) collective-permute-start(f32[1,8,256]{2,1,0:T(8,128)S(1)} %get-tuple-element.66), channel_id=1, source_target_pairs={{0,32},{8,40},{16,48},{24,56},{32,64},{40,72},{48,80},{56,88},{64,... | collective-permute-start | bytes 24584 | tf_op jit(solution)/shard_map/ppermute | solution.py:600
  125.1 14.9 %collective-permute-start.11 = (f32[1,8,256]{2,1,0:T(8,128)S(1)}, f32[1,8,256]{2,1,0:T(8,128)S(1)}, u32[]{:S(2)}, u32[]{:S(2)}) collective-permute-start(f32[1,8,256]{2,1,0:T(8,128)S(1)} %get-tuple-element.67), channel_id=1, source_target_pairs={{0,224},{8,232},{16,240},{24,248},{32,0},{40,8},{48,16},{56,24},{6... | collective-permute-start | bytes 24584 | tf_op jit(solution)/shard_map/ppermute | solution.py:600
  140.0 2.3 %collective-permute-start.12 = (f32[4,8,256]{2,1,0:T(8,128)S(1)}, f32[4,8,256]{2,1,0:T(8,128)S(1)}, u32[]{:S(2)}, u32[]{:S(2)}) collective-permute-start(f32[4,8,256]{2,1,0:T(8,128)S(1)} %pad_maximum_fusion.2.g_own), channel_id=1, source_target_pairs={{0,8},{8,0},{16,24},{24,16},{32,40},{40,32},{48,56},{56,48},{64,72... | collective-permute-start | bytes 98312 | tf_op jit(solution)/shard_map/ppermute | solution.py:487
  150.1 0.8 copy-start.2
  150.9 0.8 copy-start.9
  151.7 2.1 %collective-permute-start.13 = (f32[8,16,8,128]{3,2,1,0:T(8,128)}, f32[8,16,8,128]{3,2,1,0:T(8,128)S(1)}, u32[]{:S(2)}, u32[]{:S(2)}) collective-permute-start(f32[8,16,8,128]{3,2,1,0:T(8,128)} %copy-done.9), channel_id=1, source_target_pairs={{0,8},{8,0},{16,24},{24,16},{32,40},{40,32},{48,56},{56,48},{64,72... | collective-permute-start | bytes 1572872 | tf_op jit(solution)/shard_map/ppermute | solution.py:487
  184.4 4.7 %collective-permute-start.14 = (f32[128,128]{1,0:T(8,128)S(1)}, f32[128,128]{1,0:T(8,128)S(1)}, u32[]{:S(2)}, u32[]{:S(2)}) collective-permute-start(f32[128,128]{1,0:T(8,128)S(1)} %sum_z.1.own_ref), channel_id=1, source_target_pairs={{0,16},{8,24},{16,0},{24,8},{32,48},{40,56},{48,32},{56,40},{64,80... | collective-permute-start | bytes 196616 | tf_op jit(solution)/shard_map/ppermute | solution.py:635
  189.8 9.0 %all-to-all-start.7 = ((f32[8,8,128]{2,1,0:T(8,128)}), f32[8,8,128]{2,1,0:T(8,128)S(1)}, u32[]{:S(2)}, u32[]{:S(2)}) async-start(f32[8,8,128]{2,1,0:T(8,128)} %get-tuple-element.60), calls=%async_computation.7 | async-start | bytes 65536 | tf_op jit(solution)/shard_map/all_to_all | solution.py:503
  193.1 10.8 %collective-permute-start.15 = (f32[128,128]{1,0:T(8,128)S(1)}, f32[128,128]{1,0:T(8,128)S(1)}, u32[]{:S(2)}, u32[]{:S(2)}) collective-permute-start(f32[128,128]{1,0:T(8,128)S(1)} %get-tuple-element.59.own_ref), channel_id=1, source_target_pairs={{0,8},{8,0},{16,24},{24,16},{32,40},{40,32},{48,56},{56,48},{64,72... | collective-permute-start | bytes 196616 | tf_op jit(solution)/shard_map/ppermute | solution.py:487
  198.8 5.2 %collective-permute-start.16 = (f32[8,8,128]{2,1,0:T(8,128)S(1)}, f32[8,8,128]{2,1,0:T(8,128)S(1)}, u32[]{:S(2)}, u32[]{:S(2)}) collective-permute-start(f32[8,8,128]{2,1,0:T(8,128)S(1)} %all-to-all-done.7.squares_ref), channel_id=1, source_target_pairs={{0,8},{8,0},{16,24},{24,16},{32,40},{40,32},{48,56},{56,48},{64,72... | collective-permute-start | bytes 98312 | tf_op jit(solution)/shard_map/ppermute | solution.py:487
Sparse Core Ops, SparseCore 0:
  12.1 95.0 all-gather.2

commit v5 on v4

--- a/solution.py
+++ b/solution.py
@@ -178,7 +178,7 @@
         rerun_ref[m] = query_grad[2 * m : 2 * m + 2]
 
 
-def passage_terms_kernel(scalar_ref, w_ref, col_ref, q_ref, own_ref, other_ref, keep_ref, give_ref):
+def passage_terms_kernel(w_ref, col_ref, q_ref, own_ref, other_ref, keep_ref, give_ref):
     q = q_ref[...]
     twice = jnp.concatenate([q, q], axis=0)
     for c in range(N_FSDP):
@@ -187,9 +187,7 @@
         scale = column_of(col_ref[c, 0:1, :], 256)
         value = pulled - scale * chunk_of(c, own_ref, other_ref).astype(F32)
         out_ref = keep_ref if c < 4 else give_ref
-        for b in range(4):
-            place = (c % 4) * 256 + (b // 2) * 128 + (scalar_ref[2] + b % 2) % 2 * 64
-            out_ref[pl.ds(pl.multiple_of(place, 64), 64), :] = value[64 * b : 64 * (b + 1)]
+        out_ref[(c % 4) * 256 : (c % 4 + 1) * 256, :] = value
 
 
 def project_kernel(
@@ -583,18 +581,18 @@
     keep, give = pl.pallas_call(
         passage_terms_kernel,
         name="passage_terms",
-        in_specs=[SMEM] + [VMEM] * 5,
         out_shape=[jax.ShapeDtypeStruct((RING * 64, 256), F32)] * 2,
         compiler_params=params(),
         cost_estimate=cost(2 * 128 * 256 * 2048, 6e6),
-    )(scalars, after(pulls, g), columns_sum, query_rows, own, other)
+    )(after(pulls, g), columns_sum, query_rows, own, other)
     received = to_sibling(give)
 
     tokens = [first, second, to_sibling(first), to_sibling(second)]
     tokens += [from_below, from_above, to_sibling(from_below), to_sibling(from_above)]
-    sent = (keep + received).astype(BF16).reshape(RING, 64, 256)
-    arrived = swap_dp(sent)
-    passage_grad = jnp.sum(arrived.astype(F32), axis=0)
+    sent = (keep + received).astype(BF16).reshape(N_DP // 4, 2, 64, 256)
+    arrived = swap_z(sent)
+    over_z = jnp.sum(arrived.astype(F32), axis=0)
+    passage_grad = over_z[0] + lax.ppermute(over_z[1], "dp", Y_PARTNER)
 
     g = jnp.swapaxes(g, 0, 1)
     below, above = lax.ppermute(g[0:1], "dp", UPWARD), lax.ppermute(g[1:2], "dp", DOWNWARD)

time: 213 us -> 210 us (0.986)
  starting transfers between devices: 57.4 us -> 55.2 us
    all_to_all x1 -> x0, blocking collectives: 16.7 us -> none  [swap_z(): return lax.all_to_all(x, 'dp', 0, 0, axis_index_groups=Z_GROUPS)]
    all_to_all x2 -> x3, blocking collectives: 34.3 us -> 50.9 us  [swap_fsdp(): return lax.all_to_all(x, 'fsdp', 0, 0)]
    all_to_all x1 -> x2, waiting for transfers between devices: 0.01 us -> 9.07 us  [swap_z(): return lax.all_to_all(x, 'dp', 0, 0, axis_index_groups=Z_GROUPS)]
    all_to_all x3 -> x2, starting transfers between devices: 15.2 us -> 7.54 us  [swap_fsdp(): return lax.all_to_all(x, 'fsdp', 0, 0)]
    all_to_all x3 -> x2, waiting for transfers between devices: 21.8 us -> 14.2 us  [swap_fsdp(): return lax.all_to_all(x, 'fsdp', 0, 0)]
    all_to_all x1 -> x2, starting transfers between devices: 9.04 us -> 13.4 us  [swap_z(): return lax.all_to_all(x, 'dp', 0, 0, axis_index_groups=Z_GROUPS)]
    unnamed x26 -> x22, local copies, waits for them, and re-layouts: 6.02 us -> 4.19 us
  transfers between devices with their start and end apart: 23 -> 24, of which waited for: 9 -> 10; matrix products, arithmetic and copies ran while one was open for 2% -> 2% of each run, Pallas kernels for 14% -> 14%
where the time goes in v5:
time: 210 us; the launch traced here: 209 us
  starting transfers between devices  55.2 us (26%)
  blocking collectives  50.9 us (24%)
  waiting for transfers between devices  43.2 us (21%)
  Pallas kernels  30.9 us (15%)
  between operations  14.4 us (7%)
  local copies, waits for them, and re-layouts  9.73 us (5%)
  other arithmetic  4.98 us (2%)
    all_to_all x3, blocking collectives, swap_fsdp(): return lax.all_to_all(x, 'fsdp', 0, 0)  50.9 us
    ppermute x11, starting transfers between devices, to_sibling(): return lax.ppermute(x, 'dp', SIBLING)  14.2 us
    all_to_all x2, waiting for transfers between devices, swap_fsdp(): return lax.all_to_all(x, 'fsdp', 0, 0)  14.2 us
    all_to_all x2, starting transfers between devices, swap_z(): return lax.all_to_all(x, 'dp', 0, 0, axis_index_groups=Z_GROUPS)  13.4 us
    pallas_call x1, Pallas kernels, project(): pl.pallas_call(project_kernel, name='project', in_specs=[SMEM] + [ANY] *...  13.3 us
    all_to_all x1, waiting for transfers between devices, shards(): lax.all_to_all(jnp.broadcast_to(pair[None], (N_DP // 4, 2, 64, 256)), 'dp...  12.6 us
    all_to_all x2, waiting for transfers between devices, swap_z(): return lax.all_to_all(x, 'dp', 0, 0, axis_index_groups=Z_GROUPS)  9.07 us
    all_to_all x1, starting transfers between devices, shards(): lax.all_to_all(jnp.broadcast_to(pair[None], (N_DP // 4, 2, 64, 256)), 'dp...  8.37 us
  transfers between devices with their start and end apart: 24, of which 10 were waited for; matrix products, arithmetic and copies ran while one was open for 2% of the time, Pallas kernels for 14%

profile of v5, /device:TPU:1, one launch (start us, length us, event | category | flops | bytes accessed | tf_op | source)
XLA Modules:
  0.0 209.4 jit_solution(4207729362682702719)
XLA Ops:
  7.3 0.8 slice.31
  8.0 0.7 slice.32
  8.7 1.1 constant_dynamic-slice_fusion.2
  9.8 1.0 constant_dynamic-slice_fusion.1
  10.9 1.0 pad_maximum_fusion
  12.0 3.8 %collective-permute-start = (bf16[64,256]{1,0:T(8,128)(2,1)S(1)}, bf16[64,256]{1,0:T(8,128)(2,1)S(1)}, u32[]{:S(2)}, u32[]{:S(2)}) collective-permute-start(bf16[64,256]{1,0:T(8,128)(2,1)S(1)} %copy-done.8), channel_id=1, source_target_pairs={{0,16},{8,24},{16,0},{24,8},{32,48},{40,56},{48,32},{56,40},{64,80... | collective-permute-start | bytes 98312 | tf_op jit(solution)/shard_map/ppermute | solution.py:536
  15.8 1.3 collective-permute-done
  17.1 0.9 broadcast_in_dim.14
  18.0 8.4 %all-to-all-start = ((bf16[8,2,64,256]{3,2,1,0:T(8,128)(2,1)}), bf16[8,2,64,256]{3,2,1,0:T(8,128)(2,1)S(1)}, u32[]{:S(2)}, u32[]{:S(2)}) async-start(bf16[8,2,64,256]{3,2,1,0:T(8,128)(2,1)} %broadcast_in_dim.14), calls=%async_computation | async-start | bytes 1048576 | tf_op jit(solution)/shard_map/all_to_all | solution.py:537
  26.4 1.7 copy-done.1
  28.1 1.3 normalize.1
  29.4 12.6 %all-to-all-done = bf16[8,2,64,256]{3,2,1,0:T(8,128)(2,1)S(1)} async-done(((bf16[8,2,64,256]{3,2,1,0:T(8,128)(2,1)}), bf16[8,2,64,256]{3,2,1,0:T(8,128)(2,1)S(1)}, u32[]{:S(2)}, u32[]{:S(2)}) %all-to-all-start) | async-done | bytes 524320 | tf_op jit(solution)/shard_map/all_to_all | solution.py:537
  42.0 2.8 %collective-permute-start.1 = (bf16[1024,256]{1,0:T(8,128)(2,1)S(1)}, bf16[1024,256]{1,0:T(8,128)(2,1)S(1)}, u32[]{:S(2)}, u32[]{:S(2)}) collective-permute-start(bf16[1024,256]{1,0:T(8,128)(2,1)S(1)} %bitcast.32), channel_id=1, source_target_pairs={{0,8},{8,0},{16,24},{24,16},{32,40},{40,32},{48,56},{56,48},{64,72... | collective-permute-start | bytes 1572872 | tf_op jit(solution)/shard_map/ppermute | solution.py:485
  44.8 1.5 collective-permute-start.2
  46.3 1.0 partial_scores.1
  47.4 21.6 %all_to_all.40.parts_ref = f32[8,72,256]{2,1,0:T(8,128)S(1)} all-to-all(f32[8,72,256]{2,1,0:T(8,128)S(1)} %partial_scores.1), channel_id=1, replica_groups=mesh['dp'=32,'fsdp'=8] {'fsdp'}, dimensions={0} | all-to-all | bytes 1179648 | tf_op jit(solution)/shard_map/all_to_all | solution.py:501
  69.1 0.8 copy-done
  69.9 4.2 %all-to-all-start.2 = ((f32[8,72,256]{2,1,0:T(8,128)}), f32[8,72,256]{2,1,0:T(8,128)}, u32[]{:S(2)}, u32[]{:S(2)}) async-start(f32[8,72,256]{2,1,0:T(8,128)} %copy-done), calls=%async_computation.2 | async-start | bytes 1179648 | tf_op jit(solution)/shard_map/all_to_all | solution.py:501
  74.3 13.7 %all-to-all-done.2.s_ref = f32[8,72,256]{2,1,0:T(8,128)} async-done(((f32[8,72,256]{2,1,0:T(8,128)}), f32[8,72,256]{2,1,0:T(8,128)}, u32[]{:S(2)}, u32[]{:S(2)}) %all-to-all-start.2) | async-done | bytes 589856 | tf_op jit(solution)/shard_map/all_to_all | solution.py:501
  88.0 2.4 %query_grad.1 = (f32[64,256]{1,0:T(8,128)}, f32[8,64,256]{2,1,0:T(8,128)S(1)}, f32[8,8,256]{2,1,0:T(8,128)S(1)}, f32[8,2,256]{2,1,0:T(2,128)S(1)}) custom-call(f32[8,72,256]{2,1,0:T(8,128)} %all-to-all-done.2.s_ref, bf16[64,256]{1,0:T(8,128)(2,1)S(1)} %copy-done.3, s32[64,1]{1,0:T(8,128)S(1)} %copy.16.pos_ref, bf16[1024,256]{1,0:T(8,128)(2,1)S(1)} %bitcast.34, ...), custom_call_target="tpu_custom_call" | custom-call | flops 1 | bytes 1 | tf_op jit(solution)/shard_map/query_grad/pallas_call | solution.py:567
  90.4 16.7 %all_to_all.41 = f32[8,2,256]{2,1,0:T(2,128)S(1)} all-to-all(f32[8,2,256]{2,1,0:T(2,128)S(1)} %get-tuple-element.42), channel_id=1, replica_groups=mesh['dp'=32,'fsdp'=8] {'fsdp'}, dimensions={0} | all-to-all | bytes 32768 | tf_op jit(solution)/shard_map/all_to_all | solution.py:501
  108.8 1.5 collective-permute-done.4
  110.3 0.9 add_convert_fusion
  111.2 6.7 %all-to-all-start.4 = ((bf16[8,2,64,256]{3,2,1,0:T(8,128)(2,1)}), bf16[8,2,64,256]{3,2,1,0:T(8,128)(2,1)}, u32[]{:S(2)}, u32[]{:S(2)}) async-start(bf16[8,2,64,256]{3,2,1,0:T(8,128)(2,1)} %bitcast.39), calls=%async_computation.4 | async-start | bytes 1048576 | tf_op jit(solution)/shard_map/all_to_all | solution.py:497
  118.0 1.0 slice.26
  119.5 1.8 collective-permute-start.10
  121.3 1.5 collective-permute-start.12
  122.9 13.3 %project.1 = (bf16[8,512,128]{2,1,0:T(8,128)(2,1)S(1)}, bf16[8,128,128]{2,1,0:T(8,128)(2,1)S(1)}, bf16[8,128,128]{2,1,0:T(8,128)(2,1)S(1)}, bf16[8,128,48]{2,1,0:T(8,128)(2,1)S(1)}, bf16[48,768]{1,0:T(8,128)(2,1)S(1)}) custom-call(s32[3]{0:T(128)S(1)} %pad_add_fusion.scalar_ref, bf16[128,4096]{1,0:T(8,128)(2,1)S(1)} %get-tuple-element.37.t0, ...), custom_call_target="tpu_custom_call" | custom-call | flops 1 | bytes 1 | tf_op jit(solution)/shard_map/project/pallas_call | solution.py:257
  136.9 1.7 attend.1
  138.6 7.8 %attention_backward.1 = (f32[8,16,8,128]{3,2,1,0:T(8,128)S(1)}, f32[8,16,8,128]{3,2,1,0:T(8,128)S(1)}) custom-call(s32[3]{0:T(128)S(1)} %pad_add_fusion.scalar_ref, bf16[128,4096]{1,0:T(8,128)(2,1)S(1)} %get-tuple-element.37.t0, bf16[128,4096]{1,0:T(8,128)(2,1)S(1)} %get-tuple-element.38.t1, bf16[128,4096]{1,0:T(8,128)(2,1)S(1)} %collective-permute-done.6.t2, ...), custom_call_target="tpu_custom_call" | custom-call | flops 1 | bytes 1 | tf_op jit(solution)/shard_map/attention_backward/pallas_call | solution.py:403
  146.4 0.8 copy-done.2
  147.2 0.8 copy-done.7
  148.2 1.9 collective-permute-done.14
  150.1 1.1 add_bitcast_fusion
  151.3 12.7 %all_to_all.42.parts_ref = f32[8,128,128]{2,1,0:T(8,128)S(1)} all-to-all(f32[8,128,128]{2,1,0:T(8,128)S(1)} %add_bitcast_fusion), channel_id=1, replica_groups=mesh['dp'=32,'fsdp'=8] {'fsdp'}, dimensions={0} | all-to-all | bytes 1048576 | tf_op jit(solution)/shard_map/all_to_all | solution.py:501
  164.0 0.7 fold_fsdp.1
  164.7 6.7 %all-to-all-start.6 = ((bf16[8,128,128]{2,1,0:T(8,128)(2,1)}), bf16[8,128,128]{2,1,0:T(8,128)(2,1)S(1)}, u32[]{:S(2)}, u32[]{:S(2)}) async-start(bf16[8,128,128]{2,1,0:T(8,128)(2,1)} %fold_fsdp.1), calls=%async_computation.6 | async-start | bytes 524288 | tf_op jit(solution)/shard_map/all_to_all | solution.py:497
  171.4 1.1 convert_reduce_fusion
  172.5 9.1 %all-to-all-done.6.parts_ref = bf16[8,128,128]{2,1,0:T(8,128)(2,1)S(1)} async-done(((bf16[8,128,128]{2,1,0:T(8,128)(2,1)}), bf16[8,128,128]{2,1,0:T(8,128)(2,1)S(1)}, u32[]{:S(2)}, u32[]{:S(2)}) %all-to-all-start.6) | async-done | bytes 262176 | tf_op jit(solution)/shard_map/all_to_all | solution.py:497
  181.6 2.5 %collective-permute-start.15 = (f32[128,128]{1,0:T(8,128)S(1)}, f32[128,128]{1,0:T(8,128)S(1)}, u32[]{:S(2)}, u32[]{:S(2)}) collective-permute-start(f32[128,128]{1,0:T(8,128)S(1)} %sum_z.1.own_ref), channel_id=1, source_target_pairs={{0,16},{8,24},{16,0},{24,8},{32,48},{40,56},{48,32},{56,40},{64,80... | collective-permute-start | bytes 196616 | tf_op jit(solution)/shard_map/ppermute | solution.py:633
  184.7 1.6 collective-permute-done.15.other_ref
  186.3 0.6 total_dp.1
  187.0 3.3 %all-to-all-start.7 = ((f32[8,8,128]{2,1,0:T(8,128)}), f32[8,8,128]{2,1,0:T(8,128)S(1)}, u32[]{:S(2)}, u32[]{:S(2)}) async-start(f32[8,8,128]{2,1,0:T(8,128)} %get-tuple-element.60), calls=%async_computation.7 | async-start | bytes 65536 | tf_op jit(solution)/shard_map/all_to_all | solution.py:501
  190.3 3.9 %collective-permute-start.16 = (f32[128,128]{1,0:T(8,128)S(1)}, f32[128,128]{1,0:T(8,128)S(1)}, u32[]{:S(2)}, u32[]{:S(2)}) collective-permute-start(f32[128,128]{1,0:T(8,128)S(1)} %get-tuple-element.59.own_ref), channel_id=1, source_target_pairs={{0,8},{8,0},{16,24},{24,16},{32,40},{40,32},{48,56},{56,48},{64,72... | collective-permute-start | bytes 196616 | tf_op jit(solution)/shard_map/ppermute | solution.py:485
  194.2 0.6 fusion.2
  195.4 5.0 %collective-permute-start.17 = (f32[8,8,128]{2,1,0:T(8,128)S(1)}, f32[8,8,128]{2,1,0:T(8,128)S(1)}, u32[]{:S(2)}, u32[]{:S(2)}) collective-permute-start(f32[8,8,128]{2,1,0:T(8,128)S(1)} %all-to-all-done.7.squares_ref), channel_id=1, source_target_pairs={{0,8},{8,0},{16,24},{24,16},{32,40},{40,32},{48,56},{56,48},{64,72... | collective-permute-start | bytes 98312 | tf_op jit(solution)/shard_map/ppermute | solution.py:485
  200.3 0.9 collective-permute-done.17.squares_other_ref
  201.2 1.3 finish_clip.1
  (59 shorter events, 4.7 us)
Async XLA Ops:
  7.2 3.7 %copy-start.9 = (bf16[384,16]{0,1:T(8,128)(2,1)S(1)}, bf16[384,16]{0,1:T(8,128)(2,1)}, u32[]{:S(2)}) copy-start(bf16[384,16]{0,1:T(8,128)(2,1)} %param.17) | copy-start | bytes 36868
  7.2 110.8 %all-gather.3.cloned.1.call-start = ((), (), s32[]{:S(2)}) async-start(), calls=%async_computation.8 | async-start | bytes 7520256 | tf_op jit(solution)/shard_map/all_gather | solution.py:533
  9.8 2.2 %copy-start.8 = (bf16[64,256]{1,0:T(8,128)(2,1)S(1)}, bf16[64,256]{1,0:T(8,128)(2,1)}, u32[]{:S(2)}) copy-start(bf16[64,256]{1,0:T(8,128)(2,1)} %param.11) | copy-start | bytes 98308
  11.9 14.4 %copy-start.6 = (f32[4096]{0:T(1024)S(1)}, f32[4096]{0:T(1024)}, u32[]{:S(2)}) copy-start(f32[4096]{0:T(1024)} %param.14) | copy-start | bytes 49156
  12.0 5.1 %collective-permute-start = (bf16[64,256]{1,0:T(8,128)(2,1)S(1)}, bf16[64,256]{1,0:T(8,128)(2,1)S(1)}, u32[]{:S(2)}, u32[]{:S(2)}) collective-permute-start(bf16[64,256]{1,0:T(8,128)(2,1)S(1)} %copy-done.8), channel_id=1, source_target_pairs={{0,16},{8,24},{16,0},{24,8},{32,48},{40,56},{48,32},{56,40},{64,80... | collective-permute-start | bytes 98312 | tf_op jit(solution)/shard_map/ppermute | solution.py:536
  18.0 28.4 %copy-start.3 = (bf16[64,256]{1,0:T(8,128)(2,1)S(1)}, bf16[64,256]{1,0:T(8,128)(2,1)}, u32[]{:S(2)}) copy-start(bf16[64,256]{1,0:T(8,128)(2,1)} %q_ref.5) | copy-start | bytes 98308
  18.0 24.0 %all-to-all-start = ((bf16[8,2,64,256]{3,2,1,0:T(8,128)(2,1)}), bf16[8,2,64,256]{3,2,1,0:T(8,128)(2,1)S(1)}, u32[]{:S(2)}, u32[]{:S(2)}) async-start(bf16[8,2,64,256]{3,2,1,0:T(8,128)(2,1)} %broadcast_in_dim.14), calls=%async_computation | async-start | bytes 1048576 | tf_op jit(solution)/shard_map/all_to_all | solution.py:537
  26.4 1.7 copy-start.1
  42.0 4.3 %collective-permute-start.1 = (bf16[1024,256]{1,0:T(8,128)(2,1)S(1)}, bf16[1024,256]{1,0:T(8,128)(2,1)S(1)}, u32[]{:S(2)}, u32[]{:S(2)}) collective-permute-start(bf16[1024,256]{1,0:T(8,128)(2,1)S(1)} %bitcast.32), channel_id=1, source_target_pairs={{0,8},{8,0},{16,24},{24,16},{32,40},{40,32},{48,56},{56,48},{64,72... | collective-permute-start | bytes 1572872 | tf_op jit(solution)/shard_map/ppermute | solution.py:485
  44.8 29.5 %collective-permute-start.3 = (bf16[128,4096]{1,0:T(8,128)(2,1)S(1)}, bf16[128,4096]{1,0:T(8,128)(2,1)}, u32[]{:S(2)}, u32[]{:S(2)}) collective-permute-start(bf16[128,4096]{1,0:T(8,128)(2,1)S(1)} %get-tuple-element.38.t1), channel_id=1, source_target_pairs={{0,224},{8,232},{16,240},{24,248},{32,0},{40,8},{48,16},{56,24},{6... | collective-permute-start | bytes 3145736 | tf_op jit(solution)/shard_map/ppermute | solution.py:543
  44.8 29.5 %collective-permute-start.2 = (bf16[128,4096]{1,0:T(8,128)(2,1)S(1)}, bf16[128,4096]{1,0:T(8,128)(2,1)}, u32[]{:S(2)}, u32[]{:S(2)}) collective-permute-start(bf16[128,4096]{1,0:T(8,128)(2,1)S(1)} %get-tuple-element.37.t0), channel_id=1, source_target_pairs={{0,32},{8,40},{16,48},{24,56},{32,64},{40,72},{48,80},{56,88},{64,... | collective-permute-start | bytes 3145736 | tf_op jit(solution)/shard_map/ppermute | solution.py:542
  47.4 26.8 %copy-start.10 = (s32[64]{0:T(128)S(1)}, s32[64]{0:T(128)}, u32[]{:S(2)}) copy-start(s32[64]{0:T(128)} %param.12) | copy-start | bytes 772
  69.1 0.8 copy-start
  69.9 18.1 %all-to-all-start.2 = ((f32[8,72,256]{2,1,0:T(8,128)}), f32[8,72,256]{2,1,0:T(8,128)}, u32[]{:S(2)}, u32[]{:S(2)}) async-start(f32[8,72,256]{2,1,0:T(8,128)} %copy-done), calls=%async_computation.2 | async-start | bytes 1179648 | tf_op jit(solution)/shard_map/all_to_all | solution.py:501
  107.6 2.7 %collective-permute-start.4 = (f32[1024,256]{1,0:T(8,128)S(1)}, f32[1024,256]{1,0:T(8,128)S(1)}, u32[]{:S(2)}, u32[]{:S(2)}) collective-permute-start(f32[1024,256]{1,0:T(8,128)S(1)} %get-tuple-element.46), channel_id=1, source_target_pairs={{0,8},{8,0},{16,24},{24,16},{32,40},{40,32},{48,56},{56,48},{64,72... | collective-permute-start | bytes 3145736 | tf_op jit(solution)/shard_map/ppermute | solution.py:485
  107.7 11.9 %collective-permute-start.6 = (bf16[128,4096]{1,0:T(8,128)(2,1)S(1)}, bf16[128,4096]{1,0:T(8,128)(2,1)S(1)}, u32[]{:S(2)}, u32[]{:S(2)}) collective-permute-start(bf16[128,4096]{1,0:T(8,128)(2,1)S(1)} %get-tuple-element.37.t0), channel_id=1, source_target_pairs={{0,8},{8,0},{16,24},{24,16},{32,40},{40,32},{48,56},{56,48},{64,72... | collective-permute-start | bytes 3145736 | tf_op jit(solution)/shard_map/ppermute | solution.py:485
  108.2 13.2 %collective-permute-start.7 = (bf16[128,4096]{1,0:T(8,128)(2,1)S(1)}, bf16[128,4096]{1,0:T(8,128)(2,1)}, u32[]{:S(2)}, u32[]{:S(2)}) collective-permute-start(bf16[128,4096]{1,0:T(8,128)(2,1)S(1)} %get-tuple-element.38.t1), channel_id=1, source_target_pairs={{0,8},{8,0},{16,24},{24,16},{32,40},{40,32},{48,56},{56,48},{64,72... | collective-permute-start | bytes 3145736 | tf_op jit(solution)/shard_map/ppermute | solution.py:485
  108.3 14.6 %collective-permute-start.9 = (bf16[128,4096]{1,0:T(8,128)(2,1)}, bf16[128,4096]{1,0:T(8,128)(2,1)}, u32[]{:S(2)}, u32[]{:S(2)}) collective-permute-start(bf16[128,4096]{1,0:T(8,128)(2,1)} %collective-permute-done.3.t5), channel_id=1, source_target_pairs={{0,8},{8,0},{16,24},{24,16},{32,40},{40,32},{48,56},{56,48},{64,72... | collective-permute-start | bytes 3145736 | tf_op jit(solution)/shard_map/ppermute | solution.py:485
  108.7 14.2 %collective-permute-start.8 = (bf16[128,4096]{1,0:T(8,128)(2,1)}, bf16[128,4096]{1,0:T(8,128)(2,1)}, u32[]{:S(2)}, u32[]{:S(2)}) collective-permute-start(bf16[128,4096]{1,0:T(8,128)(2,1)} %collective-permute-done.2.t4), channel_id=1, source_target_pairs={{0,8},{8,0},{16,24},{24,16},{32,40},{40,32},{48,56},{56,48},{64,72... | collective-permute-start | bytes 3145736 | tf_op jit(solution)/shard_map/ppermute | solution.py:485
  110.3 12.6 %copy-start.4 = (f32[128,128]{1,0:T(8,128)S(1)}, f32[128,128]{1,0:T(8,128)}, u32[]{:S(2)}) copy-start(f32[128,128]{1,0:T(8,128)} %constant.127.clone.cos_ref) | copy-start | bytes 196612
  110.3 12.6 %copy-start.5 = (f32[128,128]{1,0:T(8,128)S(1)}, f32[128,128]{1,0:T(8,128)}, u32[]{:S(2)}) copy-start(f32[128,128]{1,0:T(8,128)} %constant.128.clone.sin_ref) | copy-start | bytes 196612
  111.2 36.8 %all-to-all-start.4 = ((bf16[8,2,64,256]{3,2,1,0:T(8,128)(2,1)}), bf16[8,2,64,256]{3,2,1,0:T(8,128)(2,1)}, u32[]{:S(2)}, u32[]{:S(2)}) async-start(bf16[8,2,64,256]{3,2,1,0:T(8,128)(2,1)} %bitcast.39), calls=%async_computation.4 | async-start | bytes 1048576 | tf_op jit(solution)/shard_map/all_to_all | solution.py:497
  119.0 3.9 %collective-permute-start.11 = (bf16[8,32,768]{2,1,0:T(8,128)(2,1)S(1)}, bf16[8,32,768]{2,1,0:T(8,128)(2,1)S(1)}, u32[]{:S(2)}, u32[]{:S(2)}) collective-permute-start(bf16[8,32,768]{2,1,0:T(8,128)(2,1)S(1)} %slice.26), channel_id=1, source_target_pairs={{0,8},{8,0},{16,24},{24,16},{32,40},{40,32},{48,56},{56,48},{64,72... | collective-permute-start | bytes 1179656 | tf_op jit(solution)/shard_map/ppermute | solution.py:485
  119.5 16.7 %collective-permute-start.10 = (f32[1,8,256]{2,1,0:T(8,128)S(1)}, f32[1,8,256]{2,1,0:T(8,128)S(1)}, u32[]{:S(2)}, u32[]{:S(2)}) collective-permute-start(f32[1,8,256]{2,1,0:T(8,128)S(1)} %get-tuple-element.66), channel_id=1, source_target_pairs={{0,32},{8,40},{16,48},{24,56},{32,64},{40,72},{48,80},{56,88},{64,... | collective-permute-start | bytes 24584 | tf_op jit(solution)/shard_map/ppermute | solution.py:598
  121.3 14.9 %collective-permute-start.12 = (f32[1,8,256]{2,1,0:T(8,128)S(1)}, f32[1,8,256]{2,1,0:T(8,128)S(1)}, u32[]{:S(2)}, u32[]{:S(2)}) collective-permute-start(f32[1,8,256]{2,1,0:T(8,128)S(1)} %get-tuple-element.67), channel_id=1, source_target_pairs={{0,224},{8,232},{16,240},{24,248},{32,0},{40,8},{48,16},{56,24},{6... | collective-permute-start | bytes 24584 | tf_op jit(solution)/shard_map/ppermute | solution.py:598
  136.3 2.3 %collective-permute-start.13 = (f32[4,8,256]{2,1,0:T(8,128)S(1)}, f32[4,8,256]{2,1,0:T(8,128)S(1)}, u32[]{:S(2)}, u32[]{:S(2)}) collective-permute-start(f32[4,8,256]{2,1,0:T(8,128)S(1)} %pad_maximum_fusion.2.g_own), channel_id=1, source_target_pairs={{0,8},{8,0},{16,24},{24,16},{32,40},{40,32},{48,56},{56,48},{64,72... | collective-permute-start | bytes 98312 | tf_op jit(solution)/shard_map/ppermute | solution.py:485
  146.4 0.8 copy-start.2
  147.2 0.8 copy-start.7
  148.0 2.1 %collective-permute-start.14 = (f32[8,16,8,128]{3,2,1,0:T(8,128)}, f32[8,16,8,128]{3,2,1,0:T(8,128)S(1)}, u32[]{:S(2)}, u32[]{:S(2)}) collective-permute-start(f32[8,16,8,128]{3,2,1,0:T(8,128)} %copy-done.7), channel_id=1, source_target_pairs={{0,8},{8,0},{16,24},{24,16},{32,40},{40,32},{48,56},{56,48},{64,72... | collective-permute-start | bytes 1572872 | tf_op jit(solution)/shard_map/ppermute | solution.py:485
  164.7 16.9 %all-to-all-start.6 = ((bf16[8,128,128]{2,1,0:T(8,128)(2,1)}), bf16[8,128,128]{2,1,0:T(8,128)(2,1)S(1)}, u32[]{:S(2)}, u32[]{:S(2)}) async-start(bf16[8,128,128]{2,1,0:T(8,128)(2,1)} %fold_fsdp.1), calls=%async_computation.6 | async-start | bytes 524288 | tf_op jit(solution)/shard_map/all_to_all | solution.py:497
  181.6 4.7 %collective-permute-start.15 = (f32[128,128]{1,0:T(8,128)S(1)}, f32[128,128]{1,0:T(8,128)S(1)}, u32[]{:S(2)}, u32[]{:S(2)}) collective-permute-start(f32[128,128]{1,0:T(8,128)S(1)} %sum_z.1.own_ref), channel_id=1, source_target_pairs={{0,16},{8,24},{16,0},{24,8},{32,48},{40,56},{48,32},{56,40},{64,80... | collective-permute-start | bytes 196616 | tf_op jit(solution)/shard_map/ppermute | solution.py:633
  184.1 10.1 %collective-permute-start.5 = (f32[64,256]{1,0:T(8,128)S(1)}, f32[64,256]{1,0:T(8,128)S(1)}, u32[]{:S(2)}, u32[]{:S(2)}) collective-permute-start(f32[64,256]{1,0:T(8,128)S(1)} %slice_bitcast_fusion), channel_id=1, source_target_pairs={{0,16},{8,24},{16,0},{24,8},{32,48},{40,56},{48,32},{56,40},{64,80... | collective-permute-start | bytes 196616 | tf_op jit(solution)/shard_map/ppermute | solution.py:595
  187.0 8.4 %all-to-all-start.7 = ((f32[8,8,128]{2,1,0:T(8,128)}), f32[8,8,128]{2,1,0:T(8,128)S(1)}, u32[]{:S(2)}, u32[]{:S(2)}) async-start(f32[8,8,128]{2,1,0:T(8,128)} %get-tuple-element.60), calls=%async_computation.7 | async-start | bytes 65536 | tf_op jit(solution)/shard_map/all_to_all | solution.py:501
  190.3 10.9 %collective-permute-start.16 = (f32[128,128]{1,0:T(8,128)S(1)}, f32[128,128]{1,0:T(8,128)S(1)}, u32[]{:S(2)}, u32[]{:S(2)}) collective-permute-start(f32[128,128]{1,0:T(8,128)S(1)} %get-tuple-element.59.own_ref), channel_id=1, source_target_pairs={{0,8},{8,0},{16,24},{24,16},{32,40},{40,32},{48,56},{56,48},{64,72... | collective-permute-start | bytes 196616 | tf_op jit(solution)/shard_map/ppermute | solution.py:485
  195.4 5.8 %collective-permute-start.17 = (f32[8,8,128]{2,1,0:T(8,128)S(1)}, f32[8,8,128]{2,1,0:T(8,128)S(1)}, u32[]{:S(2)}, u32[]{:S(2)}) collective-permute-start(f32[8,8,128]{2,1,0:T(8,128)S(1)} %all-to-all-done.7.squares_ref), channel_id=1, source_target_pairs={{0,8},{8,0},{16,24},{24,16},{32,40},{40,32},{48,56},{56,48},{64,72... | collective-permute-start | bytes 98312 | tf_op jit(solution)/shard_map/ppermute | solution.py:485
Sparse Core Ops, SparseCore 0:
  12.1 95.0 all-gather.2
